TPU v7x, 32 devices: a whole 2x2x4 slice. The times are simulated.
32 devices in a mesh: clip: 8 (over z, x), chan: 4 (over y, core).
Axes of the slice: x: 2, y: 2, z: 4, core: 2. Of those that a mesh axis runs over, the one named last changes fastest.
Arguments:
- frames_in: bfloat16 [6272, 2048], P('clip'), may hold values from -10 to 10
- boundary: int32 [16, 8], P('clip'), may hold values from 0 to 1, as said below
- w_reduce: bfloat16 [2, 2048, 512], P(None, None, 'chan'), may hold values from -0.125 to 0.125
- gain_inner: float32 [2, 2, 512], P(None, None, 'chan'), may hold values from 0.1 to 1.9
- bias_inner: float32 [2, 2, 512], P(None, None, 'chan'), may hold values from -3 to 3
- w_conv: bfloat16 [2, 9, 512, 512], P(None, None, None, 'chan'), may hold values from -0.09375 to 0.09375
- w_expand: bfloat16 [2, 512, 2048], P(None, 'chan'), may hold values from -0.25 to 0.25
- gain_outer: float32 [2, 2048], replicated, may hold values from 0.1 to 1.9
- bias_outer: float32 [2, 2048], replicated, may hold values from -3 to 3
- depth_kernels: float32 [3, 9, 512], P(None, None, 'chan'), may hold values from -2 to 2
- gate_bias: float32 [512], P('chan'), may hold values from -3 to 3
- cotangent: bfloat16 [6272, 2048], P('clip'), may hold values from -7 to 7
Outputs:
- activations: bfloat16 [6272, 2048], P('clip', 'chan')
- input_grad: float32 [6272, 2048], P('clip', 'chan')
- grad_reduce: float32 [2, 2048, 512], P(None, None, 'chan')
- grad_gain_inner: float32 [2, 2, 512], P(None, None, 'chan')
- grad_bias_inner: float32 [2, 2, 512], P(None, None, 'chan')
- grad_conv: float32 [2, 9, 512, 512], P(None, None, None, 'chan')
- grad_expand: float32 [2, 512, 2048], P(None, 'chan')
- grad_gain_outer: float32 [2, 2048], P(None, 'chan')
- grad_bias_outer: float32 [2, 2048], P(None, 'chan')
- grad_kernels: float32 [3, 9, 512], P(None, None, 'chan')
- grad_gate_bias: float32 [512], P('chan')
Inputs may be any that keep to these rules, and one draw needn't show every extreme that they name: `boundary`: each row of 8 entries has a 1 at its last segment and at exactly one earlier segment, where the first packed video ends; 0 elsewhere.
All inputs are finite; a program needn't handle non-finite values.
Results may differ from a plain program's by a relative error of at most 0.03.
Values may be sent and summed in bfloat16 or wider, within the bound.
A program may use at most 192 MiB of HBM per device.

v0:
```python
from functools import partial

import jax
import jax.numpy as jnp
from jax import lax
from jax.sharding import PartitionSpec as P

SEG = 8
SIDE = 7


epsilon = 1e-05


def framed(values):
    return values.reshape(-1, SIDE, SIDE, values.shape[-1])


def shifted(frame_grid, row_step, col_step, dilation):
    padded = jnp.pad(frame_grid, ((0, 0), (dilation, dilation), (dilation, dilation), (0, 0)))
    return padded[
        :,
        dilation + row_step : dilation + row_step + SIDE,
        dilation + col_step : dilation + col_step + SIDE,
        :,
    ]


def depthwise(values, kernel, dilation):
    frame_grid = framed(values)
    running = jnp.zeros_like(frame_grid)
    for tap_index in range(9):
        running = (
            running
            + shifted(
                frame_grid,
                (tap_index // 3 - 1) * dilation,
                (tap_index % 3 - 1) * dilation,
                dilation,
            )
            * kernel[tap_index]
        )
    return running.reshape(values.shape)


def patch_rows(values):
    frame_grid = framed(values)
    pieces = [
        shifted(frame_grid, tap_index // 3 - 1, tap_index % 3 - 1, 1) for tap_index in range(9)
    ]
    return jnp.concatenate(pieces, axis=-1).reshape(values.shape[0], 9 * values.shape[1])


def unpatch(grad_rows, chan_width):
    frame_grid = grad_rows.reshape(-1, SIDE, SIDE, 9, chan_width)
    running = jnp.zeros(frame_grid.shape[:3] + (chan_width,), jnp.float32)
    for tap_index in range(9):
        running = running + shifted(
            frame_grid[:, :, :, tap_index, :], 1 - tap_index // 3, 1 - tap_index % 3, 1
        )
    return running.reshape(-1, chan_width)


def neighbours(values, boundary):
    clip_count = boundary.shape[0]
    frame_grid = values.reshape(clip_count, SEG, SIDE * SIDE, values.shape[-1])
    stop_mask = (boundary == 1)[:, :, None, None]
    start_mask = jnp.concatenate([jnp.ones_like(stop_mask[:, :1]), stop_mask[:, :-1]], axis=1)
    after_seg = jnp.concatenate([frame_grid[:, 1:], frame_grid[:, -1:]], axis=1)
    before = jnp.concatenate([frame_grid[:, :1], frame_grid[:, :-1]], axis=1)
    later_seg = jnp.where(stop_mask, frame_grid, after_seg)
    earlier = jnp.where(start_mask, frame_grid, before)
    return (later_seg.reshape(values.shape), earlier.reshape(values.shape))


def temporal(values, kernels, gate_vec, boundary, short_range):
    later_seg, earlier = neighbours(values, boundary)
    if short_range:
        return values + depthwise(later_seg - earlier, kernels[0], 1)
    change = later_seg - values
    logits = depthwise(change, kernels[1], 1) + depthwise(change, kernels[2], 2) + gate_vec
    return values + values * jax.nn.sigmoid(logits)


def columns(values, col_start, col_share):
    return lax.dynamic_slice_in_dim(values, col_start, col_share, values.ndim - 1)


def contract(left, right, left_dim, right_dim):
    return lax.dot_general(
        left, right, (((left_dim,), (right_dim,)), ((), ())), preferred_element_type=jnp.float32
    )


def normalize(values, gain_vec, bias_vec, pixel_total):
    col_sum, sq_sum = lax.psum((jnp.sum(values, axis=0), jnp.sum(values * values, axis=0)), "clip")
    mean_val = col_sum / pixel_total
    inv_std = lax.rsqrt(sq_sum / pixel_total - mean_val * mean_val + epsilon)
    centred = (values - mean_val) * inv_std
    return (centred * gain_vec + bias_vec, centred, inv_std)


def normalize_back(grad_rows, centred, inv_std, gain_vec, pixel_total):
    shift_sum, gain_sum = lax.psum(
        (jnp.sum(grad_rows, axis=0), jnp.sum(grad_rows * centred, axis=0)), "clip"
    )
    grad_in = inv_std * gain_vec * (grad_rows - (shift_sum + centred * gain_sum) / pixel_total)
    return (grad_in, gain_sum, shift_sum)


def block_forward(inputs, boundary, weights, short_range, pixel_total):
    w_red, gain_pair, bias_pair, w_cv, w_ex, gain_out, bias_out, kernels, gate_vec = weights
    reduced = jnp.dot(inputs, w_red, preferred_element_type=jnp.float32)
    norm_one, centred_one, inv_one = normalize(reduced, gain_pair[0], bias_pair[0], pixel_total)
    hidden, gelu_one = jax.vjp(jax.nn.gelu, norm_one)
    mixed_act, mix_back = jax.vjp(
        partial(temporal, boundary=boundary, short_range=short_range), hidden, kernels, gate_vec
    )
    gathered = lax.all_gather(mixed_act.astype(jnp.bfloat16), "chan", axis=1, tiled=True)
    patches = patch_rows(gathered)
    conv_out = jnp.dot(
        patches, w_cv.reshape(-1, w_cv.shape[-1]), preferred_element_type=jnp.float32
    )
    norm_two, centred_two, inv_two = normalize(conv_out, gain_pair[1], bias_pair[1], pixel_total)
    inner_full, gelu_two = jax.vjp(jax.nn.gelu, norm_two)
    inner_act = inner_full.astype(jnp.bfloat16)
    partial_out = jnp.dot(inner_act, w_ex, preferred_element_type=jnp.float32)
    expanded = lax.psum(partial_out.astype(jnp.bfloat16), "chan").astype(jnp.float32)
    norm_three, centred_three, inv_three = normalize(expanded, gain_out, bias_out, pixel_total)
    output_full, gelu_three = jax.vjp(jax.nn.gelu, norm_three + inputs.astype(jnp.float32))
    kept_state = (
        centred_one,
        inv_one,
        gelu_one,
        mix_back,
        patches,
        centred_two,
        inv_two,
        gelu_two,
        inner_act,
        centred_three,
        inv_three,
        gelu_three,
        gain_out,
    )
    return (output_full.astype(jnp.bfloat16), kept_state)


def block_backward(grad_out, inputs, weights, kept_state, pixel_total):
    w_red, gain_pair, bias_pair, w_cv, w_ex, gain_out, bias_out, kernels, gate_vec = weights
    (
        centred_one,
        inv_one,
        gelu_one,
        mix_back,
        patches,
        centred_two,
        inv_two,
        gelu_two,
        inner_act,
        centred_three,
        inv_three,
        gelu_three,
        gain_use,
    ) = kept_state
    grad_pre = gelu_three(grad_out)[0]
    grad_exp, gain_three, bias_three = normalize_back(
        grad_pre, centred_three, inv_three, gain_use, pixel_total
    )
    low_exp = grad_exp.astype(jnp.bfloat16)
    grad_wex = contract(inner_act, low_exp, 0, 0)
    grad_inner = contract(low_exp, w_ex, 1, 1)
    grad_two = gelu_two(grad_inner)[0]
    grad_cv, gain_two, bias_two = normalize_back(
        grad_two, centred_two, inv_two, gain_pair[1], pixel_total
    )
    low_cv = grad_cv.astype(jnp.bfloat16)
    flat_cv = w_cv.reshape(-1, w_cv.shape[-1])
    grad_wcv = contract(patches, low_cv, 0, 0).reshape(w_cv.shape)
    grad_patch = contract(low_cv, flat_cv, 1, 1)
    grad_mixed = lax.psum_scatter(
        unpatch(grad_patch, w_cv.shape[1]).astype(jnp.bfloat16),
        "chan",
        scatter_dimension=1,
        tiled=True,
    ).astype(jnp.float32)
    grad_hidden, grad_kern, grad_gate = mix_back(grad_mixed)
    grad_one = gelu_one(grad_hidden)[0]
    grad_red, gain_one, bias_one = normalize_back(
        grad_one, centred_one, inv_one, gain_pair[0], pixel_total
    )
    low_red = grad_red.astype(jnp.bfloat16)
    grad_wred = contract(inputs, low_red, 0, 0)
    partial_in = contract(low_red, w_red, 1, 1)
    grad_in = grad_pre + lax.psum(partial_in.astype(jnp.bfloat16), "chan").astype(jnp.float32)
    weight_terms = (grad_wred, grad_wcv, grad_wex, grad_kern, grad_gate)
    norm_terms = (gain_one, bias_one, gain_two, bias_two, gain_three, bias_three)
    return (grad_in, weight_terms, norm_terms)


def body(
    frames_in,
    boundary,
    w_reduce,
    gain_inner,
    bias_inner,
    w_conv,
    w_expand,
    gain_outer,
    bias_outer,
    depth_kernels,
    gate_bias,
    cotangent,
):
    row_count = frames_in.shape[0]
    pixel_total = row_count * lax.axis_size("clip")
    col_share = frames_in.shape[1] // lax.axis_size("chan")
    col_start = lax.axis_index("chan") * col_share
    block_weights = [
        (
            w_reduce[block_index],
            gain_inner[block_index],
            bias_inner[block_index],
            w_conv[block_index],
            w_expand[block_index],
            gain_outer[block_index],
            bias_outer[block_index],
            depth_kernels,
            gate_bias,
        )
        for block_index in range(2)
    ]
    first_out, kept_zero = block_forward(frames_in, boundary, block_weights[0], True, pixel_total)
    final_out, kept_one = block_forward(first_out, boundary, block_weights[1], False, pixel_total)
    layer_inputs = [frames_in, first_out]
    kept_states = [kept_zero, kept_one]
    grad_flow = cotangent.astype(jnp.float32)
    weight_sums = [None, None]
    norm_sums = [None, None]
    for block_index in (1, 0):
        grad_flow, weight_terms, norm_terms = block_backward(
            grad_flow,
            layer_inputs[block_index],
            block_weights[block_index],
            kept_states[block_index],
            pixel_total,
        )
        grad_wred, grad_wcv, grad_wex, grad_kern, grad_gate = weight_terms
        weight_terms = (
            lax.psum(grad_wred.astype(jnp.bfloat16), "clip").astype(jnp.float32),
            lax.psum(grad_wcv.astype(jnp.bfloat16), "clip").astype(jnp.float32),
            lax.psum(grad_wex.astype(jnp.bfloat16), "clip").astype(jnp.float32),
            lax.psum(grad_kern.astype(jnp.bfloat16), "clip").astype(jnp.float32),
            lax.psum(grad_gate.astype(jnp.bfloat16), "clip").astype(jnp.float32),
        )
        weight_sums[block_index] = weight_terms
        norm_sums[block_index] = norm_terms
    grad_reduce = jnp.stack([weight_sums[0][0], weight_sums[1][0]])
    grad_conv = jnp.stack([weight_sums[0][1], weight_sums[1][1]])
    grad_expand = jnp.stack([weight_sums[0][2], weight_sums[1][2]])
    grad_kernels = weight_sums[0][3] + weight_sums[1][3]
    grad_gate_bias = weight_sums[0][4] + weight_sums[1][4]
    grad_gain_inner = jnp.stack(
        [
            jnp.stack([norm_sums[0][0], norm_sums[0][2]]),
            jnp.stack([norm_sums[1][0], norm_sums[1][2]]),
        ]
    )
    grad_bias_inner = jnp.stack(
        [
            jnp.stack([norm_sums[0][1], norm_sums[0][3]]),
            jnp.stack([norm_sums[1][1], norm_sums[1][3]]),
        ]
    )
    grad_gain_outer = jnp.stack([norm_sums[0][4], norm_sums[1][4]])
    grad_bias_outer = jnp.stack([norm_sums[0][5], norm_sums[1][5]])
    activations = columns(final_out, col_start, col_share)
    input_grad = columns(grad_flow, col_start, col_share)
    grad_gain_outer = columns(grad_gain_outer, col_start, col_share)
    grad_bias_outer = columns(grad_bias_outer, col_start, col_share)
    return (
        activations,
        input_grad,
        grad_reduce,
        grad_gain_inner,
        grad_bias_inner,
        grad_conv,
        grad_expand,
        grad_gain_outer,
        grad_bias_outer,
        grad_kernels,
        grad_gate_bias,
    )


def solution(mesh):
    in_specs = (
        P("clip", None),
        P("clip", None),
        P(None, None, "chan"),
        P(None, None, "chan"),
        P(None, None, "chan"),
        P(None, None, None, "chan"),
        P(None, "chan", None),
        P(),
        P(),
        P(None, None, "chan"),
        P("chan"),
        P("clip", None),
    )
    out_specs = (
        P("clip", "chan"),
        P("clip", "chan"),
        P(None, None, "chan"),
        P(None, None, "chan"),
        P(None, None, "chan"),
        P(None, None, None, "chan"),
        P(None, "chan", None),
        P(None, "chan"),
        P(None, "chan"),
        P(None, None, "chan"),
        P("chan"),
    )
    return jax.shard_map(body, mesh=mesh, in_specs=in_specs, out_specs=out_specs, check_vma=False)
```

profile of v0, /device:TPU:0, one launch (start us, length us, event | category | flops | bytes accessed | tf_op | source)
XLA Modules:
  0.0 1076.2 jit_solution(8303554137502079923)
XLA Ops:
  16.0 23.1 %all-reduce.91 = (f32[128]{0:T(128)S(1)}, f32[128]{0:T(128)S(1)}) all-reduce(f32[128]{0:T(128)S(1)} %get-tuple-element.93, f32[128]{0:T(128)S(1)} %get-tuple-element.92), channel_id=1, replica_groups=mesh['clip'=8,'chan'=4] {'clip'}, use_global_device_ids=true, to_apply=%region_3.0 | all-reduce | flops 256 | bytes 2048 | tf_op jit(solution)/shard_map/psum | solution.py:96
  47.6 9.2 all_gather.6
  82.4 17.1 %all-reduce.90 = (f32[128]{0:T(128)S(1)}, f32[128]{0:T(128)S(1)}) all-reduce(f32[128]{0:T(128)S(1)} %get-tuple-element.91, f32[128]{0:T(128)S(1)} %get-tuple-element.90), channel_id=1, replica_groups=mesh['clip'=8,'chan'=4] {'clip'}, use_global_device_ids=true, to_apply=%region_7.8 | all-reduce | flops 256 | bytes 2048 | tf_op jit(solution)/shard_map/psum | solution.py:96
  103.1 66.7 %all-reduce.100.cloned.1.call-done = bf16[784,2048]{1,0:T(8,128)(2,1)} async-done(((bf16[784,2048]{1,0:T(8,128)(2,1)}), bf16[784,2048]{1,0:T(8,128)(2,1)}) %all-reduce.100.cloned.1.call-update) | async-done | bytes 3211280 | tf_op jit(solution)/shard_map/psum | solution.py:128
  172.8 37.4 %all-reduce.89 = (f32[2048]{0:T(1024)S(1)}, f32[2048]{0:T(1024)S(1)}) all-reduce(f32[2048]{0:T(1024)S(1)} %get-tuple-element.51, f32[2048]{0:T(1024)S(1)} %get-tuple-element.50), channel_id=1, replica_groups=mesh['clip'=8,'chan'=4] {'clip'}, use_global_device_ids=true, to_apply=%region_12.13 | all-reduce | flops 4096 | bytes 32768 | tf_op jit(solution)/shard_map/psum | solution.py:96
  218.6 17.2 %all-reduce.88 = (f32[128]{0:T(128)S(1)}, f32[128]{0:T(128)S(1)}) all-reduce(f32[128]{0:T(128)S(1)} %get-tuple-element.89, f32[128]{0:T(128)S(1)} %get-tuple-element.88), channel_id=1, replica_groups=mesh['clip'=8,'chan'=4] {'clip'}, use_global_device_ids=true, to_apply=%region_16.17 | all-reduce | flops 256 | bytes 2048 | tf_op jit(solution)/shard_map/psum | solution.py:96
  299.7 19.3 %all-reduce.87 = (f32[128]{0:T(128)S(1)}, f32[128]{0:T(128)S(1)}) all-reduce(f32[128]{0:T(128)S(1)} %get-tuple-element.87, f32[128]{0:T(128)S(1)} %get-tuple-element.86), channel_id=1, replica_groups=mesh['clip'=8,'chan'=4] {'clip'}, use_global_device_ids=true, to_apply=%region_20.21 | all-reduce | flops 256 | bytes 2048 | tf_op jit(solution)/shard_map/psum | solution.py:96
  323.5 66.7 %all-reduce.102.cloned.1.call-done = bf16[784,2048]{1,0:T(8,128)(2,1)} async-done(((bf16[784,2048]{1,0:T(8,128)(2,1)}), bf16[784,2048]{1,0:T(8,128)(2,1)}) %all-reduce.102.cloned.1.call-update) | async-done | bytes 3211280 | tf_op jit(solution)/shard_map/psum | solution.py:128
  393.1 37.1 %all-reduce.86 = (f32[2048]{0:T(1024)S(1)}, f32[2048]{0:T(1024)S(1)}) all-reduce(f32[2048]{0:T(1024)S(1)} %get-tuple-element.49, f32[2048]{0:T(1024)S(1)} %get-tuple-element.48), channel_id=1, replica_groups=mesh['clip'=8,'chan'=4] {'clip'}, use_global_device_ids=true, to_apply=%region_25.26 | all-reduce | flops 4096 | bytes 32768 | tf_op jit(solution)/shard_map/psum | solution.py:96
  430.2 11.5 %fusion.173 = (f32[2048]{0:T(1024)S(1)}, f32[2048]{0:T(1024)S(1)}, f32[784,2048]{1,0:T(8,128)}, f32[784,2048]{1,0:T(8,128)}) fusion(f32[2048]{0:T(1024)S(1)} %get-tuple-element.230, f32[2048]{0:T(1024)S(1)} %get-tuple-element.236, bf16[784,2048]{1,0:T(8,128)(2,1)} %all-reduce.102.cloned.1.call-done, bf16[784,2048]{1,0:T(8,128)(2,1)} %param.23, ...), kind=kLoop, calls=%fused_computation.478 | loop fusion | flops 48164864 | bytes 22528000 | tf_op jit(solution)/shard_map/reduce_sum | solution.py:105
  441.7 33.0 %all-reduce.85 = (f32[2048]{0:T(1024)S(1)}, f32[2048]{0:T(1024)S(1)}) all-reduce(f32[2048]{0:T(1024)S(1)} %get-tuple-element.47, f32[2048]{0:T(1024)S(1)} %get-tuple-element.46), channel_id=1, replica_groups=mesh['clip'=8,'chan'=4] {'clip'}, use_global_device_ids=true, to_apply=%region_29.30 | all-reduce | flops 4096 | bytes 32768 | tf_op jit(solution)/shard_map/psum | solution.py:104
  482.3 17.5 %all-reduce.84 = (f32[128]{0:T(128)S(1)}, f32[128]{0:T(128)S(1)}) all-reduce(f32[128]{0:T(128)S(1)} %get-tuple-element.85, f32[128]{0:T(128)S(1)} %get-tuple-element.84), channel_id=1, replica_groups=mesh['clip'=8,'chan'=4] {'clip'}, use_global_device_ids=true, to_apply=%region_33.34 | all-reduce | flops 256 | bytes 2048 | tf_op jit(solution)/shard_map/psum | solution.py:104
  510.5 10.2 slice_bitcast_fusion.9
  531.5 22.0 %reduce-scatter.7.cloned.1.call-done = bf16[128,784]{1,0:T(8,128)(2,1)} async-done(((bf16[512,784]{1,0:T(8,128)(2,1)}), bf16[128,784]{1,0:T(8,128)(2,1)}) %reduce-scatter.7.cloned.1.call-update) | async-done | bytes 200720
  578.2 21.3 %all-reduce.83 = (f32[128]{0:T(128)S(1)}, f32[128]{0:T(128)S(1)}) all-reduce(f32[128]{0:T(128)S(1)} %get-tuple-element.83, f32[128]{0:T(128)S(1)} %get-tuple-element.82), channel_id=1, replica_groups=mesh['clip'=8,'chan'=4] {'clip'}, use_global_device_ids=true, to_apply=%region_38.39 | all-reduce | flops 256 | bytes 2048 | tf_op jit(solution)/shard_map/psum | solution.py:104
  605.5 65.8 %all-reduce.104.cloned.1.call-done = bf16[784,2048]{1,0:T(8,128)(2,1)} async-done(((bf16[784,2048]{1,0:T(8,128)(2,1)}), bf16[784,2048]{1,0:T(8,128)(2,1)}) %all-reduce.104.cloned.1.call-update) | async-done | bytes 3211280 | tf_op jit(solution)/shard_map/psum | solution.py:195
  671.3 11.2 %fusion.172 = (f32[2048]{0:T(1024)S(1)}, f32[2048]{0:T(1024)S(1)}, f32[784,2048]{1,0:T(8,128)}) fusion(f32[2048]{0:T(1024)S(1)} %get-tuple-element.228, f32[2048]{0:T(1024)S(1)} %get-tuple-element.235, bf16[784,2048]{1,0:T(8,128)(2,1)S(1)} %copy-done, bf16[784,2048]{1,0:T(8,128)(2,1)} %param.12, f32[2048]{0:T(1024)S(1)} %bitcast.333, ...), kind=kLoop, calls=%fused_computation.477 | loop fusion | flops 49770496 | bytes 22528000 | tf_op jit(solution)/shard_map/reduce_sum | solution.py:105
  682.5 37.1 %all-reduce.82 = (f32[2048]{0:T(1024)S(1)}, f32[2048]{0:T(1024)S(1)}) all-reduce(f32[2048]{0:T(1024)S(1)} %get-tuple-element.45, f32[2048]{0:T(1024)S(1)} %get-tuple-element.44), channel_id=1, replica_groups=mesh['clip'=8,'chan'=4] {'clip'}, use_global_device_ids=true, to_apply=%region_43.44 | all-reduce | flops 4096 | bytes 32768 | tf_op jit(solution)/shard_map/psum | solution.py:104
  726.3 17.5 %all-reduce.81 = (f32[128]{0:T(128)S(1)}, f32[128]{0:T(128)S(1)}) all-reduce(f32[128]{0:T(128)S(1)} %get-tuple-element.81, f32[128]{0:T(128)S(1)} %get-tuple-element.80), channel_id=1, replica_groups=mesh['clip'=8,'chan'=4] {'clip'}, use_global_device_ids=true, to_apply=%region_47.48 | all-reduce | flops 256 | bytes 2048 | tf_op jit(solution)/shard_map/psum | solution.py:104
  767.8 11.2 %copy.104 = bf16[4608,784]{1,0:T(8,128)(2,1)} copy(bf16[4608,784]{0,1:T(8,128)(2,1)} %bitcast.313) | data formatting | bytes 14450688 | tf_op jit(solution)/shard_map/dot_general | solution.py:90
  779.0 11.2 %copy.106 = bf16[4608,784]{1,0:T(8,128)(2,1)} copy(bf16[4608,784]{0,1:T(8,128)(2,1)} %bitcast.314) | data formatting | bytes 14450688 | tf_op jit(solution)/shard_map/dot_general | solution.py:90
  802.0 19.3 %all-reduce.80 = (f32[128]{0:T(128)S(1)}, f32[128]{0:T(128)S(1)}) all-reduce(f32[128]{0:T(128)S(1)} %get-tuple-element.79, f32[128]{0:T(128)S(1)} %get-tuple-element.78), channel_id=1, replica_groups=mesh['clip'=8,'chan'=4] {'clip'}, use_global_device_ids=true, to_apply=%region_52.53 | all-reduce | flops 256 | bytes 2048 | tf_op jit(solution)/shard_map/psum | solution.py:104
  849.5 33.1 %all-reduce.92 = (bf16[3,9,128]{2,1,0:T(8,128)(2,1)S(1)}, bf16[3,9,128]{2,1,0:T(8,128)(2,1)S(1)}, bf16[128]{0:T(256)(128)(2,1)S(1)}) all-reduce(bf16[3,9,128]{2,1,0:T(8,128)(2,1)S(1)} %add_convert_fusion.1, bf16[3,9,128]{2,1,0:T(8,128)(2,1)S(1)} %pad.480, bf16[128]{0:T(256)(128)(2,1)S(1)} %copy-done.121), channel_id=1, replica_groups=mesh['clip'=8,'chan'=4] {'clip'}, use_global_device_ids=true, to_apply=%region_87.88 | all-reduce | flops 7040 | bytes 28160 | tf_op jit(solution)/shard_map/psum | solution.py:253
  893.2 167.3 %all-reduce.108.cloned.1.call-done = (bf16[1,2048,128]{1,2,0:T(8,128)(2,1)}, bf16[1,2048,128]{1,2,0:T(8,128)(2,1)}, bf16[1,9,512,128]{3,2,1,0:T(8,128)(2,1)}, bf...) async-done(((bf16[1,2048,128]{1,2,0:T(8,128)(2,1)}, bf16[1,2048,128]{1,2,0:T(8,128)(2,1)}, ...) | async-done | bytes 4456464 | tf_op jit(solution)/shard_map/psum | solution.py:250
  (478 shorter events, 276.7 us)
Async XLA Ops:
  7.2 162.6 %all-reduce.100.cloned.1.call-start = ((), (), s32[]{:S(2)}) async-start(), calls=%async_computation.2 | async-start | bytes 6422528 | tf_op jit(solution)/shard_map/psum | solution.py:128
  7.9 32.3 %copy-start.60 = (pred[2,8]{1,0:T(4,128)(4,1)}, pred[2,8]{1,0:T(4,128)(4,1)S(1)}, u32[]{:S(2)}) copy-start(pred[2,8]{1,0:T(4,128)(4,1)S(1)} %broadcast_compare_fusion) | copy-start | bytes 52
  10.0 33.2 %copy-start.69 = (f32[128]{0:T(128)}, f32[128]{0:T(128)S(1)}, u32[]{:S(2)}) copy-start(f32[128]{0:T(128)S(1)} %get-tuple-element.221) | copy-start | bytes 1540
  10.0 33.2 %copy-start.71 = (f32[128]{0:T(128)}, f32[128]{0:T(128)S(1)}, u32[]{:S(2)}) copy-start(f32[128]{0:T(128)S(1)} %get-tuple-element.220) | copy-start | bytes 1540
  10.0 33.2 %copy-start.73 = (f32[128]{0:T(128)}, f32[128]{0:T(128)S(1)}, u32[]{:S(2)}) copy-start(f32[128]{0:T(128)S(1)} %get-tuple-element.222) | copy-start | bytes 1540
  10.0 33.2 %copy-start.75 = (f32[128]{0:T(128)}, f32[128]{0:T(128)S(1)}, u32[]{:S(2)}) copy-start(f32[128]{0:T(128)S(1)} %get-tuple-element.223) | copy-start | bytes 1540
  10.0 33.2 %copy-start.77 = (f32[128]{0:T(128)}, f32[128]{0:T(128)S(1)}, u32[]{:S(2)}) copy-start(f32[128]{0:T(128)S(1)} %get-tuple-element.224) | copy-start | bytes 1540
  10.0 33.2 %copy-start.79 = (f32[128]{0:T(128)}, f32[128]{0:T(128)S(1)}, u32[]{:S(2)}) copy-start(f32[128]{0:T(128)S(1)} %get-tuple-element.225) | copy-start | bytes 1540
  11.6 31.7 %copy-start.81 = (f32[128]{0:T(128)}, f32[128]{0:T(128)S(1)}, u32[]{:S(2)}) copy-start(f32[128]{0:T(128)S(1)} %get-tuple-element.216) | copy-start | bytes 1540
  11.6 31.7 %copy-start.83 = (f32[128]{0:T(128)}, f32[128]{0:T(128)S(1)}, u32[]{:S(2)}) copy-start(f32[128]{0:T(128)S(1)} %get-tuple-element.217) | copy-start | bytes 1540
  11.6 31.7 %copy-start.85 = (f32[128]{0:T(128)}, f32[128]{0:T(128)S(1)}, u32[]{:S(2)}) copy-start(f32[128]{0:T(128)S(1)} %get-tuple-element.218) | copy-start | bytes 1540
  12.9 33.4 %copy-start.56 = (f32[128]{0:T(128)}, f32[128]{0:T(128)S(1)}, u32[]{:S(2)}) copy-start(f32[128]{0:T(128)S(1)} %get-tuple-element.247) | copy-start | bytes 1540
  12.9 33.4 %copy-start.58 = (f32[128]{0:T(128)}, f32[128]{0:T(128)S(1)}, u32[]{:S(2)}) copy-start(f32[128]{0:T(128)S(1)} %get-tuple-element.266) | copy-start | bytes 1540
  102.3 287.9 %all-reduce.102.cloned.1.call-start = ((), (), s32[]{:S(2)}) async-start(), calls=%async_computation.3 | async-start | bytes 6422528 | tf_op jit(solution)/shard_map/psum | solution.py:128
  169.7 40.4 %copy-start = (bf16[784,2048]{1,0:T(8,128)(2,1)S(1)}, bf16[784,2048]{1,0:T(8,128)(2,1)}, u32[]{:S(2)}) copy-start(bf16[784,2048]{1,0:T(8,128)(2,1)} %all-reduce.100.cloned.1.call-done) | copy-start | bytes 9633796
  323.5 230.1 %reduce-scatter.7.cloned.1.call-start = ((), (), s32[]{:S(2)}) async-start(), calls=%async_computation.6 | async-start | bytes 1146880
  531.4 34.9 %copy-start.95 = (f32[128]{0:T(128)S(1)}, f32[128]{0:T(128)}, u32[]{:S(2)}) copy-start(f32[128]{0:T(128)} %get-tuple-element.202) | copy-start | bytes 1540
  531.4 34.9 %copy-start.97 = (f32[128]{0:T(128)S(1)}, f32[128]{0:T(128)}, u32[]{:S(2)}) copy-start(f32[128]{0:T(128)} %get-tuple-element.204) | copy-start | bytes 1540
  531.4 34.9 %copy-start.99 = (f32[128]{0:T(128)S(1)}, f32[128]{0:T(128)}, u32[]{:S(2)}) copy-start(f32[128]{0:T(128)} %get-tuple-element.205) | copy-start | bytes 1540
  531.4 34.9 %copy-start.101 = (f32[128]{0:T(128)S(1)}, f32[128]{0:T(128)}, u32[]{:S(2)}) copy-start(f32[128]{0:T(128)} %get-tuple-element.206) | copy-start | bytes 1540
  531.4 139.8 %all-reduce.104.cloned.1.call-start = ((), (), s32[]{:S(2)}) async-start(), calls=%async_computation.4 | async-start | bytes 6422528 | tf_op jit(solution)/shard_map/psum | solution.py:195
  605.3 191.7 %reduce-scatter.9.cloned.1.call-start = ((), (), s32[]{:S(2)}) async-start(), calls=%async_computation.7 | async-start | bytes 1146880
  767.8 122.4 %all-reduce.106.cloned.1.call-start = ((), (), s32[]{:S(2)}) async-start(), calls=%async_computation.5 | async-start | bytes 6422528 | tf_op jit(solution)/shard_map/psum | solution.py:195
  824.1 236.4 %all-reduce.108.cloned.1.call-start = ((), (), s32[]{:S(2)}) async-start(), calls=%async_computation.8 | async-start | bytes 8912896 | tf_op jit(solution)/shard_map/psum | solution.py:250
  (130 other events, 1010.3 us)
Sparse Core Ops, SparseCore 0:
  102.4 67.2 all-reduce.99
  323.6 66.5 all-reduce.101
  531.6 21.9 reduce-scatter.6
  605.4 65.8 all-reduce.103
  767.9 21.9 reduce-scatter.8
  824.2 65.9 all-reduce.105
  895.2 165.2 all-reduce.107
where the time goes:
time: 1090 us; the launch traced here: 1080 us
  waiting for transfers between devices  394 us (36%)
  blocking collectives  348 us (32%)
  local copies, waits for them, and re-layouts  140 us (13%)
  other arithmetic  113 us (10%)
  matrix products  65.1 us (6%)
  between operations  16.5 us (2%)
    psum x1, waiting for transfers between devices, body(): lax.psum(grad_wred.astype(jnp.bfloat16), 'clip').astype(jnp.float32)  167 us
    psum x6, blocking collectives, normalize(): lax.psum((jnp.sum(values, axis=0), jnp.sum(values * values, axis=0)), 'cl...  151 us
    psum x6, blocking collectives, normalize_back(): lax.psum((jnp.sum(grad_rows, axis=0), jnp.sum(grad_rows * centred, axis=0...  146 us
    psum x2, waiting for transfers between devices, block_forward(): lax.psum(partial_out.astype(jnp.bfloat16), 'chan').astype(jnp.float32)  133 us
    psum x2, waiting for transfers between devices, block_backward(): lax.psum(partial_in.astype(jnp.bfloat16), 'chan').astype(jnp.float32)  71 us
    dot_general x12, matrix products, contract(): lax.dot_general(left, right, (((left_dim,), (right_dim,)), ((), ())), pre...  48.9 us
    psum x1, blocking collectives, body(): lax.psum(grad_kern.astype(jnp.bfloat16), 'clip').astype(jnp.float32)  33.1 us
    concatenate x18, local copies, waits for them, and re-layouts, patch_rows(): jnp.concatenate(pieces, axis=-1)  29.7 us
  transfers between devices with their start and end apart: 7, of which 6 were waited for; matrix products, arithmetic and copies ran while one was open for 5% of the time, Pallas kernels for 0%

commit v1 on v0

--- a/solution.py
+++ b/solution.py
@@ -1,8 +1,11 @@
 from functools import partial
+from types import SimpleNamespace
 
 import jax
 import jax.numpy as jnp
 from jax import lax
+from jax.experimental import pallas as pl
+from jax.experimental.pallas import tpu as pltpu
 from jax.sharding import PartitionSpec as P
 
 SEG = 8
@@ -293,6 +296,822 @@
     )
 
 
+MESH = pl.DeviceIdType.MESH
+LANES = 128
+FRAME = SIDE * 8
+PAIR = 2 * FRAME
+GELU_A = 0.7978845608028654
+GELU_B = 0.044715
+COPIES = 224
+LOADS = 40
+
+
+def fused_fits(mesh, frame_shape, reduce_shape):
+    n_clip, n_chan = mesh.shape["clip"], mesh.shape["chan"]
+    share = reduce_shape[2] // n_chan
+    frames = frame_shape[0] // (n_clip * SIDE * SIDE)
+    return n_chan == 4 and share == LANES and frames == 2 * SEG
+
+
+def gelu(z):
+    return 0.5 * z * (1.0 + jnp.tanh(GELU_A * (z + GELU_B * z * z * z)))
+
+
+def gelu_both(z):
+    square = z * z
+    t = jnp.tanh(GELU_A * (z + GELU_B * square * z))
+    slope = 0.5 * (1.0 + t) + 0.5 * z * (1.0 - t * t) * (GELU_A * (1.0 + 3.0 * GELU_B * square))
+    return 0.5 * z * (1.0 + t), slope
+
+
+def real_columns(shape):
+    return lax.rem(lax.broadcasted_iota(jnp.int32, shape, len(shape) - 2), 8) < SIDE
+
+
+def real(values):
+    return jnp.where(real_columns(values.shape), values, 0.0)
+
+
+def fold(values):
+    return jnp.sum(values.reshape(-1, 8, values.shape[-1]), axis=0)
+
+
+def tiles(values):
+    return values.reshape(SIDE, 8, values.shape[-1])
+
+
+def flat(values):
+    return values.reshape(FRAME, values.shape[-1])
+
+
+def row_pad(v, reach):
+    zeros = jnp.zeros((reach,) + v.shape[1:], v.dtype)
+    return jnp.concatenate([zeros, v, zeros], axis=0)
+
+
+def col_shift(v, step):
+    if step == 0:
+        return v
+    moved = pltpu.roll(v, (-step) % 8, v.ndim - 2)
+    if abs(step) == 2:
+        place = lax.broadcasted_iota(jnp.int32, v.shape, v.ndim - 2)
+        moved = jnp.where(place < 6 if step > 0 else place >= 2, moved, 0.0)
+    return moved
+
+
+def dw_tiles(v, taps, reach, sign):
+    padded = row_pad(v, reach)
+    total = None
+    for b in (-1, 0, 1):
+        part = None
+        for a in (-1, 0, 1):
+            start = reach + sign * reach * a
+            term = taps[3 * (a + 1) + b + 1] * padded[start : start + SIDE]
+            part = term if part is None else part + term
+        part = col_shift(part, sign * reach * b)
+        total = part if total is None else total + part
+    return total
+
+
+def dot(left, right, left_dim=1, right_dim=0):
+    return lax.dot_general(
+        left, right, (((left_dim,), (right_dim,)), ((), ())), preferred_element_type=jnp.float32
+    )
+
+
+NAMES = (
+    "x_hbm", "cot_hbm", "wred_hbm", "wconv_hbm", "wexp_hbm", "bnd", "gi", "bi", "go", "bo",
+    "dk", "gb", "act_out", "gin_out", "ggi", "gbi", "ggo", "gbo", "gk_out", "ggb_out", "gc_out",
+    "ge_out", "gr_out", "x", "cot", "wr0", "wrf", "wef", "wc", "dkb", "red", "hid", "sig",
+    "conv", "mixf", "inf", "ex", "out0", "act", "y", "gpre", "gin", "gexp", "gs", "pb", "ysend",
+    "rcore", "ryy", "grf", "gm", "gd", "g1", "gk", "kst", "stn", "stw", "gc", "geo", "ge",
+    "gro", "gr", "ssem", "rsem", "lsem",
+)
+
+
+def fused_kernel(n_clip, n_chan, pixel_total, *refs):
+    r = SimpleNamespace(**dict(zip(NAMES, refs)))
+    rows, cs = r.cot.shape
+    ib = LANES
+    inner = ib * n_chan
+    chunk = rows // 2
+    frames = rows // FRAME
+    bf16, f32 = jnp.bfloat16, jnp.float32
+    clip = lax.axis_index("clip")
+    chan = lax.axis_index("chan")
+    core, high = lax.rem(chan, 2), lax.div(chan, 2)
+    j_core = (1 - core) + 2 * high
+    j_y = core + 2 * (1 - high)
+    j_far = (1 - core) + 2 * (1 - high)
+    others = (j_core, j_y, j_far)
+    clip_others = [lax.rem(clip + d, n_clip) for d in range(1, n_clip)]
+
+    def cols(j):
+        return pl.ds(pl.multiple_of(j * ib, ib), ib)
+
+    def wide(j):
+        return pl.ds(pl.multiple_of(j * cs, cs), cs)
+
+    def part(h):
+        return pl.ds(h * chunk, chunk)
+
+    counters = {"copy": 0, "load": 0}
+    unsent = []
+
+    def remote(src, dst, target):
+        index = counters["copy"]
+        counters["copy"] += 1
+        made = pltpu.make_async_remote_copy(
+            src_ref=src,
+            dst_ref=dst,
+            send_sem=r.ssem.at[index],
+            recv_sem=r.rsem.at[index],
+            device_id=target,
+            device_id_type=MESH,
+        )
+        made.start()
+        unsent.append(made)
+        return made
+
+    def sent(made):
+        made.wait_send()
+        unsent[:] = [other for other in unsent if other is not made]
+
+    def local(src, dst):
+        index = counters["load"]
+        counters["load"] += 1
+        made = pltpu.make_async_copy(src, dst, r.lsem.at[index])
+        made.start()
+        return made
+
+    load_wr0 = local(r.wred_hbm.at[0], r.wr0)
+    load_x = [local(r.x_hbm.at[part(h)], r.x.at[part(h)]) for h in range(2)]
+    load_we = [
+        local(r.wexp_hbm.at[s, :, wide(chan)], r.wef.at[s, cols(chan)]) for s in range(2)
+    ]
+    load_wr = [
+        local(r.wred_hbm.at[s, wide(chan)], r.wrf.at[s, :, cols(chan)]) for s in range(2)
+    ]
+    load_wc = [
+        [
+            local(r.wconv_hbm.at[s, tap], r.wc.at[s, :, tap * ib : (tap + 1) * ib])
+            for tap in range(9)
+        ]
+        for s in range(2)
+    ]
+    load_cot = local(r.cot_hbm, r.cot)
+
+    barrier = pltpu.get_barrier_semaphore()
+    for target in clip_others:
+        pl.semaphore_signal(barrier, inc=1, device_id=(target, chan), device_id_type=MESH)
+    for target in others:
+        pl.semaphore_signal(barrier, inc=1, device_id=(clip, target), device_id_type=MESH)
+    pl.semaphore_wait(barrier, n_clip - 1 + n_chan - 1)
+
+    def share_we(s):
+        return [
+            remote(r.wexp_hbm.at[s, :, wide(j)], r.wef.at[s, cols(chan)], (clip, j))
+            for j in others
+        ]
+
+    def share_wr(s):
+        return [
+            remote(r.wred_hbm.at[s, wide(j)], r.wrf.at[s, :, cols(chan)], (clip, j))
+            for j in others
+        ]
+
+    def arrive(copies):
+        for made in copies:
+            made.wait_recv()
+
+    def stat_start(buf, slot, values):
+        for k, value in enumerate(values):
+            buf[slot, clip, k : k + 1, :] = jnp.sum(value, axis=0, keepdims=True)
+        return [remote(buf.at[slot, clip], buf.at[slot, clip], (t, chan)) for t in clip_others]
+
+    def stat_end(buf, slot, copies):
+        arrive(copies)
+        total = buf[slot, 0]
+        for k in range(1, n_clip):
+            total = total + buf[slot, k]
+        return total[0:1], total[1:2]
+
+    def moments(pair):
+        mean = pair[0] / pixel_total
+        return mean, lax.rsqrt(pair[1] / pixel_total - mean * mean + epsilon)
+
+    def gather_start(full, h):
+        mine = full.at[part(h), cols(chan)]
+        return [remote(mine, mine, (clip, j_y)), remote(mine, mine, (clip, j_core))]
+
+    def gather_pass(full, h, copies):
+        copies[0].wait_recv()
+        theirs = full.at[part(h), cols(j_y)]
+        copies.append(remote(theirs, theirs, (clip, j_core)))
+
+    def gather_end(copies):
+        copies[1].wait_recv()
+        copies[2].wait_recv()
+
+    def scatter_start(slot, h):
+        return [
+            remote(r.pb.at[part(h), cols(j_far)], r.rcore.at[slot, 1, part(h)], (clip, j_core)),
+            remote(r.pb.at[part(h), cols(j_core)], r.rcore.at[slot, 0, part(h)], (clip, j_core)),
+        ]
+
+    def scatter_pass(slot, h, copies):
+        copies[0].wait_recv()
+        both = r.pb[part(h), cols(j_y)].astype(f32) + r.rcore[slot, 1, part(h)].astype(f32)
+        r.ysend[slot % 2, part(h)] = both.astype(bf16)
+        copies.append(
+            remote(r.ysend.at[slot % 2, part(h)], r.ryy.at[slot, part(h)], (clip, j_y))
+        )
+
+    def scatter_end(slot, h, copies):
+        copies[1].wait_recv()
+        copies[2].wait_recv()
+        sent(copies[0])
+        sent(copies[1])
+        sent(copies[2])
+
+    def scatter_value(slot, at):
+        mine = r.pb[at, cols(chan)].astype(f32)
+        return mine + r.rcore[slot, 0, at].astype(f32) + r.ryy[slot, at].astype(f32)
+
+    def keep_flag(f):
+        return 1.0 - r.bnd[lax.div(f, SEG), lax.rem(f, SEG)].astype(f32)
+
+    def taps_of(index):
+        return [r.dkb[9 * index + tap] for tap in range(9)]
+
+    def pair_rows(h, i):
+        return pl.ds(pl.multiple_of(h * chunk + i * PAIR, 16), PAIR)
+
+    def frame_rows(f):
+        return pl.ds(pl.multiple_of(f * FRAME, 8), FRAME)
+
+    pairs = frames // 4
+    zero_n = jnp.zeros((8, ib), f32)
+    zero_w = jnp.zeros((8, cs), f32)
+    STEP = 32
+    steps = rows // STEP
+
+    def step_rows(i):
+        return pl.ds(pl.multiple_of(i * STEP, STEP), STEP)
+
+    moments_in = [[None, None, None], [None, None, None]]
+
+    def row(ref, s, k=None):
+        return ref[s, k : k + 1, :] if k is not None else ref[s : s + 1, wide(chan)]
+
+    def norm_inner(s, k, x):
+        mean, inv = moments_in[s][k]
+        centred = (x - mean) * inv
+        return centred, centred * row(r.gi, s, k) + row(r.bi, s, k)
+
+    def norm_outer(s, x):
+        mean, inv = moments_in[s][2]
+        centred = (x - mean) * inv
+        return centred, centred * row(r.go, s) + row(r.bo, s)
+
+    def inner_input(s, at):
+        return r.x[at, wide(chan)] if s == 0 else r.out0[at]
+
+    def temporal_forward(s, h):
+        def hide(i, _):
+            at = pair_rows(h, i)
+            r.hid[s, at] = real(gelu(norm_inner(s, 0, r.red[s, at])[1]))
+            return _
+
+        lax.fori_loop(0, pairs, hide, 0)
+
+        def mix(i, before):
+            base = pl.multiple_of(h * chunk + i * PAIR, 16)
+            last = jnp.minimum(base + PAIR, (h + 1) * chunk - FRAME)
+            f = h * (frames // 2) + 2 * i
+            h0 = tiles(r.hid[s, pl.ds(base, FRAME)])
+            h1 = tiles(r.hid[s, pl.ds(base + FRAME, FRAME)])
+            h2 = tiles(r.hid[s, pl.ds(pl.multiple_of(last, 8), FRAME)])
+            e0 = keep_flag(f) * (h1 - h0)
+            e1 = keep_flag(f + 1) * (h2 - h1)
+            if s == 0:
+                taps = taps_of(0)
+                m0 = real(h0 + dw_tiles(e0 + before, taps, 1, 1))
+                m1 = real(h1 + dw_tiles(e1 + e0, taps, 1, 1))
+            else:
+                near, far = taps_of(1), taps_of(2)
+                mixed = []
+                for k, (hk, ek) in enumerate(((h0, e0), (h1, e1))):
+                    logits = dw_tiles(ek, near, 1, 1) + dw_tiles(ek, far, 2, 1) + r.gb[...]
+                    gate = 0.5 * (1.0 + jnp.tanh(0.5 * logits))
+                    r.sig[pl.ds(base + k * FRAME, FRAME)] = flat(gate)
+                    mixed.append(hk + hk * gate)
+                m0, m1 = mixed
+            both = jnp.concatenate([flat(m0), flat(m1)], axis=0).astype(bf16)
+            r.mixf[s, pl.ds(base, PAIR), cols(chan)] = both
+            return e1
+
+        lax.fori_loop(0, pairs, mix, jnp.zeros((SIDE, 8, ib), f32))
+
+    def conv_forward(s, h, sums):
+        r.y[...] = dot(r.mixf[s, part(h)], r.wc[s])
+
+        def add_taps(i, sums):
+            at = pl.ds(pl.multiple_of(i * FRAME, 8), FRAME)
+            total = None
+            for b in (-1, 0, 1):
+                run = None
+                for a in (-1, 0, 1):
+                    tap = 3 * (a + 1) + b + 1
+                    term = row_pad(tiles(r.y[at, tap * ib : (tap + 1) * ib]), 1)
+                    term = term[1 + a : 1 + a + SIDE]
+                    run = term if run is None else run + term
+                run = col_shift(run, b)
+                total = run if total is None else total + run
+            total = flat(real(total))
+            r.conv[s, pl.ds(pl.multiple_of(h * chunk + i * FRAME, 8), FRAME)] = total
+            return sums[0] + fold(total), sums[1] + fold(total * total)
+
+        return lax.fori_loop(0, frames // 2, add_taps, sums)
+
+    def forward(s, stat_base, wide_slot):
+        copies = []
+        for h in range(2):
+            temporal_forward(s, h)
+            copies.append(gather_start(r.mixf.at[s], h))
+        sums = (zero_n, zero_n)
+        for made in load_wc[s]:
+            made.wait()
+        gather_pass(r.mixf.at[s], 0, copies[0])
+        for h in range(2):
+            gather_end(copies[h])
+            sums = conv_forward(s, h, sums)
+            if h == 0:
+                gather_pass(r.mixf.at[s], 1, copies[1])
+        made = stat_start(r.stn, stat_base, sums)
+        yield
+        moments_in[s][1] = moments(stat_end(r.stn, stat_base, made))
+        copies = []
+        for h in range(2):
+
+            def inside(i, _):
+                at = pair_rows(h, i)
+                value = real(gelu(norm_inner(s, 1, r.conv[s, at])[1]))
+                r.inf[s, at, cols(chan)] = value.astype(bf16)
+                return _
+
+            lax.fori_loop(0, pairs, inside, 0)
+            copies.append(gather_start(r.inf.at[s], h))
+        yield
+        gather_pass(r.inf.at[s], 0, copies[0])
+        gather_pass(r.inf.at[s], 1, copies[1])
+        sums = (zero_w, zero_w)
+        for h in range(2):
+            gather_end(copies[h])
+            value = dot(r.inf[s, part(h)], r.wef[s])
+            r.ex[s, part(h)] = value
+            sums = (sums[0] + fold(value), sums[1] + fold(value * value))
+        made = stat_start(r.stw, wide_slot, sums)
+        yield
+        moments_in[s][2] = moments(stat_end(r.stw, wide_slot, made))
+
+    def spread_taps():
+        for index in range(3):
+            for tap in range(9):
+                r.dkb[9 * index + tap] = jnp.broadcast_to(r.dk[index, tap : tap + 1, :], (8, ib))
+
+    def clear(i, _):
+        r.gk[i] = zero_n
+        return _
+
+    weights_in = {}
+    weights_in["we0"] = share_we(0)
+    sums = (zero_n, zero_n)
+    load_wr0.wait()
+    for h in range(2):
+        load_x[h].wait()
+        value = dot(r.x[part(h)], r.wr0[...])
+        r.red[0, part(h)] = value
+        sums = (sums[0] + fold(value), sums[1] + fold(value * value))
+    made = stat_start(r.stn, 0, sums)
+    spread_taps()
+    lax.fori_loop(0, r.gk.shape[0], clear, 0)
+    moments_in[0][0] = moments(stat_end(r.stn, 0, made))
+
+    stage = forward(0, 1, 0)
+    next(stage)
+    weights_in["wr1"] = share_wr(1)
+    next(stage)
+    load_we[0].wait()
+    arrive(weights_in["we0"])
+    next(stage)
+    for _ in stage:
+        pass
+
+    def out_zero(i, _):
+        at = step_rows(i)
+        z = norm_outer(0, r.ex[0, at])[1] + inner_input(0, at).astype(f32)
+        r.out0[at] = real(gelu(z)).astype(bf16)
+        return _
+
+    lax.fori_loop(0, steps, out_zero, 0)
+
+    def scatter_all(slot, product, use, beside=None):
+        copies = []
+        for h in range(2):
+            r.pb[part(h)] = product(h).astype(bf16)
+            copies.append(scatter_start(slot, h))
+        scatter_pass(slot, 0, copies[0])
+        scatter_pass(slot, 1, copies[1])
+        if beside is not None:
+            beside()
+        for h in range(2):
+            scatter_end(slot, h, copies[h])
+            use(h)
+
+    held = {"sums": (zero_n, zero_n)}
+
+    def use_reduced(h):
+        value = scatter_value(0, part(h))
+        r.red[1, part(h)] = value
+        held["sums"] = (held["sums"][0] + fold(value), held["sums"][1] + fold(value * value))
+
+    load_wr[1].wait()
+    arrive(weights_in["wr1"])
+    scatter_all(0, lambda h: dot(r.out0[part(h)], r.wrf[1]), use_reduced)
+    made = stat_start(r.stn, 2, held["sums"])
+    weights_in["we1"] = share_we(1)
+    moments_in[1][0] = moments(stat_end(r.stn, 2, made))
+    stage = forward(1, 3, 1)
+    next(stage)
+    weights_in["wr0"] = share_wr(0)
+    next(stage)
+    load_we[1].wait()
+    arrive(weights_in["we1"])
+    next(stage)
+    for _ in stage:
+        pass
+
+    load_cot.wait()
+
+    def out_one(i, sums):
+        at = step_rows(i)
+        centred, z = norm_outer(1, r.ex[1, at])
+        value, slope = gelu_both(z + r.out0[at].astype(f32))
+        r.act[at] = value.astype(bf16)
+        grad = r.cot[at].astype(f32) * slope
+        r.gpre[at] = grad
+        return sums[0] + fold(grad), sums[1] + fold(grad * centred)
+
+    def top_zero(i, sums):
+        at = step_rows(i)
+        centred, z = norm_outer(0, r.ex[0, at])
+        grad = r.gin[at] * gelu_both(z + inner_input(0, at).astype(f32))[1]
+        r.gpre[at] = grad
+        return sums[0] + fold(grad), sums[1] + fold(grad * centred)
+
+    def backward(s, stat_base, wide_slot, slot):
+        made = stat_start(
+            r.stw, wide_slot, lax.fori_loop(0, steps, out_one if s else top_zero, (zero_w, zero_w))
+        )
+        if s == 1:
+            local_out.append(local(r.act, r.act_out))
+        shift_sum, gain_sum = stat_end(r.stw, wide_slot, made)
+        r.gbo[s : s + 1] = shift_sum
+        r.ggo[s : s + 1] = gain_sum
+        mean, inv = moments_in[s][2]
+        scale = inv * row(r.go, s)
+        shift_mean, gain_mean = shift_sum / pixel_total, gain_sum / pixel_total
+
+        def expand_back(i, _):
+            at = step_rows(i)
+            centred = (r.ex[s, at] - mean) * inv
+            grad = scale * (r.gpre[at] - (shift_mean + centred * gain_mean))
+            r.gexp[at] = real(grad).astype(bf16)
+            return _
+
+        lax.fori_loop(0, steps, expand_back, 0)
+        held["sums"] = (zero_n, zero_n)
+
+        def weight_expand():
+            r.geo[s] = dot(r.inf[s], r.gexp[...], 0, 0).astype(bf16)
+            weights_out.append(local(r.geo.at[s, cols(chan)], r.ge.at[s, :, wide(chan)]))
+            for j in others:
+                arrivals.append(
+                    remote(r.geo.at[s, cols(j)], r.ge.at[s, :, wide(chan)], (clip, j))
+                )
+
+        def use_inner(h):
+            def one(i, sums):
+                at = pair_rows(h, i)
+                centred, z = norm_inner(s, 1, r.conv[s, at])
+                grad = real(scatter_value(slot, at) * gelu_both(z)[1])
+                r.g1[at] = grad
+                return sums[0] + fold(grad), sums[1] + fold(grad * centred)
+
+            held["sums"] = lax.fori_loop(0, pairs, one, held["sums"])
+
+        scatter_all(
+            slot, lambda h: dot(r.gexp[part(h)], r.wef[s], 1, 1), use_inner, weight_expand
+        )
+        made = stat_start(r.stn, stat_base, held["sums"])
+        shift_sum, gain_sum = stat_end(r.stn, stat_base, made)
+        r.gbi[s, 1:2] = shift_sum
+        r.ggi[s, 1:2] = gain_sum
+        mean, inv = moments_in[s][1]
+        scale = inv * row(r.gi, s, 1)
+        shift_mean, gain_mean = shift_sum / pixel_total, gain_sum / pixel_total
+
+        def conv_back(i, _):
+            at = pair_rows(0, i)
+            centred = (r.conv[s, at] - mean) * inv
+            grad = real(scale * (r.g1[at] - (shift_mean + centred * gain_mean)))
+            halves = [tiles(grad[:FRAME]), tiles(grad[FRAME:])]
+            for b in (-1, 0, 1):
+                moved = [row_pad(col_shift(v, -b), 1) for v in halves]
+                for a in (-1, 0, 1):
+                    tap = 3 * (a + 1) + b + 1
+                    both = jnp.concatenate([flat(v[1 - a : 1 - a + SIDE]) for v in moved], axis=0)
+                    r.gs[at, tap * ib : (tap + 1) * ib] = both.astype(bf16)
+            return _
+
+        lax.fori_loop(0, 2 * pairs, conv_back, 0)
+
+        def weight_conv():
+            for piece in range(n_chan):
+                at = pl.ds(piece * ib, ib)
+                value = dot(r.mixf[s, :, piece * ib : (piece + 1) * ib], r.gs[...], 0, 0)
+                r.gc[s, at] = value.astype(bf16)
+
+        def use_mixed(h):
+            def one(i, _):
+                at = pair_rows(h, i)
+                r.gm[at] = real(scatter_value(slot + 1, at))
+                return _
+
+            lax.fori_loop(0, pairs, one, 0)
+
+        scatter_all(
+            slot + 1, lambda h: dot(r.gs[part(h)], r.wc[s], 1, 1), use_mixed, weight_conv
+        )
+
+        def tap_sums(grad, v, index, reach):
+            for b in (-1, 0, 1):
+                padded = row_pad(col_shift(v, reach * b), reach)
+                for a in (-1, 0, 1):
+                    start = reach + reach * a
+                    place = 9 * index + 3 * (a + 1) + b + 1
+                    r.gk[place] = r.gk[place] + jnp.sum(grad * padded[start : start + SIDE], axis=0)
+
+        def mix_back(f, before):
+            at = frame_rows(f)
+            following = frame_rows(jnp.minimum(f + 1, frames - 1))
+            here = tiles(r.hid[s, at])
+            step = keep_flag(f) * (tiles(r.hid[s, following]) - here)
+            grad = tiles(r.gm[at])
+            if s == 0:
+                r.gd[at] = flat(dw_tiles(grad, taps_of(0), 1, -1))
+                tap_sums(grad, step + before, 0, 1)
+            else:
+                gate = tiles(r.sig[at])
+                grad = grad * here * gate * (1.0 - gate)
+                r.gd[at] = flat(dw_tiles(grad, taps_of(1), 1, -1) + dw_tiles(grad, taps_of(2), 2, -1))
+                tap_sums(grad, step, 1, 1)
+                tap_sums(grad, step, 2, 2)
+                r.gk[27] = r.gk[27] + jnp.sum(grad, axis=0)
+            return step
+
+        lax.fori_loop(0, frames, mix_back, jnp.zeros((SIDE, 8, ib), f32))
+
+        def hide_back(f, sums):
+            at = frame_rows(f)
+            previous = frame_rows(jnp.maximum(f - 1, 0))
+            keep = keep_flag(f)
+            keep_before = jnp.where(f > 0, keep_flag(jnp.maximum(f - 1, 0)), 0.0)
+            now = r.gd[at]
+            earlier = r.gd[previous]
+            grad = r.gm[at]
+            if s == 0:
+                following = frame_rows(jnp.minimum(f + 1, frames - 1))
+                later = now + r.gd[following]
+                earlier = earlier + now
+            else:
+                later = now
+                grad = grad * (1.0 + r.sig[at])
+            grad = grad + keep_before * earlier - keep * later
+            centred, z = norm_inner(s, 0, r.red[s, at])
+            grad = real(grad * gelu_both(z)[1])
+            r.g1[at] = grad
+            return sums[0] + fold(grad), sums[1] + fold(grad * centred)
+
+        sums = lax.fori_loop(0, frames, hide_back, (zero_n, zero_n))
+        made = stat_start(r.stn, stat_base + 1, sums)
+        shift_sum, gain_sum = stat_end(r.stn, stat_base + 1, made)
+        r.gbi[s, 0:1] = shift_sum
+        r.ggi[s, 0:1] = gain_sum
+        mean, inv = moments_in[s][0]
+        scale = inv * row(r.gi, s, 0)
+        shift_mean, gain_mean = shift_sum / pixel_total, gain_sum / pixel_total
+        copies = []
+        for h in range(2):
+
+            def reduce_back(i, _):
+                at = pair_rows(h, i)
+                centred = (r.red[s, at] - mean) * inv
+                grad = real(scale * (r.g1[at] - (shift_mean + centred * gain_mean)))
+                r.grf[s, at, cols(chan)] = grad.astype(bf16)
+                return _
+
+            lax.fori_loop(0, pairs, reduce_back, 0)
+            copies.append(gather_start(r.grf.at[s], h))
+        if s == 0:
+            own = r.grf[0, :, cols(chan)]
+            for piece in range(n_chan):
+                at = slice(piece * cs, (piece + 1) * cs)
+                r.gr[0, at] = dot(r.x[:, at], own, 0, 0).astype(bf16)
+        gather_pass(r.grf.at[s], 0, copies[0])
+        gather_pass(r.grf.at[s], 1, copies[1])
+        if s == 0:
+            load_wr[0].wait()
+            arrive(weights_in["wr0"])
+        for h in range(2):
+            gather_end(copies[h])
+            r.gin[part(h)] = dot(r.grf[s, part(h)], r.wrf[s], 1, 1) + r.gpre[part(h)]
+            if s == 0:
+                local_out.append(local(r.gin.at[part(h)], r.gin_out.at[part(h)]))
+        if s == 1:
+            r.gro[...] = dot(r.out0[...], r.grf[1], 0, 0).astype(bf16)
+            weights_out.append(local(r.gro.at[:, cols(chan)], r.gr.at[1, wide(chan)]))
+            for j in others:
+                arrivals.append(remote(r.gro.at[:, cols(j)], r.gr.at[1, wide(chan)], (clip, j)))
+
+    local_out, weights_out, arrivals = [], [], []
+    backward(1, 4, 2, 1)
+    backward(0, 6, 3, 3)
+
+    for place in range(r.gk.shape[0]):
+        r.kst[clip, place : place + 1, :] = jnp.sum(r.gk[place], axis=0, keepdims=True)
+    made = [remote(r.kst.at[clip], r.kst.at[clip], (t, chan)) for t in clip_others]
+    arrive(arrivals)
+    for copy in weights_out:
+        copy.wait()
+    for s in range(2):
+        local_out.append(local(r.gc.at[s], r.gc_out.at[s]))
+        local_out.append(local(r.ge.at[s], r.ge_out.at[s]))
+        local_out.append(local(r.gr.at[s], r.gr_out.at[s]))
+    arrive(made)
+    total = r.kst[0]
+    for k in range(1, n_clip):
+        total = total + r.kst[k]
+    for index in range(3):
+        r.gk_out[index] = total[9 * index : 9 * index + 9]
+    r.ggb_out[...] = total[27:28]
+    for copy in local_out:
+        copy.wait()
+    for copy in list(unsent):
+        sent(copy)
+
+
+def fused_call(n_clip, n_chan, pixel_total, *operands):
+    rows, width = operands[0].shape
+    cs = width // n_chan
+    ib = LANES
+    inner = ib * n_chan
+    bf16, f32 = jnp.bfloat16, jnp.float32
+    whole = pl.BlockSpec(memory_space=pltpu.VMEM)
+    anywhere = pl.BlockSpec(memory_space=pl.ANY)
+    scalars = pl.BlockSpec(memory_space=pltpu.SMEM)
+    shape = jax.ShapeDtypeStruct
+    V = pltpu.VMEM
+    scratch = dict(
+        x=V((rows, width), bf16),
+        cot=V((rows, cs), bf16),
+        wr0=V((width, ib), bf16),
+        wrf=V((2, cs, inner), bf16),
+        wef=V((2, inner, cs), bf16),
+        wc=V((2, inner, 9 * ib), bf16),
+        dkb=V((27, 8, ib), f32),
+        red=V((2, rows, ib), f32),
+        hid=V((2, rows, ib), f32),
+        sig=V((rows, ib), f32),
+        conv=V((2, rows, ib), f32),
+        mixf=V((2, rows, inner), bf16),
+        inf=V((2, rows, inner), bf16),
+        ex=V((2, rows, cs), f32),
+        out0=V((rows, cs), bf16),
+        act=V((rows, cs), bf16),
+        y=V((rows // 2, 9 * ib), f32),
+        gpre=V((rows, cs), f32),
+        gin=V((rows, cs), f32),
+        gexp=V((rows, cs), bf16),
+        gs=V((rows, 9 * ib), bf16),
+        pb=V((rows, inner), bf16),
+        ysend=V((2, rows, ib), bf16),
+        rcore=V((5, 2, rows, ib), bf16),
+        ryy=V((5, rows, ib), bf16),
+        grf=V((2, rows, inner), bf16),
+        gm=V((rows, ib), f32),
+        gd=V((rows, ib), f32),
+        g1=V((rows, ib), f32),
+        gk=V((32, 8, ib), f32),
+        kst=V((n_clip, 32, ib), f32),
+        stn=V((8, n_clip, 2, ib), f32),
+        stw=V((4, n_clip, 2, cs), f32),
+        gc=V((2, inner, 9 * ib), bf16),
+        geo=V((2, inner, cs), bf16),
+        ge=V((2, ib, width), bf16),
+        gro=V((cs, inner), bf16),
+        gr=V((2, width, ib), bf16),
+        ssem=pltpu.SemaphoreType.DMA((COPIES,)),
+        rsem=pltpu.SemaphoreType.DMA((COPIES,)),
+        lsem=pltpu.SemaphoreType.DMA((LOADS,)),
+    )
+    first = NAMES.index("x")
+    return pl.pallas_call(
+        partial(fused_kernel, n_clip, n_chan, pixel_total),
+        out_shape=[
+            shape((rows, cs), bf16),
+            shape((rows, cs), f32),
+            shape((2, 2, ib), f32),
+            shape((2, 2, ib), f32),
+            shape((2, cs), f32),
+            shape((2, cs), f32),
+            shape((3, 9, ib), f32),
+            shape((1, ib), f32),
+            shape((2, inner, 9 * ib), bf16),
+            shape((2, ib, width), bf16),
+            shape((2, width, ib), bf16),
+        ],
+        in_specs=[anywhere] * 5 + [scalars] + [whole] * 6,
+        out_specs=[anywhere] * 2 + [whole] * 6 + [anywhere] * 3,
+        scratch_shapes=[scratch[name] for name in NAMES[first:]],
+        compiler_params=pltpu.CompilerParams(
+            collective_id=0, has_side_effects=True, vmem_limit_bytes=62 * 1024 * 1024
+        ),
+    )(*operands)
+
+
+def padded_rows(values):
+    frame_rows = values.reshape(-1, SIDE, values.shape[-1])
+    return jnp.pad(frame_rows, ((0, 0), (0, 1), (0, 0))).reshape(-1, values.shape[-1])
+
+
+def real_rows(values):
+    return values.reshape(-1, 8, values.shape[-1])[:, :SIDE].reshape(-1, values.shape[-1])
+
+
+def fused(
+    frames_in,
+    boundary,
+    w_reduce,
+    gain_inner,
+    bias_inner,
+    w_conv,
+    w_expand,
+    gain_outer,
+    bias_outer,
+    depth_kernels,
+    gate_bias,
+    cotangent,
+):
+    n_clip, n_chan = lax.axis_size("clip"), lax.axis_size("chan")
+    col_share = frames_in.shape[1] // n_chan
+    pixel_total = frames_in.shape[0] * n_clip
+    col_start = lax.axis_index("chan") * col_share
+    act, gin, ggi, gbi, ggo, gbo, gk, ggb, gc, ge, gr = fused_call(
+        n_clip,
+        n_chan,
+        float(pixel_total),
+        padded_rows(frames_in),
+        padded_rows(columns(cotangent, col_start, col_share)),
+        w_reduce,
+        w_conv,
+        w_expand,
+        boundary,
+        gain_inner,
+        bias_inner,
+        gain_outer,
+        bias_outer,
+        depth_kernels,
+        gate_bias.reshape(1, -1),
+    )
+    gr, gc, ge = lax.psum((gr, gc, ge), "clip")
+    gc = gc.reshape(2, gc.shape[1], 9, -1).transpose(0, 2, 1, 3)
+    return (
+        real_rows(act),
+        real_rows(gin),
+        gr.astype(jnp.float32),
+        ggi,
+        gbi,
+        gc.astype(jnp.float32),
+        ge.astype(jnp.float32),
+        ggo,
+        gbo,
+        gk,
+        ggb.reshape(-1),
+    )
+
+
 def solution(mesh):
     in_specs = (
         P("clip", None),
@@ -321,4 +1140,9 @@
         P(None, None, "chan"),
         P("chan"),
     )
-    return jax.shard_map(body, mesh=mesh, in_specs=in_specs, out_specs=out_specs, check_vma=False)
+
+    def run(*arguments):
+        fits = fused_fits(mesh, arguments[0].shape, arguments[2].shape)
+        return jax.shard_map(fused if fits else body, mesh=mesh, in_specs=in_specs, out_specs=out_specs, check_vma=False)(*arguments)
+
+    return run

time: 1090 us -> 382 us (0.35); the launches traced: 1080 us -> 381 us
  blocking collectives: 348 us -> 0 us
  waiting for transfers between devices: 394 us -> 160 us
  Pallas kernels: 0 us -> 175 us
  local copies, waits for them, and re-layouts: 140 us -> 28.1 us
  other arithmetic: 113 us -> 4.39 us
  matrix products: 65.1 us -> 0 us
    psum x13 -> x0, blocking collectives: 330 us -> none  [the longest x6 151 us: normalize(): lax.psum((jnp.sum(values, axis=0), jnp.sum(values * values, axis=0)), 'cl...]
    psum x5 -> x1, waiting for transfers between devices: 372 us -> 160 us  [fused(): gr, gc, ge = lax.psum((gr, gc, ge), 'clip')]
    pallas_call x0 -> x1, Pallas kernels: none -> 175 us  [fused_call(): pl.pallas_call(partial(fused_kernel, n_clip, n_chan, pixel_total), out_sh...]
    dot_general x18 -> x0, matrix products: 65.1 us -> none  [the longest x12 48.9 us: contract(): lax.dot_general(left, right, (((left_dim,), (right_dim,)), ((), ())), pre...]
    reduce_sum x9 -> x0, other arithmetic: 42.7 us -> none  [the longest x4 26.3 us: normalize_back(): jnp.sum(grad_rows, axis=0)]
    concatenate x21 -> x0, local copies, waits for them, and re-layouts: 31.6 us -> none  [the longest x18 29.7 us: patch_rows(): jnp.concatenate(pieces, axis=-1)]
    convert_element_type x14 -> x2, other arithmetic: 33.9 us -> 4.39 us  [the longest x1 2.83 us: fused(): gr.astype(jnp.float32)]
    dot_general x4 -> x0, local copies, waits for them, and re-layouts: 23.2 us -> none  [contract(): lax.dot_general(left, right, (((left_dim,), (right_dim,)), ((), ())), pre...]
  transfers between devices with their start and end apart: 7 -> 1, of which waited for: 6 -> 1; matrix products, arithmetic and copies ran while one was open for 5% -> 1% of each run, Pallas kernels for 0% -> 0%
where the time goes in v1:
time: 382 us; the launch traced here: 381 us
  Pallas kernels  175 us (46%)
  waiting for transfers between devices  160 us (42%)
  local copies, waits for them, and re-layouts  28.1 us (7%)
  between operations  14.1 us (4%)
  other arithmetic  4.39 us (1%)
    pallas_call x1, Pallas kernels, fused_call(): pl.pallas_call(partial(fused_kernel, n_clip, n_chan, pixel_total), out_sh...  175 us
    psum x1, waiting for transfers between devices, fused(): gr, gc, ge = lax.psum((gr, gc, ge), 'clip')  160 us
    unnamed x30, local copies, waits for them, and re-layouts  8.22 us
  transfers between devices with their start and end apart: 1, of which 1 were waited for; matrix products, arithmetic and copies ran while one was open for 1% of the time, Pallas kernels for 0%

profile of v1, /device:TPU:0, one launch (start us, length us, event | category | flops | bytes accessed | tf_op | source)
XLA Modules:
  0.0 381.2 jit_solution(8152712846191183308)
XLA Ops:
  7.2 0.0 all-reduce.5.cloned.1.call-start
  7.2 5.6 %reshape.55 = bf16[112,7,2048]{2,1,0:T(8,128)(2,1)} reshape(bf16[784,2048]{1,0:T(8,128)(2,1)} %param.12) | data formatting | bytes 6422528 | tf_op jit(solution)/shard_map/reshape | solution.py:1055
  12.8 4.9 %pad_bitcast_fusion.refs_0_ = bf16[896,2048]{1,0:T(8,128)(2,1)} fusion(bf16[112,7,2048]{2,1,0:T(8,128)(2,1)} %reshape.55), kind=kLoop, calls=%fused_computation | loop fusion | bytes 6881280 | tf_op jit(solution)/shard_map/reshape | solution.py:1056
  17.7 1.2 constant_dynamic-slice_fusion
  18.9 0.3 reshape.57
  19.2 1.1 pad_bitcast_fusion.1.refs_1_
  20.3 0.6 copy.26.refs_10_
  20.9 175.0 %shard_map.203 = (bf16[896,512]{1,0:T(8,128)(2,1)}, f32[896,512]{1,0:T(8,128)}, f32[2,2,128]{2,1,0:T(2,128)}, f32[2,2,128]{2,1,0:T(2,128)}, f32[2,512]{1,0:T(2,1...) custom-call(bf16[896,2048]{1,0:T(8,128)(2,1)} %pad_bitcast_fusion.re, ...), custom_call_target="tpu_custom_call" | custom-call | tf_op jit(solution)/shard_map/pallas_call | solution.py:1030
  196.0 4.3 %copy.27 = bf16[2,512,1152]{1,2,0:T(8,128)(2,1)} copy(bf16[2,512,1152]{2,1,0:T(8,128)(2,1)} %get-tuple-element.27) | data formatting | bytes 4718592 | tf_op jit(solution)/shard_map/pallas_call | solution.py:1030
  200.2 0.0 all-reduce.5.cloned.1.call-update
  200.3 0.0 copy-start.4
  200.3 1.1 copy-done.3
  201.4 1.2 reshape.61
  202.6 1.4 reshape.63
  203.9 0.6 copy.29
  204.6 159.5 %all-reduce.5.cloned.1.call-done = (bf16[2,9,512,128]{2,3,1,0:T(8,128)(2,1)}, bf16[2,2048,128]{2,1,0:T(8,128)(2,1)}, bf16[2,128,2048]{2,1,0:T(8,128)(2,1)}) async-done(((bf16[2,9,512,128]{2,3,1,0:T(8,128)(2,1)}, bf16[2,2048,128]{2,1,0:T(8,128)(2,1)}, bf16[2,128,2048]{2,1,0:T(8,128)(2,1)}), (bf16[2,9,512,128]{2,3,1,0:T(8,128)(2,1)}, bf16[2,2048,128]{2,1,0:T(8,128)(2,1)}, ...) | async-done | bytes 4456464 | tf_op jit(solution)/shard_map/psum | solution.py:1098
  364.1 2.8 convert_element_type.19
  367.0 3.0 copy.28
  369.9 1.6 convert_element_type.23
  371.5 0.6 copy.38
  372.1 0.6 copy.39
  372.6 0.6 copy.40
  373.2 0.6 copy.41
  373.8 0.5 copy.42
  (20 shorter events, 0.0 us)
Async XLA Ops:
  7.2 356.9 %all-reduce.5.cloned.1.call-start = ((), (), s32[]{:S(2)}) async-start(), calls=%async_computation | async-start | bytes 8912896 | tf_op jit(solution)/shard_map/psum | solution.py:1098
  17.7 2.6 copy-start.5
  200.2 1.2 copy-start.3
  200.2 2.3 copy-start.1
  200.3 3.7 copy-start.4
  364.1 2.8 copy-start
  366.9 3.0 copy-start.2
  366.9 4.6 %copy-start.9 = (f32[2,2,128]{2,1,0:T(2,128)S(1)}, f32[2,2,128]{2,1,0:T(2,128)}, u32[]{:S(2)}) copy-start(f32[2,2,128]{2,1,0:T(2,128)} %get-tuple-element.72) | copy-start | bytes 6148
  366.9 5.1 %copy-start.8 = (f32[2,2,128]{2,1,0:T(2,128)S(1)}, f32[2,2,128]{2,1,0:T(2,128)}, u32[]{:S(2)}) copy-start(f32[2,2,128]{2,1,0:T(2,128)} %get-tuple-element.73) | copy-start | bytes 6148
  366.9 5.7 %copy-start.7 = (f32[2,512]{1,0:T(2,128)S(1)}, f32[2,512]{1,0:T(2,128)}, u32[]{:S(2)}) copy-start(f32[2,512]{1,0:T(2,128)} %get-tuple-element.76) | copy-start | bytes 12292
  366.9 6.3 %copy-start.6 = (f32[2,512]{1,0:T(2,128)S(1)}, f32[2,512]{1,0:T(2,128)}, u32[]{:S(2)}) copy-start(f32[2,512]{1,0:T(2,128)} %get-tuple-element.77) | copy-start | bytes 12292
  366.9 6.9 %copy-start.10 = (f32[1,128]{1,0:T(1,128)S(1)}, f32[1,128]{1,0:T(1,128)}, u32[]{:S(2)}) copy-start(f32[1,128]{1,0:T(1,128)} %get-tuple-element.32) | copy-start | bytes 1540
Sparse Core Ops, SparseCore 0:
  200.4 163.6 all-reduce.4

commit v2 on v1

--- a/solution.py
+++ b/solution.py
@@ -299,18 +299,20 @@
 MESH = pl.DeviceIdType.MESH
 LANES = 128
 FRAME = SIDE * 8
+PIXELS = SIDE * SIDE
+SPLIT = 5
 PAIR = 2 * FRAME
 GELU_A = 0.7978845608028654
 GELU_B = 0.044715
-COPIES = 224
-LOADS = 40
+COPIES = 288
+LOADS = 80
 
 
 def fused_fits(mesh, frame_shape, reduce_shape):
     n_clip, n_chan = mesh.shape["clip"], mesh.shape["chan"]
     share = reduce_shape[2] // n_chan
     frames = frame_shape[0] // (n_clip * SIDE * SIDE)
-    return n_chan == 4 and share == LANES and frames == 2 * SEG
+    return n_chan == 4 and n_clip == 8 and share == LANES and frames == 2 * SEG
 
 
 def gelu(z):
@@ -384,18 +386,49 @@
     "dk", "gb", "act_out", "gin_out", "ggi", "gbi", "ggo", "gbo", "gk_out", "ggb_out", "gc_out",
     "ge_out", "gr_out", "x", "cot", "wr0", "wrf", "wef", "wc", "dkb", "red", "hid", "sig",
     "conv", "mixf", "inf", "ex", "out0", "act", "y", "gpre", "gin", "gexp", "gs", "pb", "ysend",
-    "rcore", "ryy", "grf", "gm", "gd", "g1", "gk", "kst", "stn", "stw", "gc", "geo", "ge",
-    "gro", "gr", "ssem", "rsem", "lsem",
+    "rcore", "ryy", "grf", "gm", "gd", "g1", "gk", "kst", "stn", "stw", "gca", "gcb", "geo",
+    "ge", "gro", "gr", "rxa", "rxb", "fa", "fb", "fe", "fr", "rxe", "rxr", "rza", "rzb", "rze", "rzr", "ssem", "rsem",
+    "lsem",
 )
+
+
+PLAN = {
+    (1, 3): (("ge", 1),),
+    (1, 4): (("ge", 1), ("gca", 1), ("gcb", 1)),
+    (1, 5): (("ge", 1),),
+    (1, 6): (("ge", 1), ("gca", 1)),
+    (0, 1): (("gca", 1), ("gcb", 1), ("ge", 1)),
+    (0, 2): (("gr", 1), ("gcb", 1), ("gca", 1)),
+    (0, 3): (("gr", 1), ("gcb", 1), ("gca", 1), ("ge", 0)),
+    (0, 4): (("gca", 0), ("gcb", 0), ("gr", 1), ("gcb", 1), ("ge", 0)),
+    (0, 5): (("gr", 1), ("ge", 0)),
+    (0, 6): (("gr", 0), ("gca", 0), ("gr", 1), ("ge", 0)),
+    (0, 7): (
+        ("gca", 0),
+        ("gcb", 0),
+        ("ge", 0),
+        ("gr", 0),
+        ("gcb", 0),
+        ("gca", 0),
+        ("gr", 0),
+        ("gcb", 0),
+        ("gr", 0),
+        ("gca", 0),
+        ("gcb", 0),
+        ("gr", 0),
+    ),
+}
 
 
 def fused_kernel(n_clip, n_chan, pixel_total, *refs):
     r = SimpleNamespace(**dict(zip(NAMES, refs)))
     rows, cs = r.cot.shape
     ib = LANES
-    inner = ib * n_chan
-    chunk = rows // 2
-    frames = rows // FRAME
+    frames = rows // PIXELS
+    chunk = frames // 2 * FRAME
+    n_z = n_clip // 2
+    first = -(-rows // 32) * 16
+    starts, counts = (0, first), (first, rows - first)
     bf16, f32 = jnp.bfloat16, jnp.float32
     clip = lax.axis_index("clip")
     chan = lax.axis_index("chan")
@@ -404,6 +437,8 @@
     j_y = core + 2 * (1 - high)
     j_far = (1 - core) + 2 * (1 - high)
     others = (j_core, j_y, j_far)
+    z, side = lax.div(clip, 2), lax.rem(clip, 2)
+    z_others = [lax.rem(z + d, n_z) for d in range(1, n_z)]
     clip_others = [lax.rem(clip + d, n_clip) for d in range(1, n_clip)]
 
     def cols(j):
@@ -414,6 +449,9 @@
 
     def part(h):
         return pl.ds(h * chunk, chunk)
+
+    def raw(h):
+        return pl.ds(starts[h], counts[h])
 
     counters = {"copy": 0, "load": 0}
     unsent = []
@@ -445,7 +483,7 @@
         return made
 
     load_wr0 = local(r.wred_hbm.at[0], r.wr0)
-    load_x = [local(r.x_hbm.at[part(h)], r.x.at[part(h)]) for h in range(2)]
+    load_x = [local(r.x_hbm.at[raw(h)], r.x.at[raw(h)]) for h in range(2)]
     load_we = [
         local(r.wexp_hbm.at[s, :, wide(chan)], r.wef.at[s, cols(chan)]) for s in range(2)
     ]
@@ -459,7 +497,7 @@
         ]
         for s in range(2)
     ]
-    load_cot = local(r.cot_hbm, r.cot)
+    load_cot = local(r.cot_hbm.at[:, wide(chan)], r.cot)
 
     barrier = pltpu.get_barrier_semaphore()
     for target in clip_others:
@@ -500,34 +538,32 @@
         mean = pair[0] / pixel_total
         return mean, lax.rsqrt(pair[1] / pixel_total - mean * mean + epsilon)
 
-    def gather_start(full, h):
-        mine = full.at[part(h), cols(chan)]
+    def gather_start(full, at):
+        mine = full.at[at, cols(chan)]
         return [remote(mine, mine, (clip, j_y)), remote(mine, mine, (clip, j_core))]
 
-    def gather_pass(full, h, copies):
+    def gather_pass(full, at, copies):
         copies[0].wait_recv()
-        theirs = full.at[part(h), cols(j_y)]
+        theirs = full.at[at, cols(j_y)]
         copies.append(remote(theirs, theirs, (clip, j_core)))
 
     def gather_end(copies):
         copies[1].wait_recv()
         copies[2].wait_recv()
 
-    def scatter_start(slot, h):
+    def scatter_start(slot, at):
         return [
-            remote(r.pb.at[part(h), cols(j_far)], r.rcore.at[slot, 1, part(h)], (clip, j_core)),
-            remote(r.pb.at[part(h), cols(j_core)], r.rcore.at[slot, 0, part(h)], (clip, j_core)),
+            remote(r.pb.at[at, cols(j_far)], r.rcore.at[slot, 1, at], (clip, j_core)),
+            remote(r.pb.at[at, cols(j_core)], r.rcore.at[slot, 0, at], (clip, j_core)),
         ]
 
-    def scatter_pass(slot, h, copies):
+    def scatter_pass(slot, at, copies):
         copies[0].wait_recv()
-        both = r.pb[part(h), cols(j_y)].astype(f32) + r.rcore[slot, 1, part(h)].astype(f32)
-        r.ysend[slot % 2, part(h)] = both.astype(bf16)
-        copies.append(
-            remote(r.ysend.at[slot % 2, part(h)], r.ryy.at[slot, part(h)], (clip, j_y))
-        )
-
-    def scatter_end(slot, h, copies):
+        both = r.pb[at, cols(j_y)].astype(f32) + r.rcore[slot, 1, at].astype(f32)
+        r.ysend[slot % 2, at] = both.astype(bf16)
+        copies.append(remote(r.ysend.at[slot % 2, at], r.ryy.at[slot, at], (clip, j_y)))
+
+    def scatter_end(copies):
         copies[1].wait_recv()
         copies[2].wait_recv()
         sent(copies[0])
@@ -550,14 +586,31 @@
     def frame_rows(f):
         return pl.ds(pl.multiple_of(f * FRAME, 8), FRAME)
 
+    def spread(ref, f):
+        return jnp.stack(
+            [ref[pl.ds(f * PIXELS + SIDE * k, 8), :] for k in range(SIDE)], axis=0
+        )
+
+    def squeeze(ref, f, value):
+        for k in range(SIDE):
+            ref[pl.ds(f * PIXELS + SIDE * k, 8), :] = value[k]
+
     pairs = frames // 4
     zero_n = jnp.zeros((8, ib), f32)
     zero_w = jnp.zeros((8, cs), f32)
-    STEP = 32
-    steps = rows // STEP
-
-    def step_rows(i):
-        return pl.ds(pl.multiple_of(i * STEP, STEP), STEP)
+
+    def each(start, count, step, one, begin):
+        def at_step(i, carry):
+            return one(pl.ds(pl.multiple_of(start + i * step, 16), step), carry)
+
+        return lax.fori_loop(0, count // step, at_step, begin)
+
+    def narrow(h, one, begin):
+        step = next(n for n in (112, 96, 80, 64, 48, 32, 16) if counts[h] % n == 0)
+        return each(starts[h], counts[h], step, one, begin)
+
+    def broad(one, begin):
+        return each(0, rows, 16, one, begin)
 
     moments_in = [[None, None, None], [None, None, None]]
 
@@ -579,11 +632,12 @@
 
     def temporal_forward(s, h):
         def hide(i, _):
-            at = pair_rows(h, i)
-            r.hid[s, at] = real(gelu(norm_inner(s, 0, r.red[s, at])[1]))
+            f = h * (frames // 2) + i
+            value = real(gelu(norm_inner(s, 0, spread(r.red.at[s], f))[1]))
+            r.hid[s, frame_rows(f)] = flat(value)
             return _
 
-        lax.fori_loop(0, pairs, hide, 0)
+        lax.fori_loop(0, frames // 2, hide, 0)
 
         def mix(i, before):
             base = pl.multiple_of(h * chunk + i * PAIR, 16)
@@ -628,9 +682,9 @@
                     run = term if run is None else run + term
                 run = col_shift(run, b)
                 total = run if total is None else total + run
-            total = flat(real(total))
-            r.conv[s, pl.ds(pl.multiple_of(h * chunk + i * FRAME, 8), FRAME)] = total
-            return sums[0] + fold(total), sums[1] + fold(total * total)
+            total = real(total)
+            squeeze(r.conv.at[s], h * (frames // 2) + i, total)
+            return sums[0] + jnp.sum(total, axis=0), sums[1] + jnp.sum(total * total, axis=0)
 
         return lax.fori_loop(0, frames // 2, add_taps, sums)
 
@@ -638,38 +692,37 @@
         copies = []
         for h in range(2):
             temporal_forward(s, h)
-            copies.append(gather_start(r.mixf.at[s], h))
+            copies.append(gather_start(r.mixf.at[s], part(h)))
         sums = (zero_n, zero_n)
         for made in load_wc[s]:
             made.wait()
-        gather_pass(r.mixf.at[s], 0, copies[0])
+        gather_pass(r.mixf.at[s], part(0), copies[0])
         for h in range(2):
             gather_end(copies[h])
             sums = conv_forward(s, h, sums)
             if h == 0:
-                gather_pass(r.mixf.at[s], 1, copies[1])
+                gather_pass(r.mixf.at[s], part(1), copies[1])
         made = stat_start(r.stn, stat_base, sums)
         yield
         moments_in[s][1] = moments(stat_end(r.stn, stat_base, made))
         copies = []
         for h in range(2):
 
-            def inside(i, _):
-                at = pair_rows(h, i)
-                value = real(gelu(norm_inner(s, 1, r.conv[s, at])[1]))
+            def inside(at, _):
+                value = gelu(norm_inner(s, 1, r.conv[s, at])[1])
                 r.inf[s, at, cols(chan)] = value.astype(bf16)
                 return _
 
-            lax.fori_loop(0, pairs, inside, 0)
-            copies.append(gather_start(r.inf.at[s], h))
+            narrow(h, inside, 0)
+            copies.append(gather_start(r.inf.at[s], raw(h)))
         yield
-        gather_pass(r.inf.at[s], 0, copies[0])
-        gather_pass(r.inf.at[s], 1, copies[1])
+        gather_pass(r.inf.at[s], raw(0), copies[0])
+        gather_pass(r.inf.at[s], raw(1), copies[1])
         sums = (zero_w, zero_w)
         for h in range(2):
             gather_end(copies[h])
-            value = dot(r.inf[s, part(h)], r.wef[s])
-            r.ex[s, part(h)] = value
+            value = dot(r.inf[s, raw(h)], r.wef[s])
+            r.ex[s, raw(h)] = value
             sums = (sums[0] + fold(value), sums[1] + fold(value * value))
         made = stat_start(r.stw, wide_slot, sums)
         yield
@@ -683,6 +736,9 @@
     def clear(i, _):
         r.gk[i] = zero_n
         return _
+
+    for s in range(2):
+        r.red[s, rows : rows + 8] = zero_n
 
     weights_in = {}
     weights_in["we0"] = share_we(0)
@@ -690,8 +746,8 @@
     load_wr0.wait()
     for h in range(2):
         load_x[h].wait()
-        value = dot(r.x[part(h)], r.wr0[...])
-        r.red[0, part(h)] = value
+        value = dot(r.x[raw(h)], r.wr0[...])
+        r.red[0, raw(h)] = value
         sums = (sums[0] + fold(value), sums[1] + fold(value * value))
     made = stat_start(r.stn, 0, sums)
     spread_taps()
@@ -708,37 +764,36 @@
     for _ in stage:
         pass
 
-    def out_zero(i, _):
-        at = step_rows(i)
+    def out_zero(at, _):
         z = norm_outer(0, r.ex[0, at])[1] + inner_input(0, at).astype(f32)
-        r.out0[at] = real(gelu(z)).astype(bf16)
+        r.out0[at] = gelu(z).astype(bf16)
         return _
 
-    lax.fori_loop(0, steps, out_zero, 0)
-
-    def scatter_all(slot, product, use, beside=None):
+    broad(out_zero, 0)
+
+    def scatter_all(slot, chunk_rows, product, use, beside=None):
         copies = []
         for h in range(2):
-            r.pb[part(h)] = product(h).astype(bf16)
-            copies.append(scatter_start(slot, h))
-        scatter_pass(slot, 0, copies[0])
-        scatter_pass(slot, 1, copies[1])
+            r.pb[chunk_rows(h)] = product(h).astype(bf16)
+            copies.append(scatter_start(slot, chunk_rows(h)))
+        scatter_pass(slot, chunk_rows(0), copies[0])
+        scatter_pass(slot, chunk_rows(1), copies[1])
         if beside is not None:
             beside()
         for h in range(2):
-            scatter_end(slot, h, copies[h])
+            scatter_end(copies[h])
             use(h)
 
     held = {"sums": (zero_n, zero_n)}
 
     def use_reduced(h):
-        value = scatter_value(0, part(h))
-        r.red[1, part(h)] = value
+        value = scatter_value(0, raw(h))
+        r.red[1, raw(h)] = value
         held["sums"] = (held["sums"][0] + fold(value), held["sums"][1] + fold(value * value))
 
     load_wr[1].wait()
     arrive(weights_in["wr1"])
-    scatter_all(0, lambda h: dot(r.out0[part(h)], r.wrf[1]), use_reduced)
+    scatter_all(0, raw, lambda h: dot(r.out0[raw(h)], r.wrf[1]), use_reduced)
     made = stat_start(r.stn, 2, held["sums"])
     weights_in["we1"] = share_we(1)
     moments_in[1][0] = moments(stat_end(r.stn, 2, made))
@@ -754,8 +809,7 @@
 
     load_cot.wait()
 
-    def out_one(i, sums):
-        at = step_rows(i)
+    def out_one(at, sums):
         centred, z = norm_outer(1, r.ex[1, at])
         value, slope = gelu_both(z + r.out0[at].astype(f32))
         r.act[at] = value.astype(bf16)
@@ -763,19 +817,18 @@
         r.gpre[at] = grad
         return sums[0] + fold(grad), sums[1] + fold(grad * centred)
 
-    def top_zero(i, sums):
-        at = step_rows(i)
+    def top_zero(at, sums):
         centred, z = norm_outer(0, r.ex[0, at])
         grad = r.gin[at] * gelu_both(z + inner_input(0, at).astype(f32))[1]
         r.gpre[at] = grad
         return sums[0] + fold(grad), sums[1] + fold(grad * centred)
 
     def backward(s, stat_base, wide_slot, slot):
-        made = stat_start(
-            r.stw, wide_slot, lax.fori_loop(0, steps, out_one if s else top_zero, (zero_w, zero_w))
-        )
+        sums = broad(out_one if s else top_zero, (zero_w, zero_w))
+        made = stat_start(r.stw, wide_slot, sums)
         if s == 1:
             local_out.append(local(r.act, r.act_out))
+        service(s, 1)
         shift_sum, gain_sum = stat_end(r.stw, wide_slot, made)
         r.gbo[s : s + 1] = shift_sum
         r.ggo[s : s + 1] = gain_sum
@@ -783,38 +836,38 @@
         scale = inv * row(r.go, s)
         shift_mean, gain_mean = shift_sum / pixel_total, gain_sum / pixel_total
 
-        def expand_back(i, _):
-            at = step_rows(i)
+        def expand_back(at, _):
             centred = (r.ex[s, at] - mean) * inv
             grad = scale * (r.gpre[at] - (shift_mean + centred * gain_mean))
-            r.gexp[at] = real(grad).astype(bf16)
+            r.gexp[at] = grad.astype(bf16)
             return _
 
-        lax.fori_loop(0, steps, expand_back, 0)
+        broad(expand_back, 0)
         held["sums"] = (zero_n, zero_n)
 
         def weight_expand():
-            r.geo[s] = dot(r.inf[s], r.gexp[...], 0, 0).astype(bf16)
-            weights_out.append(local(r.geo.at[s, cols(chan)], r.ge.at[s, :, wide(chan)]))
-            for j in others:
-                arrivals.append(
-                    remote(r.geo.at[s, cols(j)], r.ge.at[s, :, wide(chan)], (clip, j))
-                )
+            value = dot(r.inf[s], r.gexp[...], 0, 0).astype(bf16)
+            r.geo[s] = value.reshape(r.geo.shape[1:])
+            place = r.ge.at[s, :, :, :, wide(chan)]
+            turned["ge", s] = [local(r.geo.at[s, chan], place)], [
+                remote(r.geo.at[s, j], place, (clip, j)) for j in others
+            ]
+            service(s, 2)
 
         def use_inner(h):
-            def one(i, sums):
-                at = pair_rows(h, i)
+            def one(at, sums):
                 centred, z = norm_inner(s, 1, r.conv[s, at])
-                grad = real(scatter_value(slot, at) * gelu_both(z)[1])
+                grad = scatter_value(slot, at) * gelu_both(z)[1]
                 r.g1[at] = grad
                 return sums[0] + fold(grad), sums[1] + fold(grad * centred)
 
-            held["sums"] = lax.fori_loop(0, pairs, one, held["sums"])
+            held["sums"] = narrow(h, one, held["sums"])
 
         scatter_all(
-            slot, lambda h: dot(r.gexp[part(h)], r.wef[s], 1, 1), use_inner, weight_expand
+            slot, raw, lambda h: dot(r.gexp[raw(h)], r.wef[s], 1, 1), use_inner, weight_expand
         )
         made = stat_start(r.stn, stat_base, held["sums"])
+        service(s, 3)
         shift_sum, gain_sum = stat_end(r.stn, stat_base, made)
         r.gbi[s, 1:2] = shift_sum
         r.ggi[s, 1:2] = gain_sum
@@ -824,9 +877,11 @@
 
         def conv_back(i, _):
             at = pair_rows(0, i)
-            centred = (r.conv[s, at] - mean) * inv
-            grad = real(scale * (r.g1[at] - (shift_mean + centred * gain_mean)))
-            halves = [tiles(grad[:FRAME]), tiles(grad[FRAME:])]
+            halves = []
+            for f in (2 * i, 2 * i + 1):
+                centred = (spread(r.conv.at[s], f) - mean) * inv
+                grad = scale * (spread(r.g1, f) - (shift_mean + centred * gain_mean))
+                halves.append(real(grad))
             for b in (-1, 0, 1):
                 moved = [row_pad(col_shift(v, -b), 1) for v in halves]
                 for a in (-1, 0, 1):
@@ -838,10 +893,10 @@
         lax.fori_loop(0, 2 * pairs, conv_back, 0)
 
         def weight_conv():
-            for piece in range(n_chan):
-                at = pl.ds(piece * ib, ib)
-                value = dot(r.mixf[s, :, piece * ib : (piece + 1) * ib], r.gs[...], 0, 0)
-                r.gc[s, at] = value.astype(bf16)
+            for ref, taps in ((r.gca, slice(0, SPLIT * ib)), (r.gcb, slice(SPLIT * ib, 9 * ib))):
+                value = dot(r.mixf[s], r.gs[:, taps], 0, 0).astype(bf16)
+                ref[s] = value.reshape(ref.shape[1:])
+            service(s, 4)
 
         def use_mixed(h):
             def one(i, _):
@@ -852,7 +907,7 @@
             lax.fori_loop(0, pairs, one, 0)
 
         scatter_all(
-            slot + 1, lambda h: dot(r.gs[part(h)], r.wc[s], 1, 1), use_mixed, weight_conv
+            slot + 1, part, lambda h: dot(r.gs[part(h)], r.wc[s], 1, 1), use_mixed, weight_conv
         )
 
         def tap_sums(grad, v, index, reach):
@@ -899,13 +954,14 @@
                 later = now
                 grad = grad * (1.0 + r.sig[at])
             grad = grad + keep_before * earlier - keep * later
-            centred, z = norm_inner(s, 0, r.red[s, at])
-            grad = real(grad * gelu_both(z)[1])
-            r.g1[at] = grad
-            return sums[0] + fold(grad), sums[1] + fold(grad * centred)
+            centred, z = norm_inner(s, 0, spread(r.red.at[s], f))
+            grad = real(tiles(grad) * gelu_both(z)[1])
+            squeeze(r.g1, f, grad)
+            return sums[0] + jnp.sum(grad, axis=0), sums[1] + jnp.sum(grad * centred, axis=0)
 
         sums = lax.fori_loop(0, frames, hide_back, (zero_n, zero_n))
         made = stat_start(r.stn, stat_base + 1, sums)
+        service(s, 5)
         shift_sum, gain_sum = stat_end(r.stn, stat_base + 1, made)
         r.gbi[s, 0:1] = shift_sum
         r.ggi[s, 0:1] = gain_sum
@@ -915,50 +971,110 @@
         copies = []
         for h in range(2):
 
-            def reduce_back(i, _):
-                at = pair_rows(h, i)
+            def reduce_back(at, _):
                 centred = (r.red[s, at] - mean) * inv
-                grad = real(scale * (r.g1[at] - (shift_mean + centred * gain_mean)))
+                grad = scale * (r.g1[at] - (shift_mean + centred * gain_mean))
                 r.grf[s, at, cols(chan)] = grad.astype(bf16)
                 return _
 
-            lax.fori_loop(0, pairs, reduce_back, 0)
-            copies.append(gather_start(r.grf.at[s], h))
+            narrow(h, reduce_back, 0)
+            copies.append(gather_start(r.grf.at[s], raw(h)))
         if s == 0:
             own = r.grf[0, :, cols(chan)]
             for piece in range(n_chan):
-                at = slice(piece * cs, (piece + 1) * cs)
-                r.gr[0, at] = dot(r.x[:, at], own, 0, 0).astype(bf16)
-        gather_pass(r.grf.at[s], 0, copies[0])
-        gather_pass(r.grf.at[s], 1, copies[1])
+                value = dot(r.x[:, piece * cs : (piece + 1) * cs], own, 0, 0).astype(bf16)
+                r.gr[0, piece] = value.reshape(r.gr.shape[2:])
+        service(s, 6)
+        gather_pass(r.grf.at[s], raw(0), copies[0])
+        gather_pass(r.grf.at[s], raw(1), copies[1])
         if s == 0:
             load_wr[0].wait()
             arrive(weights_in["wr0"])
         for h in range(2):
             gather_end(copies[h])
-            r.gin[part(h)] = dot(r.grf[s, part(h)], r.wrf[s], 1, 1) + r.gpre[part(h)]
+            r.gin[raw(h)] = dot(r.grf[s, raw(h)], r.wrf[s], 1, 1) + r.gpre[raw(h)]
             if s == 0:
-                local_out.append(local(r.gin.at[part(h)], r.gin_out.at[part(h)]))
+                local_out.append(local(r.gin.at[raw(h)], r.gin_out.at[raw(h)]))
         if s == 1:
-            r.gro[...] = dot(r.out0[...], r.grf[1], 0, 0).astype(bf16)
-            weights_out.append(local(r.gro.at[:, cols(chan)], r.gr.at[1, wide(chan)]))
-            for j in others:
-                arrivals.append(remote(r.gro.at[:, cols(j)], r.gr.at[1, wide(chan)], (clip, j)))
-
-    local_out, weights_out, arrivals = [], [], []
+            value = dot(r.out0[...], r.grf[1], 0, 0).astype(bf16)
+            r.gro[...] = value.reshape(r.gro.shape)
+            place = r.gr.at[1, chan]
+            turned["gr", 1] = [local(r.gro.at[:, :, cols(chan)], place)], [
+                remote(r.gro.at[:, :, cols(j)], place, (clip, j)) for j in others
+            ]
+
+    turned = {}
+
+    def reduce_task(name, s, ref, from_side, from_z, result, write_out):
+        mine, across = ref.at[s], (2 * z + 1 - side, chan)
+        if (name, s) in turned:
+            for copy in turned[name, s][0]:
+                copy.wait()
+            arrive(turned[name, s][1])
+        made = remote(mine.at[:, 1 - side], from_side.at[s], across)
+        yield
+        made.wait_recv()
+        for k in range(n_z):
+            both = ref[s, k, side].astype(f32) + from_side[s, k].astype(f32)
+            ref[s, k, side] = both.astype(bf16)
+        made = [
+            remote(mine.at[there, side], from_z.at[s, k], (2 * there + side, chan))
+            for k, there in enumerate(z_others)
+        ]
+        yield
+        arrive(made)
+        total = ref[s, z, side].astype(f32)
+        for k in range(n_z - 1):
+            total = total + from_z[s, k].astype(f32)
+        result[s, z, side] = total.astype(bf16)
+        done = result.at[s, z, side]
+        made = [remote(done, done, (2 * there + side, chan)) for there in z_others]
+        yield
+        arrive(made)
+        done = result.at[s, :, side]
+        made = remote(done, done, across)
+        yield
+        made.wait_recv()
+        write_out(s)
+        yield
+
+    def write_conv(result, base):
+        def write(s):
+            for k in range(result.shape[-1] // ib):
+                here = result.at[s, :, :, :, k * ib : (k + 1) * ib]
+                local_out.append(local(here, r.gc_out.at[s, base + k]))
+
+        return write
+
+    def write_expand(s):
+        local_out.append(local(r.fe.at[s], r.ge_out.at[s]))
+
+    def write_reduce(s):
+        local_out.append(local(r.fr.at[s], r.gr_out.at[s]))
+
+    kinds = {
+        "gca": (r.gca, r.rxa, r.rza, r.fa, write_conv(r.fa, 0)),
+        "gcb": (r.gcb, r.rxb, r.rzb, r.fb, write_conv(r.fb, SPLIT)),
+        "ge": (r.ge, r.rxe, r.rze, r.fe, write_expand),
+        "gr": (r.gr, r.rxr, r.rzr, r.fr, write_reduce),
+    }
+    tasks = {(name, s): reduce_task(name, s, *kinds[name]) for name in kinds for s in range(2)}
+
+    def advance(*steps):
+        for step in steps:
+            next(tasks[step])
+
+    def service(s, point):
+        advance(*PLAN.get((s, point), ()))
+
+    local_out = []
     backward(1, 4, 2, 1)
     backward(0, 6, 3, 3)
 
     for place in range(r.gk.shape[0]):
         r.kst[clip, place : place + 1, :] = jnp.sum(r.gk[place], axis=0, keepdims=True)
     made = [remote(r.kst.at[clip], r.kst.at[clip], (t, chan)) for t in clip_others]
-    arrive(arrivals)
-    for copy in weights_out:
-        copy.wait()
-    for s in range(2):
-        local_out.append(local(r.gc.at[s], r.gc_out.at[s]))
-        local_out.append(local(r.ge.at[s], r.ge_out.at[s]))
-        local_out.append(local(r.gr.at[s], r.gr_out.at[s]))
+    service(0, 7)
     arrive(made)
     total = r.kst[0]
     for k in range(1, n_clip):
@@ -970,6 +1086,7 @@
         copy.wait()
     for copy in list(unsent):
         sent(copy)
+    assert counters["copy"] <= COPIES and counters["load"] <= LOADS, counters
 
 
 def fused_call(n_clip, n_chan, pixel_total, *operands):
@@ -977,6 +1094,9 @@
     cs = width // n_chan
     ib = LANES
     inner = ib * n_chan
+    n_z = n_clip // 2
+    padded = rows // PIXELS * FRAME
+    over = rows + 8
     bf16, f32 = jnp.bfloat16, jnp.float32
     whole = pl.BlockSpec(memory_space=pltpu.VMEM)
     anywhere = pl.BlockSpec(memory_space=pl.ANY)
@@ -991,37 +1111,50 @@
         wef=V((2, inner, cs), bf16),
         wc=V((2, inner, 9 * ib), bf16),
         dkb=V((27, 8, ib), f32),
-        red=V((2, rows, ib), f32),
-        hid=V((2, rows, ib), f32),
-        sig=V((rows, ib), f32),
-        conv=V((2, rows, ib), f32),
-        mixf=V((2, rows, inner), bf16),
+        red=V((2, over, ib), f32),
+        hid=V((2, padded, ib), f32),
+        sig=V((padded, ib), f32),
+        conv=V((2, over, ib), f32),
+        mixf=V((2, padded, inner), bf16),
         inf=V((2, rows, inner), bf16),
         ex=V((2, rows, cs), f32),
         out0=V((rows, cs), bf16),
         act=V((rows, cs), bf16),
-        y=V((rows // 2, 9 * ib), f32),
+        y=V((padded // 2, 9 * ib), f32),
         gpre=V((rows, cs), f32),
         gin=V((rows, cs), f32),
         gexp=V((rows, cs), bf16),
-        gs=V((rows, 9 * ib), bf16),
-        pb=V((rows, inner), bf16),
-        ysend=V((2, rows, ib), bf16),
-        rcore=V((5, 2, rows, ib), bf16),
-        ryy=V((5, rows, ib), bf16),
+        gs=V((padded, 9 * ib), bf16),
+        pb=V((padded, inner), bf16),
+        ysend=V((2, padded, ib), bf16),
+        rcore=V((5, 2, padded, ib), bf16),
+        ryy=V((5, padded, ib), bf16),
         grf=V((2, rows, inner), bf16),
-        gm=V((rows, ib), f32),
-        gd=V((rows, ib), f32),
-        g1=V((rows, ib), f32),
+        gm=V((padded, ib), f32),
+        gd=V((padded, ib), f32),
+        g1=V((over, ib), f32),
         gk=V((32, 8, ib), f32),
         kst=V((n_clip, 32, ib), f32),
         stn=V((8, n_clip, 2, ib), f32),
         stw=V((4, n_clip, 2, cs), f32),
-        gc=V((2, inner, 9 * ib), bf16),
-        geo=V((2, inner, cs), bf16),
-        ge=V((2, ib, width), bf16),
-        gro=V((cs, inner), bf16),
-        gr=V((2, width, ib), bf16),
+        gca=V((2, n_z, 2, inner // n_clip, SPLIT * ib), bf16),
+        gcb=V((2, n_z, 2, inner // n_clip, (9 - SPLIT) * ib), bf16),
+        geo=V((2, n_chan, n_z, 2, ib // n_clip, cs), bf16),
+        ge=V((2, n_z, 2, ib // n_clip, width), bf16),
+        gro=V((2, cs // 2, inner), bf16),
+        gr=V((2, n_z, 2, width // n_clip, ib), bf16),
+        fa=V((2, n_z, 2, inner // n_clip, SPLIT * ib), bf16),
+        fb=V((2, n_z, 2, inner // n_clip, (9 - SPLIT) * ib), bf16),
+        fe=V((2, n_z, 2, ib // n_clip, width), bf16),
+        fr=V((2, n_z, 2, width // n_clip, ib), bf16),
+        rxa=V((2, n_z, inner // n_clip, SPLIT * ib), bf16),
+        rxb=V((2, n_z, inner // n_clip, (9 - SPLIT) * ib), bf16),
+        rxe=V((2, n_z, ib // n_clip, width), bf16),
+        rxr=V((2, n_z, width // n_clip, ib), bf16),
+        rza=V((2, n_z - 1, inner // n_clip, SPLIT * ib), bf16),
+        rzb=V((2, n_z - 1, inner // n_clip, (9 - SPLIT) * ib), bf16),
+        rze=V((2, n_z - 1, ib // n_clip, width), bf16),
+        rzr=V((2, n_z - 1, width // n_clip, ib), bf16),
         ssem=pltpu.SemaphoreType.DMA((COPIES,)),
         rsem=pltpu.SemaphoreType.DMA((COPIES,)),
         lsem=pltpu.SemaphoreType.DMA((LOADS,)),
@@ -1038,9 +1171,9 @@
             shape((2, cs), f32),
             shape((3, 9, ib), f32),
             shape((1, ib), f32),
-            shape((2, inner, 9 * ib), bf16),
-            shape((2, ib, width), bf16),
-            shape((2, width, ib), bf16),
+            shape((2, 9, n_z, 2, inner // n_clip, ib), bf16),
+            shape((2, n_z, 2, ib // n_clip, width), bf16),
+            shape((2, n_z, 2, width // n_clip, ib), bf16),
         ],
         in_specs=[anywhere] * 5 + [scalars] + [whole] * 6,
         out_specs=[anywhere] * 2 + [whole] * 6 + [anywhere] * 3,
@@ -1049,15 +1182,6 @@
             collective_id=0, has_side_effects=True, vmem_limit_bytes=62 * 1024 * 1024
         ),
     )(*operands)
-
-
-def padded_rows(values):
-    frame_rows = values.reshape(-1, SIDE, values.shape[-1])
-    return jnp.pad(frame_rows, ((0, 0), (0, 1), (0, 0))).reshape(-1, values.shape[-1])
-
-
-def real_rows(values):
-    return values.reshape(-1, 8, values.shape[-1])[:, :SIDE].reshape(-1, values.shape[-1])
 
 
 def fused(
@@ -1075,15 +1199,13 @@
     cotangent,
 ):
     n_clip, n_chan = lax.axis_size("clip"), lax.axis_size("chan")
-    col_share = frames_in.shape[1] // n_chan
     pixel_total = frames_in.shape[0] * n_clip
-    col_start = lax.axis_index("chan") * col_share
     act, gin, ggi, gbi, ggo, gbo, gk, ggb, gc, ge, gr = fused_call(
         n_clip,
         n_chan,
         float(pixel_total),
-        padded_rows(frames_in),
-        padded_rows(columns(cotangent, col_start, col_share)),
+        frames_in,
+        cotangent,
         w_reduce,
         w_conv,
         w_expand,
@@ -1095,16 +1217,14 @@
         depth_kernels,
         gate_bias.reshape(1, -1),
     )
-    gr, gc, ge = lax.psum((gr, gc, ge), "clip")
-    gc = gc.reshape(2, gc.shape[1], 9, -1).transpose(0, 2, 1, 3)
     return (
-        real_rows(act),
-        real_rows(gin),
-        gr.astype(jnp.float32),
+        act,
+        gin,
+        gr.astype(jnp.float32).reshape(w_reduce.shape),
         ggi,
         gbi,
-        gc.astype(jnp.float32),
-        ge.astype(jnp.float32),
+        gc.astype(jnp.float32).reshape(w_conv.shape),
+        ge.astype(jnp.float32).reshape(w_expand.shape),
         ggo,
         gbo,
         gk,

time: 382 us -> 251 us (0.66)
  waiting for transfers between devices: 160 us -> 0 us
  Pallas kernels: 175 us -> 233 us
  local copies, waits for them, and re-layouts: 28.1 us -> 6.88 us
  between operations: 14.1 us -> 0.69 us
    psum x1 -> x0, waiting for transfers between devices: 160 us -> none  [fused(): gr, gc, ge = lax.psum((gr, gc, ge), 'clip')]
    pallas_call x1, Pallas kernels: 175 us -> 233 us  [fused_call(): pl.pallas_call(partial(fused_kernel, n_clip, n_chan, pixel_total), out_sh...]
    reshape x6 -> x0, local copies, waits for them, and re-layouts: 14.4 us -> none  [the longest x2 6.03 us: padded_rows(): jnp.pad(frame_rows, ((0, 0), (0, 1), (0, 0))).reshape(-1, values.shape[-1])]
    reshape x0 -> x3, other arithmetic: none -> 7.3 us  [the longest x1 2.84 us: fused(): gc.astype(jnp.float32).reshape(w_conv.shape)]
    convert_element_type x2 -> x0, other arithmetic: 4.39 us -> none  [the longest x1 2.83 us: fused(): gr.astype(jnp.float32)]
    pallas_call x1 -> x0, local copies, waits for them, and re-layouts: 4.27 us -> none  [fused_call(): pl.pallas_call(partial(fused_kernel, n_clip, n_chan, pixel_total), out_sh...]
    unnamed x30 -> x29, local copies, waits for them, and re-layouts: 8.22 us -> 6.88 us
  transfers between devices with their start and end apart: 1 -> 0, of which waited for: 1 -> 0; matrix products, arithmetic and copies ran while one was open for 1% -> 0% of each run, Pallas kernels for 0% -> 0%
where the time goes in v2:
time: 251 us; the launch traced here: 248 us
  Pallas kernels  233 us (93%)
  other arithmetic  7.3 us (3%)
  local copies, waits for them, and re-layouts  6.88 us (3%)
    pallas_call x1, Pallas kernels, fused_call(): pl.pallas_call(partial(fused_kernel, n_clip, n_chan, pixel_total), out_sh...  233 us
    unnamed x29, local copies, waits for them, and re-layouts  6.88 us

profile of v2, /device:TPU:0, one launch (start us, length us, event | category | flops | bytes accessed | tf_op | source)
XLA Modules:
  0.0 248.1 jit_solution(5785610014292426003)
XLA Ops:
  0.6 1.3 copy.23.refs_10_
  2.0 233.2 %shard_map.203 = (bf16[784,512]{1,0:T(8,128)(2,1)}, f32[784,512]{1,0:T(8,128)}, f32[2,2,128]{2,1,0:T(2,128)}, f32[2,2,128]{2,1,0:T(2,128)}, f32[2,512]{1,0:T(2,1...) custom-call(bf16[784,2048]{1,0:T(8,128)(2,1)} %refs_0_.1, ...), custom_call_target="tpu_custom_call" | custom-call | tf_op jit(solution)/shard_map/pallas_call | solution.py:1163
  235.2 0.0 copy-start
  235.2 2.8 %bitcast_convert_fusion.2 = f32[2,2048,128]{2,1,0:T(8,128)} fusion(bf16[2,4,2,256,128]{4,3,2,1,0:T(8,128)(2,1)} %get-tuple-element.24), kind=kLoop, calls=%fused_computation.2 | loop fusion | flops 524288 | bytes 3145728 | tf_op jit(solution)/shard_map/reshape | solution.py:1223
  238.0 0.0 copy-done
  238.0 2.8 %bitcast_convert_fusion = f32[2,9,512,128]{3,2,1,0:T(8,128)} fusion(bf16[2,9,4,2,64,128]{5,4,3,2,1,0:T(8,128)(2,1)S(1)} %copy-done), kind=kLoop, calls=%fused_computation | loop fusion | flops 1179648 | bytes 7077888 | tf_op jit(solution)/shard_map/reshape | solution.py:1226
  240.9 0.0 copy-done.2
  240.9 1.6 bitcast_convert_fusion.1
  242.5 0.0 copy-done.4
  242.5 0.6 copy.24
  243.1 0.0 copy-done.3
  243.1 0.0 copy-start.5
  243.1 0.0 copy-start.9
  243.2 0.9 copy.32
  244.0 0.0 copy-done.1
  244.0 1.2 copy.33
  245.2 0.0 copy-done.8
  245.2 0.6 copy.34
  245.8 0.6 copy.35
  246.4 0.0 copy-done.6
  246.4 0.6 copy.36
  247.0 0.6 copy.37
  247.6 0.0 copy-done.9
  247.6 0.5 copy.38
  (9 shorter events, 0.0 us)
Async XLA Ops:
  235.2 2.8 %copy-start = (bf16[2,9,4,2,64,128]{5,4,3,2,1,0:T(8,128)(2,1)S(1)}, bf16[2,9,4,2,64,128]{5,4,3,2,1,0:T(8,128)(2,1)}, u32[]{:S(2)}) copy-start(bf16[2,9,4,2,64,128]{5,4,3,2,1,0:T(8,128)(2,1)} %get-tuple-element.27) | copy-start | bytes 7077892
  238.0 2.8 %copy-start.2 = (bf16[2,4,2,16,2048]{4,3,2,1,0:T(8,128)(2,1)S(1)}, bf16[2,4,2,16,2048]{4,3,2,1,0:T(8,128)(2,1)}, u32[]{:S(2)}) copy-start(bf16[2,4,2,16,2048]{4,3,2,1,0:T(8,128)(2,1)} %get-tuple-element.28) | copy-start | bytes 3145732
  240.9 1.6 copy-start.4
  240.9 2.3 copy-start.3
  240.9 3.2 %copy-start.1 = (f32[784,512]{1,0:T(8,128)S(1)}, f32[784,512]{1,0:T(8,128)}, u32[]{:S(2)}) copy-start(f32[784,512]{1,0:T(8,128)} %get-tuple-element.56) | copy-start | bytes 4816900
  243.1 2.1 copy-start.8
  243.1 2.7 %copy-start.7 = (f32[2,2,128]{2,1,0:T(2,128)S(1)}, f32[2,2,128]{2,1,0:T(2,128)}, u32[]{:S(2)}) copy-start(f32[2,2,128]{2,1,0:T(2,128)} %get-tuple-element.59) | copy-start | bytes 6148
  243.1 3.2 %copy-start.6 = (f32[2,512]{1,0:T(2,128)S(1)}, f32[2,512]{1,0:T(2,128)}, u32[]{:S(2)}) copy-start(f32[2,512]{1,0:T(2,128)} %get-tuple-element.62) | copy-start | bytes 12292
  243.1 3.8 %copy-start.5 = (f32[2,512]{1,0:T(2,128)S(1)}, f32[2,512]{1,0:T(2,128)}, u32[]{:S(2)}) copy-start(f32[2,512]{1,0:T(2,128)} %get-tuple-element.63) | copy-start | bytes 12292
  243.1 4.4 %copy-start.9 = (f32[1,128]{1,0:T(1,128)S(1)}, f32[1,128]{1,0:T(1,128)}, u32[]{:S(2)}) copy-start(f32[1,128]{1,0:T(1,128)} %get-tuple-element.32) | copy-start | bytes 1540

commit v3 on v2

--- a/solution.py
+++ b/solution.py
@@ -731,7 +731,7 @@
     def spread_taps():
         for index in range(3):
             for tap in range(9):
-                r.dkb[9 * index + tap] = jnp.broadcast_to(r.dk[index, tap : tap + 1, :], (8, ib))
+                r.dkb[9 * index + tap] = jnp.broadcast_to(r.dk[tap, index : index + 1, :], (8, ib))
 
     def clear(i, _):
         r.gk[i] = zero_n
@@ -742,6 +742,7 @@
 
     weights_in = {}
     weights_in["we0"] = share_we(0)
+    weights_in["wr1"] = share_wr(1)
     sums = (zero_n, zero_n)
     load_wr0.wait()
     for h in range(2):
@@ -756,11 +757,11 @@
 
     stage = forward(0, 1, 0)
     next(stage)
-    weights_in["wr1"] = share_wr(1)
     next(stage)
     load_we[0].wait()
     arrive(weights_in["we0"])
     next(stage)
+    weights_in["we1"] = share_we(1)
     for _ in stage:
         pass
 
@@ -795,15 +796,14 @@
     arrive(weights_in["wr1"])
     scatter_all(0, raw, lambda h: dot(r.out0[raw(h)], r.wrf[1]), use_reduced)
     made = stat_start(r.stn, 2, held["sums"])
-    weights_in["we1"] = share_we(1)
     moments_in[1][0] = moments(stat_end(r.stn, 2, made))
     stage = forward(1, 3, 1)
     next(stage)
-    weights_in["wr0"] = share_wr(0)
     next(stage)
     load_we[1].wait()
     arrive(weights_in["we1"])
     next(stage)
+    weights_in["wr0"] = share_wr(0)
     for _ in stage:
         pass
 
@@ -1080,7 +1080,9 @@
     for k in range(1, n_clip):
         total = total + r.kst[k]
     for index in range(3):
-        r.gk_out[index] = total[9 * index : 9 * index + 9]
+        for tap in range(9):
+            place = 9 * index + tap
+            r.gk_out[tap, index : index + 1, :] = total[place : place + 1]
     r.ggb_out[...] = total[27:28]
     for copy in local_out:
         copy.wait()
@@ -1169,7 +1171,7 @@
             shape((2, 2, ib), f32),
             shape((2, cs), f32),
             shape((2, cs), f32),
-            shape((3, 9, ib), f32),
+            shape((9, 3, ib), f32),
             shape((1, ib), f32),
             shape((2, 9, n_z, 2, inner // n_clip, ib), bf16),
             shape((2, n_z, 2, ib // n_clip, width), bf16),
@@ -1182,6 +1184,37 @@
             collective_id=0, has_side_effects=True, vmem_limit_bytes=62 * 1024 * 1024
         ),
     )(*operands)
+
+
+def finish_kernel(*refs):
+    count = len(refs) // 2
+    sources, results = refs[:count], refs[count:]
+    for here, there in zip(sources[:5], results[:5]):
+        there[...] = here[...].astype(there.dtype)
+
+    @pl.when(pl.program_id(0) == 0)
+    def _():
+        for here, there in zip(sources[5:], results[5:]):
+            there[...] = here[...]
+
+
+def finish(steps, gc, ge, gr, act, gin, *small):
+    arrays = [a.reshape(-1, a.shape[-1]) for a in (gc, ge, gr)] + [act, gin]
+    blocks = [
+        pl.BlockSpec((-(-a.shape[0] // (16 * steps)) * 16, a.shape[1]), lambda i: (i, 0))
+        for a in arrays
+    ]
+    whole = [pl.BlockSpec(memory_space=pltpu.VMEM)] * len(small)
+    shapes = [jax.ShapeDtypeStruct(a.shape, jnp.float32) for a in arrays[:3]]
+    shapes += [jax.ShapeDtypeStruct(a.shape, a.dtype) for a in (act, gin, *small)]
+    return pl.pallas_call(
+        finish_kernel,
+        grid=(steps,),
+        out_shape=shapes,
+        in_specs=blocks + whole,
+        out_specs=blocks + whole,
+        compiler_params=pltpu.CompilerParams(vmem_limit_bytes=62 * 1024 * 1024),
+    )(*arrays, *small)
 
 
 def fused(
@@ -1214,20 +1247,23 @@
         bias_inner,
         gain_outer,
         bias_outer,
-        depth_kernels,
+        depth_kernels.transpose(1, 0, 2),
         gate_bias.reshape(1, -1),
+    )
+    gc, ge, gr, act, gin, ggi, gbi, ggo, gbo, gk, ggb = finish(
+        2, gc, ge, gr, act, gin, ggi, gbi, ggo, gbo, gk, ggb
     )
     return (
         act,
         gin,
-        gr.astype(jnp.float32).reshape(w_reduce.shape),
+        gr.reshape(w_reduce.shape),
         ggi,
         gbi,
-        gc.astype(jnp.float32).reshape(w_conv.shape),
-        ge.astype(jnp.float32).reshape(w_expand.shape),
+        gc.reshape(w_conv.shape),
+        ge.reshape(w_expand.shape),
         ggo,
         gbo,
-        gk,
+        gk.transpose(1, 0, 2),
         ggb.reshape(-1),
     )
 

time: 251 us -> 242 us (0.964)
  other arithmetic: 7.3 us -> 0 us
  local copies, waits for them, and re-layouts: 6.88 us -> 0 us
  Pallas kernels: 233 us -> 239 us
    reshape x3 -> x0, other arithmetic: 7.3 us -> none  [the longest x1 2.84 us: fused(): gc.astype(jnp.float32).reshape(w_conv.shape)]
    unnamed x29 -> x0, local copies, waits for them, and re-layouts: 6.88 us -> none
    pallas_call x0 -> x1, Pallas kernels: none -> 6.56 us  [finish(): pl.pallas_call(finish_kernel, grid=(steps,), out_shape=shapes, in_specs=b...]
where the time goes in v3:
time: 242 us; the launch traced here: 240 us
  Pallas kernels  239 us (99%)
    pallas_call x1, Pallas kernels, fused_call(): pl.pallas_call(partial(fused_kernel, n_clip, n_chan, pixel_total), out_sh...  232 us
    pallas_call x1, Pallas kernels, finish(): pl.pallas_call(finish_kernel, grid=(steps,), out_shape=shapes, in_specs=b...  6.56 us

profile of v3, /device:TPU:0, one launch (start us, length us, event | category | flops | bytes accessed | tf_op | source)
XLA Modules:
  0.0 239.5 jit_solution(9165762922230808409)
XLA Ops:
  0.6 232.2 %shard_map.203 = (bf16[784,512]{1,0:T(8,128)(2,1)}, f32[784,512]{1,0:T(8,128)}, f32[2,2,128]{2,1,0:T(2,128)}, f32[2,2,128]{2,1,0:T(2,128)}, f32[2,512]{1,0:T(2,1...) custom-call(bf16[784,2048]{1,0:T(8,128)(2,1)} %refs_0_.1, ...), custom_call_target="tpu_custom_call" | custom-call | tf_op jit(solution)/shard_map/pallas_call | solution.py:1165
  232.8 6.6 %shard_map.204 = (f32[9216,128]{1,0:T(8,128)}, f32[256,2048]{1,0:T(8,128)}, f32[4096,128]{1,0:T(8,128)}, bf16[784,512]{1,0:T(8,128)(2,1)}, f32[784,512]{1,0:T(8,...) custom-call(bf16[9216,128]{1,0:T(8,128)(2,1)} %bitcast.10, ...), custom_call_target="tpu_custom_call" | custom-call | tf_op jit(solution)/shard_map/pallas_call | solution.py:1210

commit v4 on v3

--- a/solution.py
+++ b/solution.py
@@ -300,12 +300,11 @@
 LANES = 128
 FRAME = SIDE * 8
 PIXELS = SIDE * SIDE
-SPLIT = 5
 PAIR = 2 * FRAME
 GELU_A = 0.7978845608028654
 GELU_B = 0.044715
-COPIES = 288
-LOADS = 80
+SENDS = 64
+LOADS = 32
 
 
 def fused_fits(mesh, frame_shape, reduce_shape):
@@ -386,36 +385,62 @@
     "dk", "gb", "act_out", "gin_out", "ggi", "gbi", "ggo", "gbo", "gk_out", "ggb_out", "gc_out",
     "ge_out", "gr_out", "x", "cot", "wr0", "wrf", "wef", "wc", "dkb", "red", "hid", "sig",
     "conv", "mixf", "inf", "ex", "out0", "act", "y", "gpre", "gin", "gexp", "gs", "pb", "ysend",
-    "rcore", "ryy", "grf", "gm", "gd", "g1", "gk", "kst", "stn", "stw", "gca", "gcb", "geo",
-    "ge", "gro", "gr", "rxa", "rxb", "fa", "fb", "fe", "fr", "rxe", "rxr", "rza", "rzb", "rze", "rzr", "ssem", "rsem",
-    "lsem",
+    "rcore", "ryy", "grf", "gm", "gd", "g1", "gk", "kst", "stn", "stw", "gc", "geo", "ge",
+    "gro", "gr", "xc", "xe", "xr", "zc", "ze", "zr", "fc", "fe", "fr", "ssem", "rsem", "lsem",
 )
 
 
+PIECES = {"gc": 9, "ge": 1, "gr": 2}
+ARRIVALS = 40 + 8 * sum(PIECES.values())
 PLAN = {
-    (1, 3): (("ge", 1),),
-    (1, 4): (("ge", 1), ("gca", 1), ("gcb", 1)),
-    (1, 5): (("ge", 1),),
-    (1, 6): (("ge", 1), ("gca", 1)),
-    (0, 1): (("gca", 1), ("gcb", 1), ("ge", 1)),
-    (0, 2): (("gr", 1), ("gcb", 1), ("gca", 1)),
-    (0, 3): (("gr", 1), ("gcb", 1), ("gca", 1), ("ge", 0)),
-    (0, 4): (("gca", 0), ("gcb", 0), ("gr", 1), ("gcb", 1), ("ge", 0)),
-    (0, 5): (("gr", 1), ("ge", 0)),
-    (0, 6): (("gr", 0), ("gca", 0), ("gr", 1), ("ge", 0)),
-    (0, 7): (
-        ("gca", 0),
-        ("gcb", 0),
-        ("ge", 0),
-        ("gr", 0),
-        ("gcb", 0),
-        ("gca", 0),
-        ("gr", 0),
-        ("gcb", 0),
-        ("gr", 0),
-        ("gca", 0),
-        ("gcb", 0),
-        ("gr", 0),
+    (1, "conv_before"): (
+        ("e0", 1),
+    ),
+    (1, "conv"): (
+        ("c0", 1), ("c5", 1), ("c2", 1),
+    ),
+    (1, "red"): (
+        ("c0", 1), ("e0", 1), ("c4", 1), ("c6", 1), ("c8", 1), ("c7", 1), ("c1", 1), ("c3", 1),
+    ),
+    (1, "gather"): (
+        ("c5", 1), ("c2", 1), ("c4", 1),
+    ),
+    (0, "top"): (
+        ("c0", 1), ("c5", 1), ("e0", 1), ("c6", 1), ("c8", 1), ("c7", 1), ("c1", 1),
+    ),
+    (0, "expand_before"): (
+        ("r0", 1), ("r1", 1),
+    ),
+    (0, "inner"): (
+        ("c0", 1), ("c5", 1), ("c2", 1), ("e0", 1), ("c4", 1), ("r0", 1), ("c6", 1), ("c8", 1),
+        ("c7", 1), ("c3", 1), ("r1", 1),
+    ),
+    (0, "conv_before"): (
+        ("c0", 1), ("c1", 1), ("e0", 0),
+    ),
+    (0, "conv"): (
+        ("c8", 0), ("c5", 1), ("c0", 0), ("c2", 1), ("e0", 1),
+    ),
+    (0, "hide_before"): (
+        ("c3", 1),
+    ),
+    (0, "red"): (
+        ("c8", 0), ("c1", 0), ("c2", 0), ("c5", 0), ("c6", 0), ("c4", 1), ("r0", 1), ("c6", 1),
+        ("c8", 1), ("e0", 0),
+    ),
+    (0, "gather"): (
+        ("c2", 1),
+    ),
+    (0, "end"): (
+        ("c3", 0), ("c4", 0), ("c7", 0), ("r0", 0), ("r1", 0), ("c7", 1), ("r1", 1), ("c0", 0),
+        ("c1", 1), ("c3", 1), ("c1", 0), ("c8", 0), ("c2", 0), ("c5", 0), ("r0", 1), ("c6", 0),
+        ("c4", 1), ("c6", 1), ("c8", 1), ("e0", 0), ("c3", 0), ("c4", 0), ("c7", 0), ("r1", 1),
+        ("c0", 0), ("r0", 0), ("c1", 0), ("c8", 0), ("r1", 0), ("c2", 0), ("c7", 1), ("c5", 0),
+        ("c1", 1), ("c6", 0), ("c3", 1), ("r0", 1), ("e0", 0), ("r1", 1), ("c3", 0), ("c8", 0),
+        ("c4", 0), ("c7", 0), ("c0", 0), ("e0", 0), ("r0", 0), ("c0", 0), ("c1", 0), ("r1", 0),
+        ("c1", 0), ("c2", 0), ("c5", 0), ("c6", 0), ("c2", 0), ("c3", 0), ("c5", 0), ("c4", 0),
+        ("c6", 0), ("c7", 0), ("c3", 0), ("c4", 0), ("r0", 0), ("c7", 0), ("r1", 0), ("r0", 0),
+        ("r1", 0),
     ),
 }
 
@@ -453,34 +478,67 @@
     def raw(h):
         return pl.ds(starts[h], counts[h])
 
-    counters = {"copy": 0, "load": 0}
-    unsent = []
-
-    def remote(src, dst, target):
-        index = counters["copy"]
-        counters["copy"] += 1
+    def spans(total):
+        tiles_left, at, chunks = total // 16, 0, []
+        for left in range(4, 0, -1):
+            take = -(-tiles_left // left)
+            chunks.append((at * 16, take * 16))
+            at, tiles_left = at + take, tiles_left - take
+        return chunks
+
+    raw_spans, padded_spans = spans(rows), spans(frames * FRAME)
+
+    places, in_flight, counters = {}, {}, {"send": 0, "load": 0, "phase": 0, "sums": 0}
+
+    def arrival(key):
+        return r.rsem.at[places.setdefault(key, len(places))]
+
+    def sent(index):
+        if index in in_flight:
+            in_flight.pop(index).wait_send()
+
+    def remote(src, dst, target, key):
+        index = counters["send"] % SENDS
+        counters["send"] += 1
+        sent(index)
         made = pltpu.make_async_remote_copy(
             src_ref=src,
             dst_ref=dst,
             send_sem=r.ssem.at[index],
-            recv_sem=r.rsem.at[index],
+            recv_sem=arrival(key),
             device_id=target,
             device_id_type=MESH,
         )
         made.start()
-        unsent.append(made)
-        return made
-
-    def sent(made):
-        made.wait_send()
-        unsent[:] = [other for other in unsent if other is not made]
-
-    def local(src, dst):
-        index = counters["load"]
-        counters["load"] += 1
+        in_flight[index] = made
+        return made, index
+
+    def arrive(place, key):
+        pltpu.make_async_remote_copy(
+            src_ref=place,
+            dst_ref=place,
+            send_sem=r.ssem.at[0],
+            recv_sem=arrival(key),
+            device_id=(clip, j_core),
+            device_id_type=MESH,
+        ).wait_recv()
+
+    def local(src, dst, index=None):
+        if index is None:
+            index = counters["load"]
+            counters["load"] += 1
         made = pltpu.make_async_copy(src, dst, r.lsem.at[index])
         made.start()
         return made
+
+    outgoing = {}
+
+    def write_out(src, dst):
+        turn = counters.setdefault("out", 0) % 8
+        counters["out"] += 1
+        if turn in outgoing:
+            outgoing.pop(turn).wait()
+        outgoing[turn] = local(src, dst, LOADS - 8 + turn)
 
     load_wr0 = local(r.wred_hbm.at[0], r.wr0)
     load_x = [local(r.x_hbm.at[raw(h)], r.x.at[raw(h)]) for h in range(2)]
@@ -490,13 +548,13 @@
     load_wr = [
         local(r.wred_hbm.at[s, wide(chan)], r.wrf.at[s, :, cols(chan)]) for s in range(2)
     ]
-    load_wc = [
-        [
-            local(r.wconv_hbm.at[s, tap], r.wc.at[s, :, tap * ib : (tap + 1) * ib])
-            for tap in range(9)
-        ]
-        for s in range(2)
-    ]
+    load_wc = []
+    for s in range(2):
+        index = counters["load"]
+        counters["load"] += 1
+        for tap in range(9):
+            local(r.wconv_hbm.at[s, tap], r.wc.at[s, :, tap * ib : (tap + 1) * ib], index)
+        load_wc.append(pltpu.make_async_copy(r.wc.at[s], r.wc.at[s], r.lsem.at[index]))
     load_cot = local(r.cot_hbm.at[:, wide(chan)], r.cot)
 
     barrier = pltpu.get_barrier_semaphore()
@@ -507,28 +565,34 @@
     pl.semaphore_wait(barrier, n_clip - 1 + n_chan - 1)
 
     def share_we(s):
-        return [
-            remote(r.wexp_hbm.at[s, :, wide(j)], r.wef.at[s, cols(chan)], (clip, j))
-            for j in others
-        ]
+        for j in others:
+            target = r.wef.at[s, cols(chan)]
+            remote(r.wexp_hbm.at[s, :, wide(j)], target, (clip, j), ("we", s))
 
     def share_wr(s):
-        return [
-            remote(r.wred_hbm.at[s, wide(j)], r.wrf.at[s, :, cols(chan)], (clip, j))
-            for j in others
-        ]
-
-    def arrive(copies):
-        for made in copies:
-            made.wait_recv()
+        for j in others:
+            target = r.wrf.at[s, :, cols(chan)]
+            remote(r.wred_hbm.at[s, wide(j)], target, (clip, j), ("wr", s))
+
+    def shared_we(s):
+        load_we[s].wait()
+        arrive(r.wef.at[s, pl.ds(0, (n_chan - 1) * ib)], ("we", s))
+
+    def shared_wr(s):
+        load_wr[s].wait()
+        arrive(r.wrf.at[s, :, pl.ds(0, (n_chan - 1) * ib)], ("wr", s))
 
     def stat_start(buf, slot, values):
         for k, value in enumerate(values):
             buf[slot, clip, k : k + 1, :] = jnp.sum(value, axis=0, keepdims=True)
-        return [remote(buf.at[slot, clip], buf.at[slot, clip], (t, chan)) for t in clip_others]
-
-    def stat_end(buf, slot, copies):
-        arrive(copies)
+        key = ("sums", counters["sums"] % 2)
+        counters["sums"] += 1
+        for t in clip_others:
+            remote(buf.at[slot, clip], buf.at[slot, clip], (t, chan), key)
+        return key
+
+    def stat_end(buf, slot, key):
+        arrive(buf.at[slot, pl.ds(0, n_clip - 1)], key)
         total = buf[slot, 0]
         for k in range(1, n_clip):
             total = total + buf[slot, k]
@@ -538,37 +602,27 @@
         mean = pair[0] / pixel_total
         return mean, lax.rsqrt(pair[1] / pixel_total - mean * mean + epsilon)
 
-    def gather_start(full, at):
+    def phase_keys(count):
+        turn = counters["phase"] % 2
+        counters["phase"] += 1
+        return [[("chan", turn, k, i) for i in range(3)] for k in range(count)]
+
+    def gather_start(full, at, key):
         mine = full.at[at, cols(chan)]
-        return [remote(mine, mine, (clip, j_y)), remote(mine, mine, (clip, j_core))]
-
-    def gather_pass(full, at, copies):
-        copies[0].wait_recv()
+        remote(mine, mine, (clip, j_y), key[0])
+        remote(mine, mine, (clip, j_core), key[1])
+
+    def gather_pass(full, at, key):
         theirs = full.at[at, cols(j_y)]
-        copies.append(remote(theirs, theirs, (clip, j_core)))
-
-    def gather_end(copies):
-        copies[1].wait_recv()
-        copies[2].wait_recv()
-
-    def scatter_start(slot, at):
-        return [
-            remote(r.pb.at[at, cols(j_far)], r.rcore.at[slot, 1, at], (clip, j_core)),
-            remote(r.pb.at[at, cols(j_core)], r.rcore.at[slot, 0, at], (clip, j_core)),
-        ]
-
-    def scatter_pass(slot, at, copies):
-        copies[0].wait_recv()
-        both = r.pb[at, cols(j_y)].astype(f32) + r.rcore[slot, 1, at].astype(f32)
-        r.ysend[slot % 2, at] = both.astype(bf16)
-        copies.append(remote(r.ysend.at[slot % 2, at], r.ryy.at[slot, at], (clip, j_y)))
-
-    def scatter_end(copies):
-        copies[1].wait_recv()
-        copies[2].wait_recv()
-        sent(copies[0])
-        sent(copies[1])
-        sent(copies[2])
+        arrive(theirs, key[0])
+        remote(theirs, theirs, (clip, j_core), key[2])
+
+    def gather_end(full, at, key):
+        arrive(full.at[at, cols(j_core)], key[1])
+        arrive(full.at[at, cols(j_far)], key[2])
+
+    def pair(value):
+        return pl.ds(pl.multiple_of(value * 2 * ib, 2 * ib), 2 * ib)
 
     def scatter_value(slot, at):
         mine = r.pb[at, cols(chan)].astype(f32)
@@ -596,6 +650,7 @@
             ref[pl.ds(f * PIXELS + SIDE * k, 8), :] = value[k]
 
     pairs = frames // 4
+    carried = {}
     zero_n = jnp.zeros((8, ib), f32)
     zero_w = jnp.zeros((8, cs), f32)
 
@@ -605,9 +660,9 @@
 
         return lax.fori_loop(0, count // step, at_step, begin)
 
-    def narrow(h, one, begin):
-        step = next(n for n in (112, 96, 80, 64, 48, 32, 16) if counts[h] % n == 0)
-        return each(starts[h], counts[h], step, one, begin)
+    def narrow(start, count, one, begin):
+        step = next(n for n in (112, 96, 80, 64, 48, 32, 16) if count % n == 0)
+        return each(start, count, step, one, begin)
 
     def broad(one, begin):
         return each(0, rows, 16, one, begin)
@@ -630,14 +685,17 @@
     def inner_input(s, at):
         return r.x[at, wide(chan)] if s == 0 else r.out0[at]
 
-    def temporal_forward(s, h):
+    def temporal_forward(s, k):
+        h, first_pair = k // 2, k % 2 * (pairs // 2)
+
         def hide(i, _):
             f = h * (frames // 2) + i
             value = real(gelu(norm_inner(s, 0, spread(r.red.at[s], f))[1]))
             r.hid[s, frame_rows(f)] = flat(value)
             return _
 
-        lax.fori_loop(0, frames // 2, hide, 0)
+        if first_pair == 0:
+            lax.fori_loop(0, frames // 2, hide, 0)
 
         def mix(i, before):
             base = pl.multiple_of(h * chunk + i * PAIR, 16)
@@ -665,10 +723,11 @@
             r.mixf[s, pl.ds(base, PAIR), cols(chan)] = both
             return e1
 
-        lax.fori_loop(0, pairs, mix, jnp.zeros((SIDE, 8, ib), f32))
-
-    def conv_forward(s, h, sums):
-        r.y[...] = dot(r.mixf[s, part(h)], r.wc[s])
+        before = carried.get(s) if first_pair else jnp.zeros((SIDE, 8, ib), f32)
+        carried[s] = lax.fori_loop(first_pair, first_pair + pairs // 2, mix, before)
+
+    def conv_forward(s, k, sums):
+        r.y[...] = dot(r.mixf[s, pl.ds(*padded_spans[k])], r.wc[s])
 
         def add_taps(i, sums):
             at = pl.ds(pl.multiple_of(i * FRAME, 8), FRAME)
@@ -683,29 +742,30 @@
                 run = col_shift(run, b)
                 total = run if total is None else total + run
             total = real(total)
-            squeeze(r.conv.at[s], h * (frames // 2) + i, total)
+            squeeze(r.conv.at[s], k * (frames // 4) + i, total)
             return sums[0] + jnp.sum(total, axis=0), sums[1] + jnp.sum(total * total, axis=0)
 
-        return lax.fori_loop(0, frames // 2, add_taps, sums)
+        return lax.fori_loop(0, frames // 4, add_taps, sums)
 
     def forward(s, stat_base, wide_slot):
-        copies = []
-        for h in range(2):
-            temporal_forward(s, h)
-            copies.append(gather_start(r.mixf.at[s], part(h)))
+        keys = phase_keys(4)
+        quarters = [pl.ds(*span) for span in padded_spans]
+        for k in range(4):
+            temporal_forward(s, k)
+            gather_start(r.mixf.at[s], quarters[k], keys[k])
+            if k > 0:
+                gather_pass(r.mixf.at[s], quarters[k - 1], keys[k - 1])
         sums = (zero_n, zero_n)
-        for made in load_wc[s]:
-            made.wait()
-        gather_pass(r.mixf.at[s], part(0), copies[0])
-        for h in range(2):
-            gather_end(copies[h])
-            sums = conv_forward(s, h, sums)
-            if h == 0:
-                gather_pass(r.mixf.at[s], part(1), copies[1])
+        load_wc[s].wait()
+        for k in range(4):
+            gather_end(r.mixf.at[s], quarters[k], keys[k])
+            if k == 0:
+                gather_pass(r.mixf.at[s], quarters[3], keys[3])
+            sums = conv_forward(s, k, sums)
         made = stat_start(r.stn, stat_base, sums)
         yield
         moments_in[s][1] = moments(stat_end(r.stn, stat_base, made))
-        copies = []
+        keys = phase_keys(2)
         for h in range(2):
 
             def inside(at, _):
@@ -713,14 +773,14 @@
                 r.inf[s, at, cols(chan)] = value.astype(bf16)
                 return _
 
-            narrow(h, inside, 0)
-            copies.append(gather_start(r.inf.at[s], raw(h)))
+            narrow(starts[h], counts[h], inside, 0)
+            gather_start(r.inf.at[s], raw(h), keys[h])
         yield
-        gather_pass(r.inf.at[s], raw(0), copies[0])
-        gather_pass(r.inf.at[s], raw(1), copies[1])
+        gather_pass(r.inf.at[s], raw(0), keys[0])
+        gather_pass(r.inf.at[s], raw(1), keys[1])
         sums = (zero_w, zero_w)
         for h in range(2):
-            gather_end(copies[h])
+            gather_end(r.inf.at[s], raw(h), keys[h])
             value = dot(r.inf[s, raw(h)], r.wef[s])
             r.ex[s, raw(h)] = value
             sums = (sums[0] + fold(value), sums[1] + fold(value * value))
@@ -740,9 +800,8 @@
     for s in range(2):
         r.red[s, rows : rows + 8] = zero_n
 
-    weights_in = {}
-    weights_in["we0"] = share_we(0)
-    weights_in["wr1"] = share_wr(1)
+    share_we(0)
+    share_wr(1)
     sums = (zero_n, zero_n)
     load_wr0.wait()
     for h in range(2):
@@ -758,10 +817,9 @@
     stage = forward(0, 1, 0)
     next(stage)
     next(stage)
-    load_we[0].wait()
-    arrive(weights_in["we0"])
+    shared_we(0)
     next(stage)
-    weights_in["we1"] = share_we(1)
+    share_we(1)
     for _ in stage:
         pass
 
@@ -772,38 +830,65 @@
 
     broad(out_zero, 0)
 
-    def scatter_all(slot, chunk_rows, product, use, beside=None):
-        copies = []
-        for h in range(2):
-            r.pb[chunk_rows(h)] = product(h).astype(bf16)
-            copies.append(scatter_start(slot, chunk_rows(h)))
-        scatter_pass(slot, chunk_rows(0), copies[0])
-        scatter_pass(slot, chunk_rows(1), copies[1])
+    def scatter_all(slot, chunks, product, use, beside=None):
+        keys = phase_keys(4)
+        ats = [pl.ds(*span) for span in chunks]
+        borrowed = []
+
+        def start(k, away):
+            two = pair(1 - high if away else high)
+            r.pb[ats[k], two] = product(ats[k], two).astype(bf16)
+            block, index = (j_far, 1) if away else (j_core, 0)
+            target = r.rcore.at[slot, index, ats[k]]
+            made = remote(r.pb.at[ats[k], cols(block)], target, (clip, j_core), keys[k][index])
+            borrowed.append(made[1])
+
+        def hand_on(k):
+            at = ats[k]
+            arrive(r.rcore.at[slot, 1, at], keys[k][1])
+            both = r.pb[at, cols(j_y)].astype(f32) + r.rcore[slot, 1, at].astype(f32)
+            r.ysend[slot % 2, at] = both.astype(bf16)
+            made = remote(r.ysend.at[slot % 2, at], r.ryy.at[slot, at], (clip, j_y), keys[k][2])
+            borrowed.append(made[1])
+
+        start(0, True)
+        start(1, True)
+        hand_on(0)
+        start(2, True)
+        hand_on(1)
+        start(3, True)
+        hand_on(2)
+        start(0, False)
+        hand_on(3)
+        for k in range(1, 4):
+            start(k, False)
         if beside is not None:
             beside()
-        for h in range(2):
-            scatter_end(copies[h])
-            use(h)
+        for k in range(4):
+            arrive(r.rcore.at[slot, 0, ats[k]], keys[k][0])
+            arrive(r.ryy.at[slot, ats[k]], keys[k][2])
+            use(*chunks[k])
+        for index in borrowed:
+            sent(index)
 
     held = {"sums": (zero_n, zero_n)}
 
-    def use_reduced(h):
-        value = scatter_value(0, raw(h))
-        r.red[1, raw(h)] = value
+    def use_reduced(begin, count):
+        at = pl.ds(begin, count)
+        value = scatter_value(0, at)
+        r.red[1, at] = value
         held["sums"] = (held["sums"][0] + fold(value), held["sums"][1] + fold(value * value))
 
-    load_wr[1].wait()
-    arrive(weights_in["wr1"])
-    scatter_all(0, raw, lambda h: dot(r.out0[raw(h)], r.wrf[1]), use_reduced)
+    shared_wr(1)
+    scatter_all(0, raw_spans, lambda at, two: dot(r.out0[at], r.wrf[1, :, two]), use_reduced)
     made = stat_start(r.stn, 2, held["sums"])
     moments_in[1][0] = moments(stat_end(r.stn, 2, made))
     stage = forward(1, 3, 1)
     next(stage)
     next(stage)
-    load_we[1].wait()
-    arrive(weights_in["we1"])
+    shared_we(1)
     next(stage)
-    weights_in["wr0"] = share_wr(0)
+    share_wr(0)
     for _ in stage:
         pass
 
@@ -827,8 +912,8 @@
         sums = broad(out_one if s else top_zero, (zero_w, zero_w))
         made = stat_start(r.stw, wide_slot, sums)
         if s == 1:
-            local_out.append(local(r.act, r.act_out))
-        service(s, 1)
+            write_out(r.act, r.act_out)
+        service(s, "top")
         shift_sum, gain_sum = stat_end(r.stw, wide_slot, made)
         r.gbo[s : s + 1] = shift_sum
         r.ggo[s : s + 1] = gain_sum
@@ -844,30 +929,35 @@
 
         broad(expand_back, 0)
         held["sums"] = (zero_n, zero_n)
+        service(s, "expand_before")
 
         def weight_expand():
             value = dot(r.inf[s], r.gexp[...], 0, 0).astype(bf16)
             r.geo[s] = value.reshape(r.geo.shape[1:])
             place = r.ge.at[s, :, :, :, wide(chan)]
-            turned["ge", s] = [local(r.geo.at[s, chan], place)], [
-                remote(r.geo.at[s, j], place, (clip, j)) for j in others
-            ]
-            service(s, 2)
-
-        def use_inner(h):
+            turned["ge", s] = local(r.geo.at[s, chan], place)
+            for j in others:
+                remote(r.geo.at[s, j], place, (clip, j), ("ge", s))
+            service(s, "expand")
+
+        def use_inner(begin, count):
             def one(at, sums):
                 centred, z = norm_inner(s, 1, r.conv[s, at])
                 grad = scatter_value(slot, at) * gelu_both(z)[1]
                 r.g1[at] = grad
                 return sums[0] + fold(grad), sums[1] + fold(grad * centred)
 
-            held["sums"] = narrow(h, one, held["sums"])
+            held["sums"] = narrow(begin, count, one, held["sums"])
 
         scatter_all(
-            slot, raw, lambda h: dot(r.gexp[raw(h)], r.wef[s], 1, 1), use_inner, weight_expand
+            slot,
+            raw_spans,
+            lambda at, two: dot(r.gexp[at], r.wef[s, two], 1, 1),
+            use_inner,
+            weight_expand,
         )
         made = stat_start(r.stn, stat_base, held["sums"])
-        service(s, 3)
+        service(s, "inner")
         shift_sum, gain_sum = stat_end(r.stn, stat_base, made)
         r.gbi[s, 1:2] = shift_sum
         r.ggi[s, 1:2] = gain_sum
@@ -892,22 +982,28 @@
 
         lax.fori_loop(0, 2 * pairs, conv_back, 0)
 
+        service(s, "conv_before")
+
         def weight_conv():
-            for ref, taps in ((r.gca, slice(0, SPLIT * ib)), (r.gcb, slice(SPLIT * ib, 9 * ib))):
+            for k in range(3):
+                taps = slice(3 * k * ib, 3 * (k + 1) * ib)
                 value = dot(r.mixf[s], r.gs[:, taps], 0, 0).astype(bf16)
-                ref[s] = value.reshape(ref.shape[1:])
-            service(s, 4)
-
-        def use_mixed(h):
-            def one(i, _):
-                at = pair_rows(h, i)
+                r.gc[s, :, :, :, taps] = value.reshape(r.gc.shape[1:4] + (3 * ib,))
+            service(s, "conv")
+
+        def use_mixed(begin, count):
+            def one(at, _):
                 r.gm[at] = real(scatter_value(slot + 1, at))
                 return _
 
-            lax.fori_loop(0, pairs, one, 0)
+            narrow(begin, count, one, 0)
 
         scatter_all(
-            slot + 1, part, lambda h: dot(r.gs[part(h)], r.wc[s], 1, 1), use_mixed, weight_conv
+            slot + 1,
+            padded_spans,
+            lambda at, two: dot(r.gs[at], r.wc[s, two], 1, 1),
+            use_mixed,
+            weight_conv,
         )
 
         def tap_sums(grad, v, index, reach):
@@ -937,6 +1033,8 @@
             return step
 
         lax.fori_loop(0, frames, mix_back, jnp.zeros((SIDE, 8, ib), f32))
+
+        service(s, "hide_before")
 
         def hide_back(f, sums):
             at = frame_rows(f)
@@ -961,14 +1059,14 @@
 
         sums = lax.fori_loop(0, frames, hide_back, (zero_n, zero_n))
         made = stat_start(r.stn, stat_base + 1, sums)
-        service(s, 5)
+        service(s, "red")
         shift_sum, gain_sum = stat_end(r.stn, stat_base + 1, made)
         r.gbi[s, 0:1] = shift_sum
         r.ggi[s, 0:1] = gain_sum
         mean, inv = moments_in[s][0]
         scale = inv * row(r.gi, s, 0)
         shift_mean, gain_mean = shift_sum / pixel_total, gain_sum / pixel_total
-        copies = []
+        keys = phase_keys(2)
         for h in range(2):
 
             def reduce_back(at, _):
@@ -977,88 +1075,96 @@
                 r.grf[s, at, cols(chan)] = grad.astype(bf16)
                 return _
 
-            narrow(h, reduce_back, 0)
-            copies.append(gather_start(r.grf.at[s], raw(h)))
+            narrow(starts[h], counts[h], reduce_back, 0)
+            gather_start(r.grf.at[s], raw(h), keys[h])
         if s == 0:
             own = r.grf[0, :, cols(chan)]
             for piece in range(n_chan):
                 value = dot(r.x[:, piece * cs : (piece + 1) * cs], own, 0, 0).astype(bf16)
                 r.gr[0, piece] = value.reshape(r.gr.shape[2:])
-        service(s, 6)
-        gather_pass(r.grf.at[s], raw(0), copies[0])
-        gather_pass(r.grf.at[s], raw(1), copies[1])
+        service(s, "gather")
+        gather_pass(r.grf.at[s], raw(0), keys[0])
+        gather_pass(r.grf.at[s], raw(1), keys[1])
         if s == 0:
-            load_wr[0].wait()
-            arrive(weights_in["wr0"])
+            shared_wr(0)
         for h in range(2):
-            gather_end(copies[h])
+            gather_end(r.grf.at[s], raw(h), keys[h])
             r.gin[raw(h)] = dot(r.grf[s, raw(h)], r.wrf[s], 1, 1) + r.gpre[raw(h)]
             if s == 0:
-                local_out.append(local(r.gin.at[raw(h)], r.gin_out.at[raw(h)]))
+                write_out(r.gin.at[raw(h)], r.gin_out.at[raw(h)])
+        service(s, "last")
         if s == 1:
             value = dot(r.out0[...], r.grf[1], 0, 0).astype(bf16)
             r.gro[...] = value.reshape(r.gro.shape)
             place = r.gr.at[1, chan]
-            turned["gr", 1] = [local(r.gro.at[:, :, cols(chan)], place)], [
-                remote(r.gro.at[:, :, cols(j)], place, (clip, j)) for j in others
-            ]
+            turned["gr", 1] = local(r.gro.at[:, :, cols(chan)], place)
+            for j in others:
+                remote(r.gro.at[:, :, cols(j)], place, (clip, j), ("gr", 1))
 
     turned = {}
 
-    def reduce_task(name, s, ref, from_side, from_z, result, write_out):
-        mine, across = ref.at[s], (2 * z + 1 - side, chan)
-        if (name, s) in turned:
-            for copy in turned[name, s][0]:
-                copy.wait()
-            arrive(turned[name, s][1])
-        made = remote(mine.at[:, 1 - side], from_side.at[s], across)
+    def reduce_task(kind, s, line, place):
+        ref, from_side, from_z, result = kinds[kind]
+        mine, done = ref.at[s, :, :, line, place], result.at[s, :, :, line, place]
+        side_in, z_in = from_side.at[s, :, line, place], from_z.at[s, :, line, place]
+        across = (2 * z + 1 - side, chan)
+        key = (kind, s, line.start, place.start)
+        if (kind, s) in turned:
+            turned.pop((kind, s)).wait()
+            three = pl.ds(0, (n_chan - 1) * cs)
+            arrive(
+                r.ge.at[s, :, :, :, three] if kind == "ge" else r.gr.at[s, pl.ds(0, n_chan - 1)],
+                (kind, s),
+            )
+        remote(mine.at[:, 1 - side], side_in, across, key + (0,))
         yield
-        made.wait_recv()
+        arrive(side_in, key + (0,))
         for k in range(n_z):
-            both = ref[s, k, side].astype(f32) + from_side[s, k].astype(f32)
-            ref[s, k, side] = both.astype(bf16)
-        made = [
-            remote(mine.at[there, side], from_z.at[s, k], (2 * there + side, chan))
-            for k, there in enumerate(z_others)
-        ]
+            both = ref[s, k, side, line, place].astype(f32)
+            both = both + from_side[s, k, line, place].astype(f32)
+            ref[s, k, side, line, place] = both.astype(bf16)
+        for k, there in enumerate(z_others):
+            remote(mine.at[there, side], z_in.at[k], (2 * there + side, chan), key + (1,))
         yield
-        arrive(made)
-        total = ref[s, z, side].astype(f32)
+        arrive(z_in, key + (1,))
+        total = ref[s, z, side, line, place].astype(f32)
         for k in range(n_z - 1):
-            total = total + from_z[s, k].astype(f32)
-        result[s, z, side] = total.astype(bf16)
-        done = result.at[s, z, side]
-        made = [remote(done, done, (2 * there + side, chan)) for there in z_others]
+            total = total + from_z[s, k, line, place].astype(f32)
+        result[s, z, side, line, place] = total.astype(bf16)
+        own = done.at[z, side]
+        for there in z_others:
+            remote(own, own, (2 * there + side, chan), key + (2,))
         yield
-        arrive(made)
-        done = result.at[s, :, side]
-        made = remote(done, done, across)
+        arrive(done.at[pl.ds(0, n_z - 1), side], key + (2,))
+        remote(done.at[:, side], done.at[:, side], across, key + (3,))
         yield
-        made.wait_recv()
-        write_out(s)
+        arrive(done.at[:, 1 - side], key + (3,))
+        if kind == "gc":
+            base = place.start // ib
+            for k in range((place.stop - place.start) // ib):
+                here = r.fc.at[s, :, :, :, (base + k) * ib : (base + k + 1) * ib]
+                write_out(here, r.gc_out.at[s, base + k])
+        else:
+            out = {"ge": r.ge_out, "gr": r.gr_out}[kind]
+            write_out(done, out.at[s, :, :, line, place])
         yield
 
-    def write_conv(result, base):
-        def write(s):
-            for k in range(result.shape[-1] // ib):
-                here = result.at[s, :, :, :, k * ib : (k + 1) * ib]
-                local_out.append(local(here, r.gc_out.at[s, base + k]))
-
-        return write
-
-    def write_expand(s):
-        local_out.append(local(r.fe.at[s], r.ge_out.at[s]))
-
-    def write_reduce(s):
-        local_out.append(local(r.fr.at[s], r.gr_out.at[s]))
-
     kinds = {
-        "gca": (r.gca, r.rxa, r.rza, r.fa, write_conv(r.fa, 0)),
-        "gcb": (r.gcb, r.rxb, r.rzb, r.fb, write_conv(r.fb, SPLIT)),
-        "ge": (r.ge, r.rxe, r.rze, r.fe, write_expand),
-        "gr": (r.gr, r.rxr, r.rzr, r.fr, write_reduce),
+        "gc": (r.gc, r.xc, r.zc, r.fc),
+        "ge": (r.ge, r.xe, r.ze, r.fe),
+        "gr": (r.gr, r.xr, r.zr, r.fr),
     }
-    tasks = {(name, s): reduce_task(name, s, *kinds[name]) for name in kinds for s in range(2)}
+    def cut(size, count):
+        return [slice(k * (size // count), (k + 1) * (size // count)) for k in range(count)]
+
+    tasks = {}
+    for s in range(2):
+        for k, place in enumerate(cut(9 * ib, PIECES["gc"])):
+            tasks[f"c{k}", s] = reduce_task("gc", s, slice(0, r.gc.shape[3]), place)
+        for k, place in enumerate(cut(r.ge.shape[4], PIECES["ge"])):
+            tasks[f"e{k}", s] = reduce_task("ge", s, slice(0, r.ge.shape[3]), place)
+        for k, line in enumerate(cut(r.gr.shape[3], PIECES["gr"])):
+            tasks[f"r{k}", s] = reduce_task("gr", s, line, slice(0, ib))
 
     def advance(*steps):
         for step in steps:
@@ -1067,15 +1173,15 @@
     def service(s, point):
         advance(*PLAN.get((s, point), ()))
 
-    local_out = []
     backward(1, 4, 2, 1)
     backward(0, 6, 3, 3)
 
     for place in range(r.gk.shape[0]):
         r.kst[clip, place : place + 1, :] = jnp.sum(r.gk[place], axis=0, keepdims=True)
-    made = [remote(r.kst.at[clip], r.kst.at[clip], (t, chan)) for t in clip_others]
-    service(0, 7)
-    arrive(made)
+    for t in clip_others:
+        remote(r.kst.at[clip], r.kst.at[clip], (t, chan), "taps")
+    service(0, "end")
+    arrive(r.kst.at[pl.ds(0, n_clip - 1)], "taps")
     total = r.kst[0]
     for k in range(1, n_clip):
         total = total + r.kst[k]
@@ -1084,11 +1190,11 @@
             place = 9 * index + tap
             r.gk_out[tap, index : index + 1, :] = total[place : place + 1]
     r.ggb_out[...] = total[27:28]
-    for copy in local_out:
+    for copy in outgoing.values():
         copy.wait()
-    for copy in list(unsent):
-        sent(copy)
-    assert counters["copy"] <= COPIES and counters["load"] <= LOADS, counters
+    for index in list(in_flight):
+        sent(index)
+    assert len(places) <= ARRIVALS and counters["load"] <= LOADS - 8, (places, counters)
 
 
 def fused_call(n_clip, n_chan, pixel_total, *operands):
@@ -1122,7 +1228,7 @@
         ex=V((2, rows, cs), f32),
         out0=V((rows, cs), bf16),
         act=V((rows, cs), bf16),
-        y=V((padded // 2, 9 * ib), f32),
+        y=V((padded // 4, 9 * ib), f32),
         gpre=V((rows, cs), f32),
         gin=V((rows, cs), f32),
         gexp=V((rows, cs), bf16),
@@ -1139,26 +1245,22 @@
         kst=V((n_clip, 32, ib), f32),
         stn=V((8, n_clip, 2, ib), f32),
         stw=V((4, n_clip, 2, cs), f32),
-        gca=V((2, n_z, 2, inner // n_clip, SPLIT * ib), bf16),
-        gcb=V((2, n_z, 2, inner // n_clip, (9 - SPLIT) * ib), bf16),
+        gc=V((2, n_z, 2, inner // n_clip, 9 * ib), bf16),
         geo=V((2, n_chan, n_z, 2, ib // n_clip, cs), bf16),
         ge=V((2, n_z, 2, ib // n_clip, width), bf16),
         gro=V((2, cs // 2, inner), bf16),
         gr=V((2, n_z, 2, width // n_clip, ib), bf16),
-        fa=V((2, n_z, 2, inner // n_clip, SPLIT * ib), bf16),
-        fb=V((2, n_z, 2, inner // n_clip, (9 - SPLIT) * ib), bf16),
+        fc=V((2, n_z, 2, inner // n_clip, 9 * ib), bf16),
         fe=V((2, n_z, 2, ib // n_clip, width), bf16),
         fr=V((2, n_z, 2, width // n_clip, ib), bf16),
-        rxa=V((2, n_z, inner // n_clip, SPLIT * ib), bf16),
-        rxb=V((2, n_z, inner // n_clip, (9 - SPLIT) * ib), bf16),
-        rxe=V((2, n_z, ib // n_clip, width), bf16),
-        rxr=V((2, n_z, width // n_clip, ib), bf16),
-        rza=V((2, n_z - 1, inner // n_clip, SPLIT * ib), bf16),
-        rzb=V((2, n_z - 1, inner // n_clip, (9 - SPLIT) * ib), bf16),
-        rze=V((2, n_z - 1, ib // n_clip, width), bf16),
-        rzr=V((2, n_z - 1, width // n_clip, ib), bf16),
-        ssem=pltpu.SemaphoreType.DMA((COPIES,)),
-        rsem=pltpu.SemaphoreType.DMA((COPIES,)),
+        xc=V((2, n_z, inner // n_clip, 9 * ib), bf16),
+        xe=V((2, n_z, ib // n_clip, width), bf16),
+        xr=V((2, n_z, width // n_clip, ib), bf16),
+        zc=V((2, n_z - 1, inner // n_clip, 9 * ib), bf16),
+        ze=V((2, n_z - 1, ib // n_clip, width), bf16),
+        zr=V((2, n_z - 1, width // n_clip, ib), bf16),
+        ssem=pltpu.SemaphoreType.DMA((SENDS,)),
+        rsem=pltpu.SemaphoreType.DMA((ARRIVALS,)),
         lsem=pltpu.SemaphoreType.DMA((LOADS,)),
     )
     first = NAMES.index("x")

time: 242 us -> 234 us (0.967); the launches traced: 240 us -> 234 us
  Pallas kernels: 239 us -> 233 us
    pallas_call x1, Pallas kernels: 232 us -> 227 us  [fused_call(): pl.pallas_call(partial(fused_kernel, n_clip, n_chan, pixel_total), out_sh...]
where the time goes in v4:
time: 234 us
  Pallas kernels  233 us (100%)
    pallas_call x1, Pallas kernels, fused_call(): pl.pallas_call(partial(fused_kernel, n_clip, n_chan, pixel_total), out_sh...  227 us
    pallas_call x1, Pallas kernels, finish(): pl.pallas_call(finish_kernel, grid=(steps,), out_shape=shapes, in_specs=b...  6.56 us

profile of v4, /device:TPU:0, one launch (start us, length us, event | category | flops | bytes accessed | tf_op | source)
XLA Modules:
  0.0 234.0 jit_solution(11739485720330835100)
XLA Ops:
  0.6 226.6 %shard_map.203 = (bf16[784,512]{1,0:T(8,128)(2,1)}, f32[784,512]{1,0:T(8,128)}, f32[2,2,128]{2,1,0:T(2,128)}, f32[2,2,128]{2,1,0:T(2,128)}, f32[2,512]{1,0:T(2,1...) custom-call(bf16[784,2048]{1,0:T(8,128)(2,1)} %refs_0_.1, ...), custom_call_target="tpu_custom_call" | custom-call | tf_op jit(solution)/shard_map/pallas_call | solution.py:1267
  227.3 6.6 %shard_map.204 = (f32[9216,128]{1,0:T(8,128)}, f32[256,2048]{1,0:T(8,128)}, f32[4096,128]{1,0:T(8,128)}, bf16[784,512]{1,0:T(8,128)(2,1)}, f32[784,512]{1,0:T(8,...) custom-call(bf16[9216,128]{1,0:T(8,128)(2,1)} %bitcast.10, ...), custom_call_target="tpu_custom_call" | custom-call | tf_op jit(solution)/shard_map/pallas_call | solution.py:1312

commit v5 on v4

--- a/solution.py
+++ b/solution.py
@@ -390,57 +390,69 @@
 )
 
 
-PIECES = {"gc": 9, "ge": 1, "gr": 2}
+PIECES = {"gc": 3, "ge": 4, "gr": 4}
 ARRIVALS = 40 + 8 * sum(PIECES.values())
 PLAN = {
     (1, "conv_before"): (
-        ("e0", 1),
+        ("e1", 1), ("e2", 1), ("e3", 1), ("e0", 1),
     ),
     (1, "conv"): (
-        ("c0", 1), ("c5", 1), ("c2", 1),
+        ("c0", 1), ("e1", 1), ("e2", 1), ("c2", 1),
+    ),
+    (1, "conv_use"): (
+        ("e3", 1), ("e0", 1),
+    ),
+    (1, "hide_before"): (
+        ("e1", 1), ("e2", 1),
     ),
     (1, "red"): (
-        ("c0", 1), ("e0", 1), ("c4", 1), ("c6", 1), ("c8", 1), ("c7", 1), ("c1", 1), ("c3", 1),
-    ),
-    (1, "gather"): (
-        ("c5", 1), ("c2", 1), ("c4", 1),
+        ("c0", 1), ("e3", 1), ("c2", 1), ("e0", 1), ("c1", 1), ("e1", 1),
+    ),
+    (1, "red_after"): (
+        ("e2", 1),
+    ),
+    (1, "last"): (
+        ("e1", 1), ("e3", 1),
     ),
     (0, "top"): (
-        ("c0", 1), ("c5", 1), ("e0", 1), ("c6", 1), ("c8", 1), ("c7", 1), ("c1", 1),
+        ("c0", 1), ("e2", 1), ("e3", 1), ("c2", 1), ("e0", 1), ("c1", 1),
     ),
     (0, "expand_before"): (
-        ("r0", 1), ("r1", 1),
+        ("r3", 1), ("r1", 1), ("r2", 1), ("r0", 1),
+    ),
+    (0, "expand"): (
+        ("c0", 1), ("r3", 1), ("r1", 1), ("e0", 1),
     ),
     (0, "inner"): (
-        ("c0", 1), ("c5", 1), ("c2", 1), ("e0", 1), ("c4", 1), ("r0", 1), ("c6", 1), ("c8", 1),
-        ("c7", 1), ("c3", 1), ("r1", 1),
+        ("r2", 1), ("c2", 1), ("r0", 1), ("c1", 1),
     ),
     (0, "conv_before"): (
-        ("c0", 1), ("c1", 1), ("e0", 0),
+        ("c0", 1), ("r3", 1), ("e1", 0), ("r1", 1), ("e0", 0), ("e2", 0), ("e3", 0), ("r2", 1),
     ),
     (0, "conv"): (
-        ("c8", 0), ("c5", 1), ("c0", 0), ("c2", 1), ("e0", 1),
+        ("c2", 0), ("e1", 0), ("c1", 0), ("e0", 0), ("e2", 0), ("c0", 0), ("c2", 1), ("r0", 1),
+    ),
+    (0, "conv_use"): (
+        ("r3", 1), ("e3", 0),
     ),
     (0, "hide_before"): (
-        ("c3", 1),
+        ("c2", 0),
     ),
     (0, "red"): (
-        ("c8", 0), ("c1", 0), ("c2", 0), ("c5", 0), ("c6", 0), ("c4", 1), ("r0", 1), ("c6", 1),
-        ("c8", 1), ("e0", 0),
+        ("e1", 0), ("c1", 0), ("r1", 1), ("e0", 0), ("e2", 0), ("c0", 0), ("e3", 0), ("r2", 1),
+        ("r0", 1), ("c1", 1), ("r3", 1),
     ),
     (0, "gather"): (
-        ("c2", 1),
+        ("r1", 0), ("r1", 1), ("r0", 0),
+    ),
+    (0, "gather_use"): (
+        ("c2", 0), ("e1", 0), ("r2", 0), ("r2", 1), ("r0", 1), ("r3", 0),
     ),
     (0, "end"): (
-        ("c3", 0), ("c4", 0), ("c7", 0), ("r0", 0), ("r1", 0), ("c7", 1), ("r1", 1), ("c0", 0),
-        ("c1", 1), ("c3", 1), ("c1", 0), ("c8", 0), ("c2", 0), ("c5", 0), ("r0", 1), ("c6", 0),
-        ("c4", 1), ("c6", 1), ("c8", 1), ("e0", 0), ("c3", 0), ("c4", 0), ("c7", 0), ("r1", 1),
-        ("c0", 0), ("r0", 0), ("c1", 0), ("c8", 0), ("r1", 0), ("c2", 0), ("c7", 1), ("c5", 0),
-        ("c1", 1), ("c6", 0), ("c3", 1), ("r0", 1), ("e0", 0), ("r1", 1), ("c3", 0), ("c8", 0),
-        ("c4", 0), ("c7", 0), ("c0", 0), ("e0", 0), ("r0", 0), ("c0", 0), ("c1", 0), ("r1", 0),
-        ("c1", 0), ("c2", 0), ("c5", 0), ("c6", 0), ("c2", 0), ("c3", 0), ("c5", 0), ("c4", 0),
-        ("c6", 0), ("c7", 0), ("c3", 0), ("c4", 0), ("r0", 0), ("c7", 0), ("r1", 0), ("r0", 0),
-        ("r1", 0),
+        ("c1", 0), ("e0", 0), ("c1", 1), ("e2", 0), ("r1", 0), ("r0", 0), ("e1", 0), ("c0", 0),
+        ("r2", 0), ("e3", 0), ("r3", 0), ("c2", 0), ("e0", 0), ("e2", 0), ("e3", 0), ("c1", 0),
+        ("r1", 0), ("r0", 0), ("c2", 0), ("c1", 0), ("c0", 0), ("r2", 0), ("r3", 0), ("r1", 0),
+        ("r0", 0), ("c0", 0), ("r2", 0), ("r1", 0), ("r3", 0), ("r0", 0), ("r2", 0), ("r3", 0),
     ),
 }
 
@@ -562,17 +574,20 @@
         pl.semaphore_signal(barrier, inc=1, device_id=(target, chan), device_id_type=MESH)
     for target in others:
         pl.semaphore_signal(barrier, inc=1, device_id=(clip, target), device_id_type=MESH)
-    pl.semaphore_wait(barrier, n_clip - 1 + n_chan - 1)
-
-    def share_we(s):
+
+    def share_we(s, half):
+        size = ib // 2
         for j in others:
-            target = r.wef.at[s, cols(chan)]
-            remote(r.wexp_hbm.at[s, :, wide(j)], target, (clip, j), ("we", s))
-
-    def share_wr(s):
+            here = r.wexp_hbm.at[s, pl.ds(half * size, size), wide(j)]
+            target = r.wef.at[s, pl.ds(pl.multiple_of(chan * ib + half * size, size), size)]
+            remote(here, target, (clip, j), ("we", s))
+
+    def share_wr(s, half):
+        size = cs // 2
         for j in others:
-            target = r.wrf.at[s, :, cols(chan)]
-            remote(r.wred_hbm.at[s, wide(j)], target, (clip, j), ("wr", s))
+            here = r.wred_hbm.at[s, pl.ds(pl.multiple_of(j * cs + half * size, size), size)]
+            target = r.wrf.at[s, pl.ds(half * size, size), cols(chan)]
+            remote(here, target, (clip, j), ("wr", s))
 
     def shared_we(s):
         load_we[s].wait()
@@ -664,8 +679,8 @@
         step = next(n for n in (112, 96, 80, 64, 48, 32, 16) if count % n == 0)
         return each(start, count, step, one, begin)
 
-    def broad(one, begin):
-        return each(0, rows, 16, one, begin)
+    def broad(k, one, begin):
+        return each(*raw_spans[k], 16, one, begin)
 
     moments_in = [[None, None, None], [None, None, None]]
 
@@ -800,8 +815,6 @@
     for s in range(2):
         r.red[s, rows : rows + 8] = zero_n
 
-    share_we(0)
-    share_wr(1)
     sums = (zero_n, zero_n)
     load_wr0.wait()
     for h in range(2):
@@ -809,17 +822,21 @@
         value = dot(r.x[raw(h)], r.wr0[...])
         r.red[0, raw(h)] = value
         sums = (sums[0] + fold(value), sums[1] + fold(value * value))
+    pl.semaphore_wait(barrier, n_clip - 1 + n_chan - 1)
     made = stat_start(r.stn, 0, sums)
+    share_we(0, 0)
+    share_we(0, 1)
     spread_taps()
     lax.fori_loop(0, r.gk.shape[0], clear, 0)
     moments_in[0][0] = moments(stat_end(r.stn, 0, made))
 
     stage = forward(0, 1, 0)
     next(stage)
+    share_wr(1, 0)
     next(stage)
     shared_we(0)
     next(stage)
-    share_we(1)
+    share_wr(1, 1)
     for _ in stage:
         pass
 
@@ -828,14 +845,15 @@
         r.out0[at] = gelu(z).astype(bf16)
         return _
 
-    broad(out_zero, 0)
-
-    def scatter_all(slot, chunks, product, use, beside=None):
+
+    def scatter_all(slot, chunks, prepare, product, use, beside=None, midway=None):
         keys = phase_keys(4)
         ats = [pl.ds(*span) for span in chunks]
         borrowed = []
 
         def start(k, away):
+            if away:
+                prepare(k)
             two = pair(1 - high if away else high)
             r.pb[ats[k], two] = product(ats[k], two).astype(bf16)
             block, index = (j_far, 1) if away else (j_core, 0)
@@ -868,6 +886,8 @@
             arrive(r.rcore.at[slot, 0, ats[k]], keys[k][0])
             arrive(r.ryy.at[slot, ats[k]], keys[k][2])
             use(*chunks[k])
+            if midway is not None and k == 1:
+                midway()
         for index in borrowed:
             sent(index)
 
@@ -880,15 +900,24 @@
         held["sums"] = (held["sums"][0] + fold(value), held["sums"][1] + fold(value * value))
 
     shared_wr(1)
-    scatter_all(0, raw_spans, lambda at, two: dot(r.out0[at], r.wrf[1, :, two]), use_reduced)
+    scatter_all(
+        0,
+        raw_spans,
+        lambda k: broad(k, out_zero, 0),
+        lambda at, two: dot(r.out0[at], r.wrf[1, :, two]),
+        use_reduced,
+    )
     made = stat_start(r.stn, 2, held["sums"])
+    share_we(1, 0)
     moments_in[1][0] = moments(stat_end(r.stn, 2, made))
     stage = forward(1, 3, 1)
     next(stage)
+    share_we(1, 1)
     next(stage)
     shared_we(1)
     next(stage)
-    share_wr(0)
+    share_wr(0, 0)
+    share_wr(0, 1)
     for _ in stage:
         pass
 
@@ -908,8 +937,14 @@
         r.gpre[at] = grad
         return sums[0] + fold(grad), sums[1] + fold(grad * centred)
 
+    top_sums = {}
+
     def backward(s, stat_base, wide_slot, slot):
-        sums = broad(out_one if s else top_zero, (zero_w, zero_w))
+        if s == 1:
+            top_sums["now"] = (zero_w, zero_w)
+            for k in range(4):
+                top_sums["now"] = broad(k, out_one, top_sums["now"])
+        sums = top_sums["now"]
         made = stat_start(r.stw, wide_slot, sums)
         if s == 1:
             write_out(r.act, r.act_out)
@@ -927,7 +962,6 @@
             r.gexp[at] = grad.astype(bf16)
             return _
 
-        broad(expand_back, 0)
         held["sums"] = (zero_n, zero_n)
         service(s, "expand_before")
 
@@ -952,9 +986,11 @@
         scatter_all(
             slot,
             raw_spans,
+            lambda k: broad(k, expand_back, 0),
             lambda at, two: dot(r.gexp[at], r.wef[s, two], 1, 1),
             use_inner,
             weight_expand,
+            lambda: service(s, "expand_use"),
         )
         made = stat_start(r.stn, stat_base, held["sums"])
         service(s, "inner")
@@ -980,7 +1016,6 @@
                     r.gs[at, tap * ib : (tap + 1) * ib] = both.astype(bf16)
             return _
 
-        lax.fori_loop(0, 2 * pairs, conv_back, 0)
 
         service(s, "conv_before")
 
@@ -1001,9 +1036,11 @@
         scatter_all(
             slot + 1,
             padded_spans,
+            lambda k: lax.fori_loop(k * pairs // 2, (k + 1) * pairs // 2, conv_back, 0),
             lambda at, two: dot(r.gs[at], r.wc[s, two], 1, 1),
             use_mixed,
             weight_conv,
+            lambda: service(s, "conv_use"),
         )
 
         def tap_sums(grad, v, index, reach):
@@ -1066,32 +1103,43 @@
         mean, inv = moments_in[s][0]
         scale = inv * row(r.gi, s, 0)
         shift_mean, gain_mean = shift_sum / pixel_total, gain_sum / pixel_total
-        keys = phase_keys(2)
-        for h in range(2):
-
-            def reduce_back(at, _):
-                centred = (r.red[s, at] - mean) * inv
-                grad = scale * (r.g1[at] - (shift_mean + centred * gain_mean))
-                r.grf[s, at, cols(chan)] = grad.astype(bf16)
-                return _
-
-            narrow(starts[h], counts[h], reduce_back, 0)
-            gather_start(r.grf.at[s], raw(h), keys[h])
+        service(s, "red_after")
+        keys = phase_keys(4)
+        quarters = [pl.ds(*span) for span in raw_spans]
+
+        def reduce_back(at, _):
+            centred = (r.red[s, at] - mean) * inv
+            grad = scale * (r.g1[at] - (shift_mean + centred * gain_mean))
+            r.grf[s, at, cols(chan)] = grad.astype(bf16)
+            return _
+
+        for k in range(4):
+            narrow(*raw_spans[k], reduce_back, 0)
+            gather_start(r.grf.at[s], quarters[k], keys[k])
         if s == 0:
             own = r.grf[0, :, cols(chan)]
             for piece in range(n_chan):
                 value = dot(r.x[:, piece * cs : (piece + 1) * cs], own, 0, 0).astype(bf16)
                 r.gr[0, piece] = value.reshape(r.gr.shape[2:])
         service(s, "gather")
-        gather_pass(r.grf.at[s], raw(0), keys[0])
-        gather_pass(r.grf.at[s], raw(1), keys[1])
+        gather_pass(r.grf.at[s], quarters[0], keys[0])
+        gather_pass(r.grf.at[s], quarters[1], keys[1])
         if s == 0:
             shared_wr(0)
-        for h in range(2):
-            gather_end(r.grf.at[s], raw(h), keys[h])
-            r.gin[raw(h)] = dot(r.grf[s, raw(h)], r.wrf[s], 1, 1) + r.gpre[raw(h)]
+        else:
+            top_sums["now"] = (zero_w, zero_w)
+        for k in range(4):
+            at = quarters[k]
+            gather_end(r.grf.at[s], at, keys[k])
+            r.gin[at] = dot(r.grf[s, at], r.wrf[s], 1, 1) + r.gpre[at]
+            if k < 2:
+                gather_pass(r.grf.at[s], quarters[k + 2], keys[k + 2])
             if s == 0:
-                write_out(r.gin.at[raw(h)], r.gin_out.at[raw(h)])
+                write_out(r.gin.at[at], r.gin_out.at[at])
+            else:
+                top_sums["now"] = broad(k, top_zero, top_sums["now"])
+            if k == 1:
+                service(s, "gather_use")
         service(s, "last")
         if s == 1:
             value = dot(r.out0[...], r.grf[1], 0, 0).astype(bf16)

time: 234 us -> 224 us (0.957)
  Pallas kernels: 233 us -> 223 us
    pallas_call x1, Pallas kernels: 227 us -> 216 us  [fused_call(): pl.pallas_call(partial(fused_kernel, n_clip, n_chan, pixel_total), out_sh...]
where the time goes in v5:
time: 224 us
  Pallas kernels  223 us (100%)
    pallas_call x1, Pallas kernels, fused_call(): pl.pallas_call(partial(fused_kernel, n_clip, n_chan, pixel_total), out_sh...  216 us
    pallas_call x1, Pallas kernels, finish(): pl.pallas_call(finish_kernel, grid=(steps,), out_shape=shapes, in_specs=b...  6.56 us

profile of v5, /device:TPU:0, one launch (start us, length us, event | category | flops | bytes accessed | tf_op | source)
XLA Modules:
  0.0 223.5 jit_solution(816182527191666436)
XLA Ops:
  0.6 216.1 %shard_map.203 = (bf16[784,512]{1,0:T(8,128)(2,1)}, f32[784,512]{1,0:T(8,128)}, f32[2,2,128]{2,1,0:T(2,128)}, f32[2,2,128]{2,1,0:T(2,128)}, f32[2,512]{1,0:T(2,1...) custom-call(bf16[784,2048]{1,0:T(8,128)(2,1)} %refs_0_.1, ...), custom_call_target="tpu_custom_call" | custom-call | tf_op jit(solution)/shard_map/pallas_call | solution.py:1315
  216.8 6.6 %shard_map.204 = (f32[9216,128]{1,0:T(8,128)}, f32[256,2048]{1,0:T(8,128)}, f32[4096,128]{1,0:T(8,128)}, bf16[784,512]{1,0:T(8,128)(2,1)}, f32[784,512]{1,0:T(8,...) custom-call(bf16[9216,128]{1,0:T(8,128)(2,1)} %bitcast.10, ...), custom_call_target="tpu_custom_call" | custom-call | tf_op jit(solution)/shard_map/pallas_call | solution.py:1360

commit v6 on v5

--- a/solution.py
+++ b/solution.py
@@ -1,5 +1,6 @@
 from functools import partial
 from types import SimpleNamespace
+from typing import Any, NamedTuple
 
 import jax
 import jax.numpy as jnp
@@ -380,85 +381,161 @@
     )
 
 
-NAMES = (
-    "x_hbm", "cot_hbm", "wred_hbm", "wconv_hbm", "wexp_hbm", "bnd", "gi", "bi", "go", "bo",
-    "dk", "gb", "act_out", "gin_out", "ggi", "gbi", "ggo", "gbo", "gk_out", "ggb_out", "gc_out",
-    "ge_out", "gr_out", "x", "cot", "wr0", "wrf", "wef", "wc", "dkb", "red", "hid", "sig",
-    "conv", "mixf", "inf", "ex", "out0", "act", "y", "gpre", "gin", "gexp", "gs", "pb", "ysend",
-    "rcore", "ryy", "grf", "gm", "gd", "g1", "gk", "kst", "stn", "stw", "gc", "geo", "ge",
-    "gro", "gr", "xc", "xe", "xr", "zc", "ze", "zr", "fc", "fe", "fr", "ssem", "rsem", "lsem",
-)
-
-
-PIECES = {"gc": 3, "ge": 4, "gr": 4}
-ARRIVALS = 40 + 8 * sum(PIECES.values())
+class Refs(NamedTuple):
+    x_hbm: Any
+    cot_hbm: Any
+    wred_hbm: Any
+    wconv_hbm: Any
+    wexp_hbm: Any
+    bnd: Any
+    gi: Any
+    bi: Any
+    go: Any
+    bo: Any
+    dk: Any
+    gb: Any
+    act_out: Any
+    gin_out: Any
+    ggi: Any
+    gbi: Any
+    ggo: Any
+    gbo: Any
+    gk_out: Any
+    ggb_out: Any
+    gc_out: Any
+    ge_out: Any
+    gr_out: Any
+    x: Any
+    cot: Any
+    wr0: Any
+    wrf: Any
+    wef: Any
+    wc: Any
+    dkb: Any
+    red: Any
+    hid: Any
+    sig: Any
+    conv: Any
+    mixf: Any
+    inf: Any
+    ex: Any
+    out0: Any
+    act: Any
+    y: Any
+    gpre: Any
+    gin: Any
+    gexp: Any
+    gs: Any
+    pb: Any
+    ysend: Any
+    rcore: Any
+    ryy: Any
+    grf: Any
+    gm: Any
+    gd: Any
+    g1: Any
+    gk: Any
+    kst: Any
+    stn: Any
+    stw: Any
+    gc: Any
+    geo: Any
+    ge: Any
+    gro: Any
+    gr: Any
+    xc: Any
+    xe: Any
+    xr: Any
+    zc: Any
+    ze: Any
+    zr: Any
+    fc: Any
+    fe: Any
+    fr: Any
+    ssem: Any
+    rsem: Any
+    lsem: Any
+
+
+PIECES = (3, 2, 2)
+ARRIVALS = 40 + 12 * sum(PIECES)
+TURN, EXPAND, REDUCE, SUMS, CHAN, TAPS = range(-6, 0)
 PLAN = {
-    (1, "conv_before"): (
-        ("e1", 1), ("e2", 1), ("e3", 1), ("e0", 1),
-    ),
-    (1, "conv"): (
-        ("c0", 1), ("e1", 1), ("e2", 1), ("c2", 1),
-    ),
-    (1, "conv_use"): (
-        ("e3", 1), ("e0", 1),
-    ),
-    (1, "hide_before"): (
-        ("e1", 1), ("e2", 1),
-    ),
-    (1, "red"): (
-        ("c0", 1), ("e3", 1), ("c2", 1), ("e0", 1), ("c1", 1), ("e1", 1),
-    ),
-    (1, "red_after"): (
-        ("e2", 1),
-    ),
-    (1, "last"): (
-        ("e1", 1), ("e3", 1),
-    ),
-    (0, "top"): (
-        ("c0", 1), ("e2", 1), ("e3", 1), ("c2", 1), ("e0", 1), ("c1", 1),
-    ),
-    (0, "expand_before"): (
-        ("r3", 1), ("r1", 1), ("r2", 1), ("r0", 1),
-    ),
-    (0, "expand"): (
-        ("c0", 1), ("r3", 1), ("r1", 1), ("e0", 1),
-    ),
-    (0, "inner"): (
-        ("r2", 1), ("c2", 1), ("r0", 1), ("c1", 1),
-    ),
-    (0, "conv_before"): (
-        ("c0", 1), ("r3", 1), ("e1", 0), ("r1", 1), ("e0", 0), ("e2", 0), ("e3", 0), ("r2", 1),
-    ),
-    (0, "conv"): (
-        ("c2", 0), ("e1", 0), ("c1", 0), ("e0", 0), ("e2", 0), ("c0", 0), ("c2", 1), ("r0", 1),
-    ),
-    (0, "conv_use"): (
-        ("r3", 1), ("e3", 0),
-    ),
-    (0, "hide_before"): (
-        ("c2", 0),
-    ),
-    (0, "red"): (
-        ("e1", 0), ("c1", 0), ("r1", 1), ("e0", 0), ("e2", 0), ("c0", 0), ("e3", 0), ("r2", 1),
-        ("r0", 1), ("c1", 1), ("r3", 1),
-    ),
-    (0, "gather"): (
-        ("r1", 0), ("r1", 1), ("r0", 0),
-    ),
-    (0, "gather_use"): (
-        ("c2", 0), ("e1", 0), ("r2", 0), ("r2", 1), ("r0", 1), ("r3", 0),
-    ),
-    (0, "end"): (
-        ("c1", 0), ("e0", 0), ("c1", 1), ("e2", 0), ("r1", 0), ("r0", 0), ("e1", 0), ("c0", 0),
-        ("r2", 0), ("e3", 0), ("r3", 0), ("c2", 0), ("e0", 0), ("e2", 0), ("e3", 0), ("c1", 0),
-        ("r1", 0), ("r0", 0), ("c2", 0), ("c1", 0), ("c0", 0), ("r2", 0), ("r3", 0), ("r1", 0),
-        ("r0", 0), ("c0", 0), ("r2", 0), ("r1", 0), ("r3", 0), ("r0", 0), ("r2", 0), ("r3", 0),
+    (1, 5): (
+        110, 111,
+    ),
+    (1, 6): (
+        101, 102,
+    ),
+    (1, 7): (
+        110,
+    ),
+    (1, 8): (
+        110, 111,
+    ),
+    (1, 9): (
+        101, 100,
+    ),
+    (1, 10): (
+        110, 111, 102,
+    ),
+    (1, 11): (
+        101,
+    ),
+    (1, 12): (
+        110, 100,
+    ),
+    (1, 13): (
+        111,
+    ),
+    (0, 0): (
+        101, 110, 102, 100, 111,
+    ),
+    (0, 1): (
+        120, 121,
+    ),
+    (0, 2): (
+        101, 110, 111, 102,
+    ),
+    (0, 3): (
+        120,
+    ),
+    (0, 4): (
+        101, 120, 111, 102, 100, 121,
+    ),
+    (0, 5): (
+        11, 10,
+    ),
+    (0, 6): (
+        101, 120, 0, 2, 11, 1, 100, 121,
+    ),
+    (0, 8): (
+        120, 0, 11, 10,
+    ),
+    (0, 9): (
+        120, 0, 2, 102, 121,
+    ),
+    (0, 10): (
+        11, 1, 100, 10,
+    ),
+    (0, 11): (
+        120, 0, 2, 21, 20,
+    ),
+    (0, 12): (
+        121,
+    ),
+    (0, 13): (
+        11, 1, 102, 10, 0, 100,
+    ),
+    (0, 14): (
+        121, 11, 2, 21, 1, 0, 20, 10, 21, 2, 121, 20, 11, 1, 10, 21, 2, 0, 20, 1, 10, 21, 20, 2,
+        21, 20, 1, 21, 20,
     ),
 }
 
 
 def fused_kernel(n_clip, n_chan, pixel_total, *refs):
-    r = SimpleNamespace(**dict(zip(NAMES, refs)))
+    r = Refs(*refs)
     rows, cs = r.cot.shape
     ib = LANES
     frames = rows // PIXELS
@@ -475,7 +552,7 @@
     j_far = (1 - core) + 2 * (1 - high)
     others = (j_core, j_y, j_far)
     z, side = lax.div(clip, 2), lax.rem(clip, 2)
-    z_others = [lax.rem(z + d, n_z) for d in range(1, n_z)]
+    low, z_near, z_far = lax.rem(z, 2), z + 1 - 2 * lax.rem(z, 2), lax.rem(z + 2, 4)
     clip_others = [lax.rem(clip + d, n_clip) for d in range(1, n_clip)]
 
     def cols(j):
@@ -500,7 +577,8 @@
 
     raw_spans, padded_spans = spans(rows), spans(frames * FRAME)
 
-    places, in_flight, counters = {}, {}, {"send": 0, "load": 0, "phase": 0, "sums": 0}
+    places, in_flight = {}, {}
+    counters = SimpleNamespace(send=0, load=0, phase=0, sums=0, out=0)
 
     def arrival(key):
         return r.rsem.at[places.setdefault(key, len(places))]
@@ -510,8 +588,8 @@
             in_flight.pop(index).wait_send()
 
     def remote(src, dst, target, key):
-        index = counters["send"] % SENDS
-        counters["send"] += 1
+        index = counters.send % SENDS
+        counters.send += 1
         sent(index)
         made = pltpu.make_async_remote_copy(
             src_ref=src,
@@ -537,8 +615,8 @@
 
     def local(src, dst, index=None):
         if index is None:
-            index = counters["load"]
-            counters["load"] += 1
+            index = counters.load
+            counters.load += 1
         made = pltpu.make_async_copy(src, dst, r.lsem.at[index])
         made.start()
         return made
@@ -546,8 +624,8 @@
     outgoing = {}
 
     def write_out(src, dst):
-        turn = counters.setdefault("out", 0) % 8
-        counters["out"] += 1
+        turn = counters.out % 8
+        counters.out += 1
         if turn in outgoing:
             outgoing.pop(turn).wait()
         outgoing[turn] = local(src, dst, LOADS - 8 + turn)
@@ -562,8 +640,8 @@
     ]
     load_wc = []
     for s in range(2):
-        index = counters["load"]
-        counters["load"] += 1
+        index = counters.load
+        counters.load += 1
         for tap in range(9):
             local(r.wconv_hbm.at[s, tap], r.wc.at[s, :, tap * ib : (tap + 1) * ib], index)
         load_wc.append(pltpu.make_async_copy(r.wc.at[s], r.wc.at[s], r.lsem.at[index]))
@@ -580,28 +658,28 @@
         for j in others:
             here = r.wexp_hbm.at[s, pl.ds(half * size, size), wide(j)]
             target = r.wef.at[s, pl.ds(pl.multiple_of(chan * ib + half * size, size), size)]
-            remote(here, target, (clip, j), ("we", s))
+            remote(here, target, (clip, j), (EXPAND, s))
 
     def share_wr(s, half):
         size = cs // 2
         for j in others:
             here = r.wred_hbm.at[s, pl.ds(pl.multiple_of(j * cs + half * size, size), size)]
             target = r.wrf.at[s, pl.ds(half * size, size), cols(chan)]
-            remote(here, target, (clip, j), ("wr", s))
+            remote(here, target, (clip, j), (REDUCE, s))
 
     def shared_we(s):
         load_we[s].wait()
-        arrive(r.wef.at[s, pl.ds(0, (n_chan - 1) * ib)], ("we", s))
+        arrive(r.wef.at[s, pl.ds(0, (n_chan - 1) * ib)], (EXPAND, s))
 
     def shared_wr(s):
         load_wr[s].wait()
-        arrive(r.wrf.at[s, :, pl.ds(0, (n_chan - 1) * ib)], ("wr", s))
+        arrive(r.wrf.at[s, :, pl.ds(0, (n_chan - 1) * ib)], (REDUCE, s))
 
     def stat_start(buf, slot, values):
         for k, value in enumerate(values):
             buf[slot, clip, k : k + 1, :] = jnp.sum(value, axis=0, keepdims=True)
-        key = ("sums", counters["sums"] % 2)
-        counters["sums"] += 1
+        key = (SUMS, counters.sums % 2)
+        counters.sums += 1
         for t in clip_others:
             remote(buf.at[slot, clip], buf.at[slot, clip], (t, chan), key)
         return key
@@ -618,9 +696,9 @@
         return mean, lax.rsqrt(pair[1] / pixel_total - mean * mean + epsilon)
 
     def phase_keys(count):
-        turn = counters["phase"] % 2
-        counters["phase"] += 1
-        return [[("chan", turn, k, i) for i in range(3)] for k in range(count)]
+        turn = counters.phase % 2
+        counters.phase += 1
+        return [[(CHAN, turn, k, i) for i in range(3)] for k in range(count)]
 
     def gather_start(full, at, key):
         mine = full.at[at, cols(chan)]
@@ -891,13 +969,13 @@
         for index in borrowed:
             sent(index)
 
-    held = {"sums": (zero_n, zero_n)}
+    held = SimpleNamespace(sums=(zero_n, zero_n))
 
     def use_reduced(begin, count):
         at = pl.ds(begin, count)
         value = scatter_value(0, at)
         r.red[1, at] = value
-        held["sums"] = (held["sums"][0] + fold(value), held["sums"][1] + fold(value * value))
+        held.sums = (held.sums[0] + fold(value), held.sums[1] + fold(value * value))
 
     shared_wr(1)
     scatter_all(
@@ -907,7 +985,7 @@
         lambda at, two: dot(r.out0[at], r.wrf[1, :, two]),
         use_reduced,
     )
-    made = stat_start(r.stn, 2, held["sums"])
+    made = stat_start(r.stn, 2, held.sums)
     share_we(1, 0)
     moments_in[1][0] = moments(stat_end(r.stn, 2, made))
     stage = forward(1, 3, 1)
@@ -937,18 +1015,18 @@
         r.gpre[at] = grad
         return sums[0] + fold(grad), sums[1] + fold(grad * centred)
 
-    top_sums = {}
+    top_sums = SimpleNamespace()
 
     def backward(s, stat_base, wide_slot, slot):
         if s == 1:
-            top_sums["now"] = (zero_w, zero_w)
+            top_sums.now = (zero_w, zero_w)
             for k in range(4):
-                top_sums["now"] = broad(k, out_one, top_sums["now"])
-        sums = top_sums["now"]
+                top_sums.now = broad(k, out_one, top_sums.now)
+        sums = top_sums.now
         made = stat_start(r.stw, wide_slot, sums)
         if s == 1:
             write_out(r.act, r.act_out)
-        service(s, "top")
+        service(s, 0)
         shift_sum, gain_sum = stat_end(r.stw, wide_slot, made)
         r.gbo[s : s + 1] = shift_sum
         r.ggo[s : s + 1] = gain_sum
@@ -962,17 +1040,17 @@
             r.gexp[at] = grad.astype(bf16)
             return _
 
-        held["sums"] = (zero_n, zero_n)
-        service(s, "expand_before")
+        held.sums = (zero_n, zero_n)
+        service(s, 1)
 
         def weight_expand():
             value = dot(r.inf[s], r.gexp[...], 0, 0).astype(bf16)
             r.geo[s] = value.reshape(r.geo.shape[1:])
             place = r.ge.at[s, :, :, :, wide(chan)]
-            turned["ge", s] = local(r.geo.at[s, chan], place)
+            turned[1, s] = local(r.geo.at[s, chan], place)
             for j in others:
-                remote(r.geo.at[s, j], place, (clip, j), ("ge", s))
-            service(s, "expand")
+                remote(r.geo.at[s, j], place, (clip, j), (TURN, 1, s))
+            service(s, 2)
 
         def use_inner(begin, count):
             def one(at, sums):
@@ -981,7 +1059,7 @@
                 r.g1[at] = grad
                 return sums[0] + fold(grad), sums[1] + fold(grad * centred)
 
-            held["sums"] = narrow(begin, count, one, held["sums"])
+            held.sums = narrow(begin, count, one, held.sums)
 
         scatter_all(
             slot,
@@ -990,10 +1068,10 @@
             lambda at, two: dot(r.gexp[at], r.wef[s, two], 1, 1),
             use_inner,
             weight_expand,
-            lambda: service(s, "expand_use"),
+            lambda: service(s, 3),
         )
-        made = stat_start(r.stn, stat_base, held["sums"])
-        service(s, "inner")
+        made = stat_start(r.stn, stat_base, held.sums)
+        service(s, 4)
         shift_sum, gain_sum = stat_end(r.stn, stat_base, made)
         r.gbi[s, 1:2] = shift_sum
         r.ggi[s, 1:2] = gain_sum
@@ -1017,14 +1095,14 @@
             return _
 
 
-        service(s, "conv_before")
+        service(s, 5)
 
         def weight_conv():
             for k in range(3):
                 taps = slice(3 * k * ib, 3 * (k + 1) * ib)
                 value = dot(r.mixf[s], r.gs[:, taps], 0, 0).astype(bf16)
                 r.gc[s, :, :, :, taps] = value.reshape(r.gc.shape[1:4] + (3 * ib,))
-            service(s, "conv")
+            service(s, 6)
 
         def use_mixed(begin, count):
             def one(at, _):
@@ -1040,7 +1118,7 @@
             lambda at, two: dot(r.gs[at], r.wc[s, two], 1, 1),
             use_mixed,
             weight_conv,
-            lambda: service(s, "conv_use"),
+            lambda: service(s, 7),
         )
 
         def tap_sums(grad, v, index, reach):
@@ -1071,7 +1149,7 @@
 
         lax.fori_loop(0, frames, mix_back, jnp.zeros((SIDE, 8, ib), f32))
 
-        service(s, "hide_before")
+        service(s, 8)
 
         def hide_back(f, sums):
             at = frame_rows(f)
@@ -1096,14 +1174,14 @@
 
         sums = lax.fori_loop(0, frames, hide_back, (zero_n, zero_n))
         made = stat_start(r.stn, stat_base + 1, sums)
-        service(s, "red")
+        service(s, 9)
         shift_sum, gain_sum = stat_end(r.stn, stat_base + 1, made)
         r.gbi[s, 0:1] = shift_sum
         r.ggi[s, 0:1] = gain_sum
         mean, inv = moments_in[s][0]
         scale = inv * row(r.gi, s, 0)
         shift_mean, gain_mean = shift_sum / pixel_total, gain_sum / pixel_total
-        service(s, "red_after")
+        service(s, 10)
         keys = phase_keys(4)
         quarters = [pl.ds(*span) for span in raw_spans]
 
@@ -1121,13 +1199,13 @@
             for piece in range(n_chan):
                 value = dot(r.x[:, piece * cs : (piece + 1) * cs], own, 0, 0).astype(bf16)
                 r.gr[0, piece] = value.reshape(r.gr.shape[2:])
-        service(s, "gather")
+        service(s, 11)
         gather_pass(r.grf.at[s], quarters[0], keys[0])
         gather_pass(r.grf.at[s], quarters[1], keys[1])
         if s == 0:
             shared_wr(0)
         else:
-            top_sums["now"] = (zero_w, zero_w)
+            top_sums.now = (zero_w, zero_w)
         for k in range(4):
             at = quarters[k]
             gather_end(r.grf.at[s], at, keys[k])
@@ -1137,17 +1215,17 @@
             if s == 0:
                 write_out(r.gin.at[at], r.gin_out.at[at])
             else:
-                top_sums["now"] = broad(k, top_zero, top_sums["now"])
+                top_sums.now = broad(k, top_zero, top_sums.now)
             if k == 1:
-                service(s, "gather_use")
-        service(s, "last")
+                service(s, 12)
+        service(s, 13)
         if s == 1:
             value = dot(r.out0[...], r.grf[1], 0, 0).astype(bf16)
             r.gro[...] = value.reshape(r.gro.shape)
             place = r.gr.at[1, chan]
-            turned["gr", 1] = local(r.gro.at[:, :, cols(chan)], place)
+            turned[2, 1] = local(r.gro.at[:, :, cols(chan)], place)
             for j in others:
-                remote(r.gro.at[:, :, cols(j)], place, (clip, j), ("gr", 1))
+                remote(r.gro.at[:, :, cols(j)], place, (clip, j), (TURN, 2, 1))
 
     turned = {}
 
@@ -1161,58 +1239,66 @@
             turned.pop((kind, s)).wait()
             three = pl.ds(0, (n_chan - 1) * cs)
             arrive(
-                r.ge.at[s, :, :, :, three] if kind == "ge" else r.gr.at[s, pl.ds(0, n_chan - 1)],
-                (kind, s),
+                r.ge.at[s, :, :, :, three] if kind == 1 else r.gr.at[s, pl.ds(0, n_chan - 1)],
+                (TURN, kind, s),
             )
+        near, far = (2 * z_near + side, chan), (2 * z_far + side, chan)
+
+        def add(k, term):
+            both = ref[s, k, side, line, place].astype(f32) + term.astype(f32)
+            return both.astype(bf16)
+
         remote(mine.at[:, 1 - side], side_in, across, key + (0,))
         yield
         arrive(side_in, key + (0,))
         for k in range(n_z):
-            both = ref[s, k, side, line, place].astype(f32)
-            both = both + from_side[s, k, line, place].astype(f32)
-            ref[s, k, side, line, place] = both.astype(bf16)
-        for k, there in enumerate(z_others):
-            remote(mine.at[there, side], z_in.at[k], (2 * there + side, chan), key + (1,))
+            ref[s, k, side, line, place] = add(k, from_side[s, k, line, place])
+        for k in range(2):
+            remote(mine.at[1 - low + 2 * k, side], z_in.at[k], near, key + (1,))
         yield
-        arrive(z_in, key + (1,))
-        total = ref[s, z, side, line, place].astype(f32)
-        for k in range(n_z - 1):
-            total = total + from_z[s, k, line, place].astype(f32)
-        result[s, z, side, line, place] = total.astype(bf16)
-        own = done.at[z, side]
-        for there in z_others:
-            remote(own, own, (2 * there + side, chan), key + (2,))
+        arrive(z_in.at[pl.ds(0, 2)], key + (1,))
+        for k in range(2):
+            ref[s, low + 2 * k, side, line, place] = add(low + 2 * k, from_z[s, k, line, place])
+        remote(mine.at[z_far, side], z_in.at[2], far, key + (2,))
         yield
-        arrive(done.at[pl.ds(0, n_z - 1), side], key + (2,))
-        remote(done.at[:, side], done.at[:, side], across, key + (3,))
+        arrive(z_in.at[2], key + (2,))
+        result[s, z, side, line, place] = add(z, from_z[s, 2, line, place])
+        remote(done.at[z, side], done.at[z, side], far, key + (3,))
         yield
-        arrive(done.at[:, 1 - side], key + (3,))
-        if kind == "gc":
+        arrive(done.at[z_far, side], key + (3,))
+        for k in (z, z_far):
+            remote(done.at[k, side], done.at[k, side], near, key + (4,))
+        yield
+        arrive(done.at[pl.ds(0, 2), side], key + (4,))
+        remote(done.at[:, side], done.at[:, side], across, key + (5,))
+        yield
+        arrive(done.at[:, 1 - side], key + (5,))
+        if kind == 0:
             base = place.start // ib
             for k in range((place.stop - place.start) // ib):
                 here = r.fc.at[s, :, :, :, (base + k) * ib : (base + k + 1) * ib]
                 write_out(here, r.gc_out.at[s, base + k])
         else:
-            out = {"ge": r.ge_out, "gr": r.gr_out}[kind]
+            out = (None, r.ge_out, r.gr_out)[kind]
             write_out(done, out.at[s, :, :, line, place])
         yield
 
-    kinds = {
-        "gc": (r.gc, r.xc, r.zc, r.fc),
-        "ge": (r.ge, r.xe, r.ze, r.fe),
-        "gr": (r.gr, r.xr, r.zr, r.fr),
-    }
+    kinds = (
+        (r.gc, r.xc, r.zc, r.fc),
+        (r.ge, r.xe, r.ze, r.fe),
+        (r.gr, r.xr, r.zr, r.fr),
+    )
     def cut(size, count):
         return [slice(k * (size // count), (k + 1) * (size // count)) for k in range(count)]
 
     tasks = {}
     for s in range(2):
-        for k, place in enumerate(cut(9 * ib, PIECES["gc"])):
-            tasks[f"c{k}", s] = reduce_task("gc", s, slice(0, r.gc.shape[3]), place)
-        for k, place in enumerate(cut(r.ge.shape[4], PIECES["ge"])):
-            tasks[f"e{k}", s] = reduce_task("ge", s, slice(0, r.ge.shape[3]), place)
-        for k, line in enumerate(cut(r.gr.shape[3], PIECES["gr"])):
-            tasks[f"r{k}", s] = reduce_task("gr", s, line, slice(0, ib))
+        for k, place in enumerate(cut(9 * ib, PIECES[0])):
+            tasks[100 * s + k] = reduce_task(0, s, slice(0, r.gc.shape[3]), place)
+        for k, place in enumerate(cut(r.ge.shape[4], PIECES[1])):
+            tasks[100 * s + 10 + k] = reduce_task(1, s, slice(0, r.ge.shape[3]), place)
+        for k, line in enumerate(cut(r.gr.shape[3], PIECES[2])):
+            tasks[100 * s + 20 + k] = reduce_task(2, s, line, slice(0, ib))
 
     def advance(*steps):
         for step in steps:
@@ -1227,9 +1313,9 @@
     for place in range(r.gk.shape[0]):
         r.kst[clip, place : place + 1, :] = jnp.sum(r.gk[place], axis=0, keepdims=True)
     for t in clip_others:
-        remote(r.kst.at[clip], r.kst.at[clip], (t, chan), "taps")
-    service(0, "end")
-    arrive(r.kst.at[pl.ds(0, n_clip - 1)], "taps")
+        remote(r.kst.at[clip], r.kst.at[clip], (t, chan), TAPS)
+    service(0, 14)
+    arrive(r.kst.at[pl.ds(0, n_clip - 1)], TAPS)
     total = r.kst[0]
     for k in range(1, n_clip):
         total = total + r.kst[k]
@@ -1242,7 +1328,7 @@
         copy.wait()
     for index in list(in_flight):
         sent(index)
-    assert len(places) <= ARRIVALS and counters["load"] <= LOADS - 8, (places, counters)
+    assert len(places) <= ARRIVALS and counters.load <= LOADS - 8
 
 
 def fused_call(n_clip, n_chan, pixel_total, *operands):
@@ -1311,7 +1397,6 @@
         rsem=pltpu.SemaphoreType.DMA((ARRIVALS,)),
         lsem=pltpu.SemaphoreType.DMA((LOADS,)),
     )
-    first = NAMES.index("x")
     return pl.pallas_call(
         partial(fused_kernel, n_clip, n_chan, pixel_total),
         out_shape=[
@@ -1329,7 +1414,7 @@
         ],
         in_specs=[anywhere] * 5 + [scalars] + [whole] * 6,
         out_specs=[anywhere] * 2 + [whole] * 6 + [anywhere] * 3,
-        scratch_shapes=[scratch[name] for name in NAMES[first:]],
+        scratch_shapes=[scratch[name] for name in Refs._fields if name in scratch],
         compiler_params=pltpu.CompilerParams(
             collective_id=0, has_side_effects=True, vmem_limit_bytes=62 * 1024 * 1024
         ),

time: 224 us -> 221 us (0.987)
  Pallas kernels: 223 us -> 220 us
    pallas_call x1, Pallas kernels: 216 us -> 214 us  [fused_call(): pl.pallas_call(partial(fused_kernel, n_clip, n_chan, pixel_total), out_sh...]
where the time goes in v6:
time: 221 us
  Pallas kernels  220 us (100%)
    pallas_call x1, Pallas kernels, fused_call(): pl.pallas_call(partial(fused_kernel, n_clip, n_chan, pixel_total), out_sh...  214 us
    pallas_call x1, Pallas kernels, finish(): pl.pallas_call(finish_kernel, grid=(steps,), out_shape=shapes, in_specs=b...  6.56 us

profile of v6, /device:TPU:0, one launch (start us, length us, event | category | flops | bytes accessed | tf_op | source)
XLA Modules:
  0.0 221.2 jit_solution(14318088011063810261)
XLA Ops:
  0.6 213.8 %shard_map.203 = (bf16[784,512]{1,0:T(8,128)(2,1)}, f32[784,512]{1,0:T(8,128)}, f32[2,2,128]{2,1,0:T(2,128)}, f32[2,2,128]{2,1,0:T(2,128)}, f32[2,512]{1,0:T(2,1...) custom-call(bf16[784,2048]{1,0:T(8,128)(2,1)} %refs_0_.1, ...), custom_call_target="tpu_custom_call" | custom-call | tf_op jit(solution)/shard_map/pallas_call | solution.py:1400
  214.4 6.6 %shard_map.204 = (f32[9216,128]{1,0:T(8,128)}, f32[256,2048]{1,0:T(8,128)}, f32[4096,128]{1,0:T(8,128)}, bf16[784,512]{1,0:T(8,128)(2,1)}, f32[784,512]{1,0:T(8,...) custom-call(bf16[9216,128]{1,0:T(8,128)(2,1)} %bitcast.10, ...), custom_call_target="tpu_custom_call" | custom-call | tf_op jit(solution)/shard_map/pallas_call | solution.py:1445

commit v7 on v6

--- a/solution.py
+++ b/solution.py
@@ -462,74 +462,77 @@
 TURN, EXPAND, REDUCE, SUMS, CHAN, TAPS = range(-6, 0)
 PLAN = {
     (1, 5): (
-        110, 111,
+        111, 110,
     ),
     (1, 6): (
-        101, 102,
+        101,
     ),
     (1, 7): (
-        110,
+        111, 110,
     ),
     (1, 8): (
-        110, 111,
+        111,
     ),
     (1, 9): (
-        101, 100,
+        101, 100, 102, 110,
     ),
     (1, 10): (
-        110, 111, 102,
+        111,
     ),
     (1, 11): (
         101,
     ),
     (1, 12): (
-        110, 100,
+        100, 110,
     ),
     (1, 13): (
         111,
     ),
     (0, 0): (
-        101, 110, 102, 100, 111,
+        111, 101, 100, 102, 110,
     ),
     (0, 1): (
         120, 121,
     ),
     (0, 2): (
-        101, 110, 111, 102,
+        111, 101, 102,
     ),
     (0, 3): (
-        120,
+        120, 110,
     ),
     (0, 4): (
-        101, 120, 111, 102, 100, 121,
+        101, 100, 120, 102, 121, 110,
     ),
     (0, 5): (
-        11, 10,
+        10, 11,
     ),
     (0, 6): (
-        101, 120, 0, 2, 11, 1, 100, 121,
+        101, 100, 1, 120, 10, 102, 121, 0, 2,
+    ),
+    (0, 7): (
+        11,
     ),
     (0, 8): (
-        120, 0, 11, 10,
+        1, 120,
     ),
     (0, 9): (
-        120, 0, 2, 102, 121,
+        100, 1, 10, 102, 121, 0, 11,
     ),
     (0, 10): (
-        11, 1, 100, 10,
+        2,
     ),
     (0, 11): (
-        120, 0, 2, 21, 20,
+        1, 120, 21, 20, 100, 10, 0,
     ),
     (0, 12): (
         121,
     ),
     (0, 13): (
-        11, 1, 102, 10, 0, 100,
+        102, 2, 11, 1, 120, 10, 21, 121,
     ),
     (0, 14): (
-        121, 11, 2, 21, 1, 0, 20, 10, 21, 2, 121, 20, 11, 1, 10, 21, 2, 0, 20, 1, 10, 21, 20, 2,
-        21, 20, 1, 21, 20,
+        0, 1, 2, 20, 10, 11, 21, 121, 0, 20, 1, 11, 2, 21, 10, 0, 20, 11, 2, 21, 0, 20, 21, 20, 2,
+        21, 20,
     ),
 }
 
@@ -817,7 +820,7 @@
             return e1
 
         before = carried.get(s) if first_pair else jnp.zeros((SIDE, 8, ib), f32)
-        carried[s] = lax.fori_loop(first_pair, first_pair + pairs // 2, mix, before)
+        carried[s] = lax.fori_loop(first_pair, first_pair + pairs // 2, mix, before, unroll=True)
 
     def conv_forward(s, k, sums):
         r.y[...] = dot(r.mixf[s, pl.ds(*padded_spans[k])], r.wc[s])
@@ -838,7 +841,7 @@
             squeeze(r.conv.at[s], k * (frames // 4) + i, total)
             return sums[0] + jnp.sum(total, axis=0), sums[1] + jnp.sum(total * total, axis=0)
 
-        return lax.fori_loop(0, frames // 4, add_taps, sums)
+        return lax.fori_loop(0, frames // 4, add_taps, sums, unroll=True)
 
     def forward(s, stat_base, wide_slot):
         keys = phase_keys(4)
@@ -1114,7 +1117,7 @@
         scatter_all(
             slot + 1,
             padded_spans,
-            lambda k: lax.fori_loop(k * pairs // 2, (k + 1) * pairs // 2, conv_back, 0),
+            lambda k: lax.fori_loop(k * pairs // 2, (k + 1) * pairs // 2, conv_back, 0, unroll=True),
             lambda at, two: dot(r.gs[at], r.wc[s, two], 1, 1),
             use_mixed,
             weight_conv,

time: 221 us -> 218 us (0.986)
  Pallas kernels: 220 us -> 217 us
    pallas_call x1, Pallas kernels: 214 us -> 211 us  [fused_call(): pl.pallas_call(partial(fused_kernel, n_clip, n_chan, pixel_total), out_sh...]
where the time goes in v7:
time: 218 us
  Pallas kernels  217 us (100%)
    pallas_call x1, Pallas kernels, fused_call(): pl.pallas_call(partial(fused_kernel, n_clip, n_chan, pixel_total), out_sh...  211 us
    pallas_call x1, Pallas kernels, finish(): pl.pallas_call(finish_kernel, grid=(steps,), out_shape=shapes, in_specs=b...  6.56 us

profile of v7, /device:TPU:0, one launch (start us, length us, event | category | flops | bytes accessed | tf_op | source)
XLA Modules:
  0.0 218.1 jit_solution(9578790312815694577)
XLA Ops:
  0.6 210.7 %shard_map.203 = (bf16[784,512]{1,0:T(8,128)(2,1)}, f32[784,512]{1,0:T(8,128)}, f32[2,2,128]{2,1,0:T(2,128)}, f32[2,2,128]{2,1,0:T(2,128)}, f32[2,512]{1,0:T(2,1...) custom-call(bf16[784,2048]{1,0:T(8,128)(2,1)} %refs_0_.1, ...), custom_call_target="tpu_custom_call" | custom-call | tf_op jit(solution)/shard_map/pallas_call | solution.py:1403
  211.4 6.6 %shard_map.204 = (f32[9216,128]{1,0:T(8,128)}, f32[256,2048]{1,0:T(8,128)}, f32[4096,128]{1,0:T(8,128)}, bf16[784,512]{1,0:T(8,128)(2,1)}, f32[784,512]{1,0:T(8,...) custom-call(bf16[9216,128]{1,0:T(8,128)(2,1)} %bitcast.10, ...), custom_call_target="tpu_custom_call" | custom-call | tf_op jit(solution)/shard_map/pallas_call | solution.py:1448

commit v8 on v7

--- a/solution.py
+++ b/solution.py
@@ -304,7 +304,7 @@
 PAIR = 2 * FRAME
 GELU_A = 0.7978845608028654
 GELU_B = 0.044715
-SENDS = 64
+SENDS = 48
 LOADS = 32
 
 
@@ -465,74 +465,68 @@
         111, 110,
     ),
     (1, 6): (
-        101,
+        102,
     ),
     (1, 7): (
+        111,
+    ),
+    (1, 9): (
+        111, 110, 102, 100, 101,
+    ),
+    (1, 11): (
         111, 110,
     ),
-    (1, 8): (
-        111,
-    ),
-    (1, 9): (
-        101, 100, 102, 110,
-    ),
-    (1, 10): (
-        111,
-    ),
-    (1, 11): (
-        101,
-    ),
     (1, 12): (
-        100, 110,
+        102, 100,
     ),
     (1, 13): (
         111,
     ),
     (0, 0): (
-        111, 101, 100, 102, 110,
+        110, 102, 100, 101,
     ),
     (0, 1): (
-        120, 121,
+        121, 111, 110, 120,
     ),
     (0, 2): (
-        111, 101, 102,
+        110, 102, 100, 101,
     ),
     (0, 3): (
-        120, 110,
+        121,
     ),
     (0, 4): (
-        101, 100, 120, 102, 121, 110,
+        111, 102, 100, 120, 121,
     ),
     (0, 5): (
-        10, 11,
+        11, 110, 10, 101,
     ),
     (0, 6): (
-        101, 100, 1, 120, 10, 102, 121, 0, 2,
+        121, 11, 102, 1, 120,
     ),
     (0, 7): (
-        11,
+        100, 2, 101,
     ),
     (0, 8): (
-        1, 120,
+        121, 11, 1, 10, 120,
     ),
     (0, 9): (
-        100, 1, 10, 102, 121, 0, 11,
+        121, 11, 1, 10, 100, 2, 0, 101,
     ),
     (0, 10): (
-        2,
+        120,
     ),
     (0, 11): (
-        1, 120, 21, 20, 100, 10, 0,
+        121, 11,
     ),
     (0, 12): (
-        121,
+        1, 10, 0,
     ),
     (0, 13): (
-        102, 2, 11, 1, 120, 10, 21, 121,
+        11, 2,
     ),
     (0, 14): (
-        0, 1, 2, 20, 10, 11, 21, 121, 0, 20, 1, 11, 2, 21, 10, 0, 20, 11, 2, 21, 0, 20, 21, 20, 2,
-        21, 20,
+        20, 21, 120, 1, 101, 0, 10, 11, 2, 1, 20, 10, 0, 21, 20, 2, 120, 21, 0, 20, 1, 2, 21, 10,
+        0, 20, 21, 2, 20, 21, 0, 20, 21,
     ),
 }
 

time: 218 us -> 218 us (level)
  no operation moved by 1% of the time
where the time goes in v8:
time: 218 us
  Pallas kernels  217 us (100%)
    pallas_call x1, Pallas kernels, fused_call(): pl.pallas_call(partial(fused_kernel, n_clip, n_chan, pixel_total), out_sh...  210 us
    pallas_call x1, Pallas kernels, finish(): pl.pallas_call(finish_kernel, grid=(steps,), out_shape=shapes, in_specs=b...  6.56 us

profile of v8, /device:TPU:0, one launch (start us, length us, event | category | flops | bytes accessed | tf_op | source)
XLA Modules:
  0.0 217.7 jit_solution(7543810664533712160)
XLA Ops:
  0.6 210.3 %shard_map.203 = (bf16[784,512]{1,0:T(8,128)(2,1)}, f32[784,512]{1,0:T(8,128)}, f32[2,2,128]{2,1,0:T(2,128)}, f32[2,2,128]{2,1,0:T(2,128)}, f32[2,512]{1,0:T(2,1...) custom-call(bf16[784,2048]{1,0:T(8,128)(2,1)} %refs_0_.1, ...), custom_call_target="tpu_custom_call" | custom-call | tf_op jit(solution)/shard_map/pallas_call | solution.py:1397
  210.9 6.6 %shard_map.204 = (f32[9216,128]{1,0:T(8,128)}, f32[256,2048]{1,0:T(8,128)}, f32[4096,128]{1,0:T(8,128)}, bf16[784,512]{1,0:T(8,128)(2,1)}, f32[784,512]{1,0:T(8,...) custom-call(bf16[9216,128]{1,0:T(8,128)(2,1)} %bitcast.10, ...), custom_call_target="tpu_custom_call" | custom-call | tf_op jit(solution)/shard_map/pallas_call | solution.py:1442

commit v9 on v8

--- a/solution.py
+++ b/solution.py
@@ -1431,11 +1431,11 @@
 
 
 def finish(steps, gc, ge, gr, act, gin, *small):
-    arrays = [a.reshape(-1, a.shape[-1]) for a in (gc, ge, gr)] + [act, gin]
-    blocks = [
-        pl.BlockSpec((-(-a.shape[0] // (16 * steps)) * 16, a.shape[1]), lambda i: (i, 0))
-        for a in arrays
-    ]
+    arrays = [a.reshape(-1, a.shape[-1]) for a in (gc, ge, gr)]
+    blocks = [pl.BlockSpec((a.shape[0] // steps, a.shape[1]), lambda i: (i, 0)) for a in arrays]
+    for a in (act, gin):
+        blocks.append(pl.BlockSpec((a.shape[0], a.shape[1] // steps), lambda i: (0, i)))
+        arrays.append(a)
     whole = [pl.BlockSpec(memory_space=pltpu.VMEM)] * len(small)
     shapes = [jax.ShapeDtypeStruct(a.shape, jnp.float32) for a in arrays[:3]]
     shapes += [jax.ShapeDtypeStruct(a.shape, a.dtype) for a in (act, gin, *small)]

time: 218 us -> 218 us (level)
  no operation moved by 1% of the time
where the time goes in v9:
time: 218 us
  Pallas kernels  217 us (100%)
    pallas_call x1, Pallas kernels, fused_call(): pl.pallas_call(partial(fused_kernel, n_clip, n_chan, pixel_total), out_sh...  210 us
    pallas_call x1, Pallas kernels, finish(): pl.pallas_call(finish_kernel, grid=(steps,), out_shape=shapes, in_specs=b...  6.7 us

profile of v9, /device:TPU:0, one launch (start us, length us, event | category | flops | bytes accessed | tf_op | source)
XLA Modules:
  0.0 217.8 jit_solution(2945095472291900597)
XLA Ops:
  0.6 210.3 %shard_map.203 = (bf16[784,512]{1,0:T(8,128)(2,1)}, f32[784,512]{1,0:T(8,128)}, f32[2,2,128]{2,1,0:T(2,128)}, f32[2,2,128]{2,1,0:T(2,128)}, f32[2,512]{1,0:T(2,1...) custom-call(bf16[784,2048]{1,0:T(8,128)(2,1)} %refs_0_.1, ...), custom_call_target="tpu_custom_call" | custom-call | tf_op jit(solution)/shard_map/pallas_call | solution.py:1397
  210.9 6.7 %shard_map.204 = (f32[9216,128]{1,0:T(8,128)}, f32[256,2048]{1,0:T(8,128)}, f32[4096,128]{1,0:T(8,128)}, bf16[784,512]{1,0:T(8,128)(2,1)}, f32[784,512]{1,0:T(8,...) custom-call(bf16[9216,128]{1,0:T(8,128)(2,1)} %bitcast.10, ...), custom_call_target="tpu_custom_call" | custom-call | tf_op jit(solution)/shard_map/pallas_call | solution.py:1442
